TPU v7x, 32 devices: a whole 2x2x4 slice. The times are simulated.
32 devices in a mesh: expert: 8 (over z, y), tensor: 4 (over x, core).
Axes of the slice: x: 2, y: 2, z: 4, core: 2. Of those that a mesh axis runs over, the one named last changes fastest.
Arguments:
- hidden: float32 [8192, 2048], P(('expert', 'tensor')), may hold values from -6 to 6
- segments: int32 [8192], P('expert'), may hold values from 0 to 2, as said below
- routes: int32 [8192, 8], P(('expert', 'tensor')), may hold values from 0 to 63, all different within a row; in each aligned block of 256 rows (0 to 255, 256 to 511, ...) at most 48 rows name the same one
- attn_gain: float32 [2048], replicated, may hold values from 0.5 to 1.5
- qkv_weight: bfloat16 [3, 2048, 2048], P(None, None, 'tensor'), may hold values from -0.125 to 0.125
- qk_gain: float32 [2, 2048], P(None, 'tensor'), may hold values from 0.5 to 1.5
- out_weight: bfloat16 [2048, 2048], P('tensor'), may hold values from -0.5 to 0.5
- moe_gain: float32 [2048], replicated, may hold values from 0.5 to 1.5
- router_weight: bfloat16 [2048, 64], replicated, may hold values from -0.06591797 to 0.06591797
- expert_up: bfloat16 [64, 2, 2048, 1024], P('expert', None, None, 'tensor'), may hold values from -0.125 to 0.125
- expert_down: bfloat16 [64, 1024, 2048], P('expert', 'tensor'), may hold values from -3 to 3
- cotangent: float32 [8192, 2048], P(('expert', 'tensor')), may hold values from -6 to 6
Outputs:
- output: float32 [8192, 2048], P(('expert', 'tensor'))
- hidden_grad: float32 [8192, 2048], P(('expert', 'tensor'))
- attn_gain_grad: float32 [2048], replicated
- qkv_grad: float32 [3, 2048, 2048], P(None, None, 'tensor')
- qk_gain_grad: float32 [2, 2048], P(None, 'tensor')
- out_grad: float32 [2048, 2048], P('tensor')
- moe_gain_grad: float32 [2048], replicated
- router_grad: float32 [2048, 64], replicated
- up_grad: float32 [64, 2, 2048, 1024], P('expert', None, None, 'tensor')
- down_grad: float32 [64, 1024, 2048], P('expert', 'tensor')
Inputs may be any that keep to these rules, and one draw needn't show every extreme that they name: `segments`: each sequence of 1024 tokens holds three documents, numbered 0, 1, 2 in order; document 1 starts within the first 256 tokens and ends within the last 256. `routes`: in the rows of one device each expert is named by at most 48 rows.
All inputs are finite; a program needn't handle non-finite values.
Results may differ from a plain program's by a relative error of at most 0.019.
Values may be sent and summed in bfloat16 or wider, within the bound.
No kernel may reach another device: no remote copies, remote signals or barrier semaphores. Data moves between devices by JAX's collectives and lax.ppermute only.
A program may use at most 640 MiB of HBM per device.

v0:
```python
import math

import jax
import jax.numpy as jnp
from jax import lax
from jax.sharding import PartitionSpec as P

HEAD_DIM = 128


EPSILON = 1e-05
THETA = 10000.0


def normalize(values, gain):
    inverse = lax.rsqrt(jnp.mean(values * values, axis=-1, keepdims=True) + EPSILON)
    return (values * inverse * gain, inverse)


def norm_back(grad_out, values, inverse, gain):
    scaled = values * inverse
    weighted = grad_out * gain
    grad_in = inverse * (weighted - scaled * jnp.mean(weighted * scaled, axis=-1, keepdims=True))
    return (grad_in, jnp.sum(grad_out * scaled, axis=0))


def doc_positions(segment_ids):
    index = jnp.arange(segment_ids.shape[0], dtype=jnp.int32)
    starts = jnp.concatenate([jnp.ones((1,), jnp.bool_), segment_ids[1:] != segment_ids[:-1]])
    first = lax.cummax(jnp.where(starts, index, 0), axis=0)
    return index - first


def rope_tables(positions, half):
    freq = jnp.exp(-math.log(THETA) * jnp.arange(half, dtype=jnp.float32) / half)
    angle = positions.astype(jnp.float32)[:, None] * freq[None, :]
    return (jnp.cos(angle)[:, None, :], jnp.sin(angle)[:, None, :])


def rotate(values, cosine, sine):
    half = values.shape[-1] // 2
    first = values[..., :half]
    second = values[..., half:]
    return jnp.concatenate(
        [first * cosine - second * sine, second * cosine + first * sine], axis=-1
    )


def swiglu_back(grad_active, gate_pre, upper_pre):
    sigma = jax.nn.sigmoid(gate_pre)
    silu_value = gate_pre * sigma
    grad_gate = grad_active * upper_pre * (sigma * (1.0 + gate_pre * (1.0 - sigma)))
    grad_upper = grad_active * silu_value
    return jnp.stack([grad_gate, grad_upper], axis=2).astype(jnp.bfloat16)


def shards(
    hidden,
    segments,
    routes,
    attn_gain,
    qkv_weight,
    qk_gain,
    out_weight,
    moe_gain,
    router_weight,
    expert_up,
    expert_down,
    cotangent,
):
    n_expert = lax.axis_size("expert")
    n_tensor = lax.axis_size("tensor")
    tok_rows, width = hidden.shape
    length = segments.shape[0]
    head_width = out_weight.shape[0]
    local_heads = head_width // HEAD_DIM
    local_experts = expert_up.shape[0]
    all_experts = router_weight.shape[1]
    top_k = routes.shape[1]
    capacity = max(2, 3 * length // (16 * n_tensor))
    scale = HEAD_DIM ** (-0.5)
    normed, inverse_attn = normalize(hidden, attn_gain)
    normed_all = lax.all_gather(normed.astype(jnp.bfloat16), "tensor", axis=0, tiled=True)
    projected = jnp.einsum(
        "td,cdf->tcf", normed_all, qkv_weight, preferred_element_type=jnp.float32
    )
    head_shape = (length, local_heads, HEAD_DIM)
    gains = qk_gain.reshape(2, local_heads, HEAD_DIM)
    cosine, sine = rope_tables(doc_positions(segments), HEAD_DIM // 2)
    query_pre = projected[:, 0].reshape(head_shape)
    key_pre = projected[:, 1].reshape(head_shape)
    query_normed, query_inverse = normalize(query_pre, gains[0])
    key_normed, key_inverse = normalize(key_pre, gains[1])
    queries = rotate(query_normed, cosine, sine).astype(jnp.bfloat16)
    keys_low = rotate(key_normed, cosine, sine).astype(jnp.bfloat16)
    values_low = projected[:, 2].reshape(head_shape).astype(jnp.bfloat16)
    index = jnp.arange(length, dtype=jnp.int32)
    allowed = ((segments[:, None] == segments[None, :]) & (index[:, None] >= index[None, :]))[None]

    def masked_scores():
        scores = (
            jnp.einsum("qhd,khd->hqk", queries, keys_low, preferred_element_type=jnp.float32)
            * scale
        )
        return jnp.where(allowed, scores, -1e30)

    masked = masked_scores()
    top = jnp.max(masked, axis=-1, keepdims=True)
    total = jnp.log(jnp.sum(jnp.exp(masked - top), axis=-1, keepdims=True)) + top
    weights_low = jnp.exp(masked - total).astype(jnp.bfloat16)
    mixed = jnp.einsum("hqk,khd->qhd", weights_low, values_low, preferred_element_type=jnp.float32)
    mixed = mixed.reshape(length, head_width).astype(jnp.bfloat16)
    attended = hidden + lax.psum_scatter(
        jnp.dot(mixed, out_weight, preferred_element_type=jnp.float32),
        "tensor",
        scatter_dimension=0,
        tiled=True,
    )
    moe_normed, inverse_moe = normalize(attended, moe_gain)
    routed_low = moe_normed.astype(jnp.bfloat16)
    logits = jnp.dot(routed_low, router_weight, preferred_element_type=jnp.float32)
    shifted = jnp.exp(logits - jnp.max(logits, axis=-1, keepdims=True))
    probs = shifted / jnp.sum(shifted, axis=-1, keepdims=True)
    expert_ids = jnp.arange(all_experts, dtype=jnp.int32)
    choose = (routes[:, :, None] == expert_ids[None, None, :]).astype(jnp.float32)
    gates = jnp.sum(choose * probs[:, None, :], axis=-1)
    flat = routes.reshape(-1)
    onehot = (flat[:, None] == expert_ids[None, :]).astype(jnp.int32)
    before = jnp.cumsum(onehot, axis=0) - onehot
    place = jnp.sum(before * onehot, axis=1)
    target = (flat // local_experts * capacity + place) * local_experts + flat % local_experts
    slot_count = n_expert * capacity * local_experts
    copies = jnp.repeat(routed_low, top_k, axis=0)
    send = jnp.zeros((slot_count, width), jnp.bfloat16).at[target].set(copies)
    send = send.reshape(n_expert, 1, capacity, local_experts, width)
    share = n_expert * capacity
    arrived = lax.all_to_all(send, "expert", split_axis=0, concat_axis=1, tiled=True)
    own_rows = arrived.reshape(share, local_experts, width)
    rows_all = lax.all_gather(arrived, "tensor", axis=1, tiled=True).reshape(
        n_tensor * share, local_experts, width
    )
    pair = jnp.einsum("red,ecdf->recf", rows_all, expert_up, preferred_element_type=jnp.float32)
    gate_pre = pair[:, :, 0]
    active = (gate_pre * jax.nn.sigmoid(gate_pre) * pair[:, :, 1]).astype(jnp.bfloat16)
    summed = lax.psum_scatter(
        jnp.einsum("ref,efd->red", active, expert_down, preferred_element_type=jnp.float32).astype(
            jnp.bfloat16
        ),
        "tensor",
        scatter_dimension=0,
        tiled=True,
    )
    back_rows = lax.all_to_all(
        summed.reshape(n_expert, capacity, local_experts, width),
        "expert",
        split_axis=0,
        concat_axis=0,
        tiled=True,
    )
    returned = (
        back_rows.reshape(-1, width)[target].reshape(tok_rows, top_k, width).astype(jnp.float32)
    )
    output = attended + jnp.sum(gates[:, :, None] * returned, axis=1)
    grad_gates = jnp.sum(returned * cotangent[:, None, :], axis=-1)
    grad_rows = (gates[:, :, None] * cotangent[:, None, :]).astype(jnp.bfloat16)
    grad_probs = jnp.sum(choose * grad_gates[:, :, None], axis=1)
    grad_logits = probs * (grad_probs - jnp.sum(probs * grad_probs, axis=-1, keepdims=True))
    logits_low = grad_logits.astype(jnp.bfloat16)
    router_grad = jnp.einsum(
        "td,te->de", routed_low, logits_low, preferred_element_type=jnp.float32
    )
    grad_moe = jnp.einsum(
        "te,de->td", logits_low, router_weight, preferred_element_type=jnp.float32
    )
    send_grads = (
        jnp.zeros((slot_count, width), jnp.bfloat16).at[target].set(grad_rows.reshape(-1, width))
    )
    owner_grads = lax.all_to_all(
        send_grads.reshape(n_expert, capacity, local_experts, width),
        "expert",
        split_axis=0,
        concat_axis=0,
        tiled=True,
    )
    owner_grads = owner_grads.reshape(share, local_experts, width)
    row_piece = lax.all_gather(own_rows, "tensor", axis=0, tiled=True)
    grad_piece = lax.all_gather(owner_grads, "tensor", axis=0, tiled=True)
    pair_piece = jnp.einsum(
        "red,ecdf->recf", row_piece, expert_up, preferred_element_type=jnp.float32
    )
    gate_piece = pair_piece[:, :, 0]
    upper_piece = pair_piece[:, :, 1]
    active_piece = (gate_piece * jax.nn.sigmoid(gate_piece) * upper_piece).astype(jnp.bfloat16)
    grad_active = jnp.einsum(
        "red,efd->ref", grad_piece, expert_down, preferred_element_type=jnp.float32
    )
    grad_pair = swiglu_back(grad_active, gate_piece, upper_piece)
    up_acc = jnp.einsum("red,recf->ecdf", row_piece, grad_pair, preferred_element_type=jnp.float32)
    down_acc = jnp.einsum(
        "ref,red->efd", active_piece, grad_piece, preferred_element_type=jnp.float32
    )
    row_sum = lax.psum_scatter(
        jnp.einsum(
            "recf,ecdf->red", grad_pair, expert_up, preferred_element_type=jnp.float32
        ).astype(jnp.bfloat16),
        "tensor",
        scatter_dimension=0,
        tiled=True,
    )
    came_back = lax.all_to_all(
        row_sum.reshape(n_expert, capacity, local_experts, width),
        "expert",
        split_axis=0,
        concat_axis=0,
        tiled=True,
    )
    route_grads = came_back.reshape(-1, width)[target].reshape(tok_rows, top_k, width)
    grad_moe = grad_moe + jnp.sum(route_grads.astype(jnp.float32), axis=1)
    grad_attended, moe_gain_grad = norm_back(grad_moe, attended, inverse_moe, moe_gain)
    grad_attended = grad_attended + cotangent
    piece = lax.all_gather(grad_attended.astype(jnp.bfloat16), "tensor", axis=0, tiled=True)
    out_acc = jnp.einsum("tf,td->fd", mixed, piece, preferred_element_type=jnp.float32)
    grad_piece = jnp.einsum(
        "td,fd->tf", piece, out_weight, preferred_element_type=jnp.float32
    ).astype(jnp.bfloat16)
    out_grad = out_acc
    grad_heads = grad_piece.reshape(head_shape)
    recomputed = masked_scores()
    weights_wide = jnp.exp(recomputed - total)
    grad_weights = jnp.einsum(
        "qhd,khd->hqk", grad_heads, values_low, preferred_element_type=jnp.float32
    )
    grad_scores = (
        weights_wide * (grad_weights - jnp.sum(grad_weights * weights_wide, axis=-1, keepdims=True))
    ).astype(jnp.bfloat16)
    grad_values = jnp.einsum(
        "hqk,qhd->khd", weights_low, grad_heads, preferred_element_type=jnp.float32
    )
    grad_queries = (
        jnp.einsum("hqk,khd->qhd", grad_scores, keys_low, preferred_element_type=jnp.float32)
        * scale
    )
    grad_keys = (
        jnp.einsum("hqk,qhd->khd", grad_scores, queries, preferred_element_type=jnp.float32) * scale
    )
    grad_query_pre, query_gain_grad = norm_back(
        rotate(grad_queries, cosine, -sine), query_pre, query_inverse, gains[0]
    )
    grad_key_pre, key_gain_grad = norm_back(
        rotate(grad_keys, cosine, -sine), key_pre, key_inverse, gains[1]
    )
    grad_proj = jnp.stack(
        [
            grad_query_pre.reshape(length, head_width),
            grad_key_pre.reshape(length, head_width),
            grad_values.reshape(length, head_width),
        ],
        axis=1,
    ).astype(jnp.bfloat16)
    qkv_grad = jnp.einsum("td,tcf->cdf", normed_all, grad_proj, preferred_element_type=jnp.float32)
    qk_gain_grad = jnp.stack([query_gain_grad.reshape(-1), key_gain_grad.reshape(-1)])
    grad_normed = lax.psum_scatter(
        jnp.einsum("tcf,cdf->td", grad_proj, qkv_weight, preferred_element_type=jnp.float32).astype(
            jnp.bfloat16
        ),
        "tensor",
        scatter_dimension=0,
        tiled=True,
    ).astype(jnp.float32)
    grad_hidden, attn_gain_grad = norm_back(grad_normed, hidden, inverse_attn, attn_gain)
    grad_hidden = grad_hidden + grad_attended
    qkv_grad, qk_gain_grad, out_grad = (
        lax.psum(qkv_grad.astype(jnp.bfloat16), "expert").astype(jnp.float32),
        lax.psum(qk_gain_grad.astype(jnp.bfloat16), "expert").astype(jnp.float32),
        lax.psum(out_grad.astype(jnp.bfloat16), "expert").astype(jnp.float32),
    )
    attn_gain_grad, moe_gain_grad, router_grad = lax.psum(
        (attn_gain_grad, moe_gain_grad, router_grad), ("expert", "tensor")
    )
    return (
        output,
        grad_hidden,
        attn_gain_grad,
        qkv_grad,
        qk_gain_grad,
        out_grad,
        moe_gain_grad,
        router_grad,
        up_acc,
        down_acc,
    )


def solution(mesh):
    return jax.shard_map(
        shards,
        mesh=mesh,
        in_specs=(
            P(("expert", "tensor"), None),
            P("expert"),
            P(("expert", "tensor"), None),
            P(),
            P(None, None, "tensor"),
            P(None, "tensor"),
            P("tensor", None),
            P(),
            P(),
            P("expert", None, None, "tensor"),
            P("expert", "tensor", None),
            P(("expert", "tensor"), None),
        ),
        out_specs=(
            P(("expert", "tensor"), None),
            P(("expert", "tensor"), None),
            P(),
            P(None, None, "tensor"),
            P(None, "tensor"),
            P("tensor", None),
            P(),
            P(),
            P("expert", None, None, "tensor"),
            P("expert", "tensor", None),
        ),
        check_vma=False,
    )
```

profile of v0, /device:TPU:0, one launch (start us, length us, event | category | flops | bytes accessed | tf_op | source)
XLA Modules:
  0.0 2983.1 jit_solution(6514143365403038782)
XLA Ops:
  17.2 32.8 %all-gather.7.cloned.1.call-done = bf16[1024,2048]{1,0:T(8,128)(2,1)} async-done(((bf16[256,2048]{1,0:T(8,128)(2,1)}), bf16[1024,2048]{1,0:T(8,128)(2,1)}) %all-gather.7.cloned.1.call-update) | async-done | bytes 4194320 | tf_op jit(solution)/shard_map/all_gather | solution.py:83
  50.0 10.1 fusion.41
  80.7 6.6 fusion.18
  93.5 7.0 convolution_convert_fusion.3
  100.5 7.0 fusion.81
  108.7 18.3 reduce-window.19
  128.5 51.2 %reduce-scatter.5.cloned.1.call-done = f32[256,2048]{1,0:T(8,128)} async-done(((f32[1024,2048]{1,0:T(8,128)}), f32[256,2048]{1,0:T(8,128)}) %reduce-scatter.5.cloned.1.call-update) | async-done | bytes 2097168 | tf_op jit(solution)/shard_map/reduce_scatter | solution.py:113
  183.7 19.3 scatter_custom_fusion
  203.1 279.9 %all_to_all.27 = bf16[8,1,48,8,2048]{4,3,2,1,0:T(8,128)(2,1)} all-to-all(bf16[8,1,48,8,2048]{4,3,2,1,0:T(8,128)(2,1)} %bitcast.253), channel_id=1, replica_groups=mesh['expert'=8,'tensor'=4] {'expert'}, dimensions={0} | all-to-all | bytes 25165824 | tf_op jit(solution)/shard_map/all_to_all | solution.py:137
  483.0 16.1 copy.187
  502.1 20.9 scatter_custom_fusion.1
  523.0 277.5 %all_to_all.28 = bf16[8,48,8,2048]{3,2,1,0:T(8,128)(2,1)S(1)} all-to-all(bf16[8,48,8,2048]{3,2,1,0:T(8,128)(2,1)} %bitcast.252), channel_id=1, replica_groups=mesh['expert'=8,'tensor'=4] {'expert'}, dimensions={0} | all-to-all | bytes 25165824 | tf_op jit(solution)/shard_map/all_to_all | solution.py:178
  800.5 16.6 copy.186
  817.2 44.1 %copy.179 = bf16[32,1,48,8,2048]{4,2,0,3,1:T(8,128)(2,1)} copy(bf16[32,1,48,8,2048]{4,3,2,1,0:T(8,128)(2,1)} %all-gather.15.cloned.1.call-done) | data formatting | bytes 100663296 | tf_op jit(solution)/shard_map/all_gather | solution.py:139
  861.2 38.9 %convolution_bitcast_fusion = f32[1536,8,2,256]{3,0,2,1:T(8,128)} fusion(bf16[1536,8,2048,1]{2,0,3,1:T(8,128)(2,1)} %bitcast.249, bf16[8,2,2048,256]{3,2,1,0:T(8,128)(2,1)} %param.21), kind=kOutput, calls=%fused_computation.14 | convolution fusion | flops 25769803776 | bytes 92274688 | tf_op jit(solution)/shard_map/red,ecdf->recf/dot_general | solution.py:142
  900.2 30.6 %convert_bitcast_fusion = bf16[1536,8,2048]{2,0,1:T(8,128)(2,1)} fusion(bf16[8,256,2048]{2,1,0:T(8,128)(2,1)} %param.22, f32[1536,8,2,256]{3,0,2,1:T(8,128)} %convolution_bitcast_fusion), kind=kOutput, calls=%fused_computation.9 | convolution fusion | flops 12928942080 | bytes 83886080 | tf_op jit(solution)/shard_map/ref,efd->red/dot_general | solution.py:146
  931.1 146.7 %all-gather.11.cloned.1.call-done = bf16[1536,8,2048]{2,0,1:T(8,128)(2,1)} async-done(((bf16[384,8,2048]{2,0,1:T(8,128)(2,1)}), bf16[1536,8,2048]{2,0,1:T(8,128)(2,1)}) %all-gather.11.cloned.1.call-update) | async-done | bytes 50331664 | tf_op jit(solution)/shard_map/all_gather | solution.py:186
  1077.7 45.5 %fusion.13 = f32[1536,8,2,256]{3,0,1,2:T(8,128)} fusion(bf16[8,2,2048,256]{3,2,1,0:T(8,128)(2,1)} %param.21, bf16[1536,8,2048]{2,0,1:T(8,128)(2,1)} %all-gather.11.cloned.1.call-done), kind=kOutput, calls=%fused_computation.27 | convolution fusion | flops 25769803776 | bytes 92274688 | tf_op jit(solution)/shard_map/red,ecdf->recf/dot_general | solution.py:188
  1123.3 253.2 %all-gather.9.cloned.1.call-done = bf16[1536,8,2048]{2,0,1:T(8,128)(2,1)} async-done(((bf16[384,8,2048]{2,0,1:T(8,128)(2,1)}), bf16[1536,8,2048]{2,0,1:T(8,128)(2,1)}) %all-gather.9.cloned.1.call-update) | async-done | bytes 50331664 | tf_op jit(solution)/shard_map/all_gather | solution.py:187
  1376.5 48.4 %fusion.39 = (bf16[1536,8,1,256]{3,0,1,2:T(8,128)(2,1)}, bf16[1536,8,1,256]{3,0,1,2:T(8,128)(2,1)}) fusion(f32[1536,8,2,256]{3,0,1,2:T(8,128)} %fusion.13, bf16[1536,8,2048]{2,0,1:T(8,128)(2,1)} %all-gather.9.cloned.1.call-done, bf16[8,256,2048]{2,1,0:T(8,128)(2,1)} %param.22), kind=kOutput, calls=%fused_computation.58 | convolution fusion | flops 12925796352 | bytes 96468992 | tf_op jit(solution)/shard_map/red,efd->ref/dot_general | solution.py:194
  1424.9 41.0 %fusion.4 = bf16[1536,8,2048]{2,0,1:T(8,128)(2,1)} fusion(bf16[8,2,2048,256]{3,2,1,0:T(8,128)(2,1)} %param.21, bf16[1536,8,1,256]{3,0,1,2:T(8,128)(2,1)} %get-tuple-element.81, bf16[1536,8,1,256]{3,0,1,2:T(8,128)(2,1)} %get-tuple-element.80), kind=kOutput, calls=%fused_computation.10 | convolution fusion | flops 25801261056 | bytes 79691776 | tf_op jit(solution)/shard_map/recf,ecdf->red/dot_general | solution.py:203
  1465.9 256.4 %reduce-scatter.7.cloned.1.call-done = bf16[384,8,2048]{2,0,1:T(8,128)(2,1)} async-done(((bf16[1536,8,2048]{2,0,1:T(8,128)(2,1)}), bf16[384,8,2048]{2,0,1:T(8,128)(2,1)}) %reduce-scatter.7.cloned.1.call-update) | async-done | bytes 12582928 | tf_op jit(solution)/shard_map/reduce_scatter | solution.py:145
  1722.3 11.3 copy.181
  1739.4 328.8 %reduce-scatter.9.cloned.1.call-done = bf16[384,8,2048]{2,0,1:T(8,128)(2,1)} async-done(((bf16[1536,8,2048]{2,0,1:T(8,128)(2,1)}), bf16[384,8,2048]{2,0,1:T(8,128)(2,1)}) %reduce-scatter.9.cloned.1.call-update) | async-done | bytes 12582928 | tf_op jit(solution)/shard_map/reduce_scatter | solution.py:202
  2068.1 10.7 copy.190
  2078.9 6.1 all-to-all-start.3
  2085.1 14.6 copy.182
  2099.6 22.5 gather_fusion
  2122.2 9.7 fusion.9
  2132.1 225.8 %all-to-all-done.3 = bf16[8,48,8,2048]{3,1,2,0:T(8,128)(2,1)} async-done(((bf16[8,48,8,2048]{3,1,2,0:T(8,128)(2,1)}), bf16[8,48,8,2048]{3,1,2,0:T(8,128)(2,1)}, u32[]{:S(2)}, u32[]{:S(2)}) %all-to-all-start.3) | async-done | bytes 12582944 | tf_op jit(solution)/shard_map/all_to_all | solution.py:210
  2358.0 14.5 copy.191
  2372.5 22.7 gather_fusion.1
  2395.2 11.3 convert_reduce_fusion
  2413.9 32.7 %all-gather.13.cloned.1.call-done = bf16[1024,2048]{1,0:T(8,128)(2,1)} async-done(((bf16[256,2048]{1,0:T(8,128)(2,1)}), bf16[1024,2048]{1,0:T(8,128)(2,1)}) %all-gather.13.cloned.1.call-update) | async-done | bytes 4194320 | tf_op jit(solution)/shard_map/all_gather | solution.py:221
  2451.1 9.6 convolution_convert_fusion.1
  2460.8 12.7 multiply_reduce_fusion
  2473.5 12.9 multiply_convert_fusion
  2512.3 8.8 bitcast_convert_fusion.1
  2521.2 6.3 convolution_convert_fusion
  2527.5 8.6 convert_bitcast_fusion.1
  2536.1 41.3 %fusion.5 = f32[8,2,2048,256]{2,3,1,0:T(8,128)} fusion(bf16[1536,8,2048]{2,0,1:T(8,128)(2,1)} %all-gather.11.cloned.1.call-done, bf16[1536,8,1,256]{3,0,1,2:T(8,128)(2,1)} %get-tuple-element.81, bf16[1536,8,1,256]{3,0,1,2:T(8,128)(2,1)} %get-tuple-element.80), kind=kOutput, calls=%fused_computation.13 | convolution fusion | flops 25776095232 | bytes 96468992 | tf_op jit(solution)/shard_map/red,recf->ecdf/dot_general | solution.py:198
  2577.5 31.9 %copy.208 = f32[8,2,2048,256]{3,2,1,0:T(8,128)} copy(f32[8,2,2048,256]{2,3,1,0:T(8,128)} %fusion.5) | data formatting | bytes 67108864
  2609.4 34.0 %fusion.33 = f32[8,256,2048]{2,1,0:T(8,128)} fusion(bf16[1536,8,2048]{2,0,1:T(8,128)(2,1)} %all-gather.9.cloned.1.call-done, f32[1536,8,2,256]{3,0,1,2:T(8,128)} %fusion.13), kind=kOutput, calls=%fused_computation.52 | convolution fusion | flops 12903776256 | bytes 92274688 | tf_op jit(solution)/shard_map/ref,red->efd/dot_general | solution.py:199
  2644.5 23.2 psum.44
  2675.0 166.7 %all-reduce.7.cloned.1.call-done = (bf16[3,2048,512]{1,2,0:T(8,128)(2,1)}, bf16[512,2048]{1,0:T(8,128)(2,1)}) async-done(((bf16[3,2048,512]{1,2,0:T(8,128)(2,1)}, bf16[512,2048]{1,0:T(8,128)(2,1)}), (bf16[3,2048,512]{1,2,0:T(8,128)(2,1)}, bf16[512,2048]{1,0:T(8,128)(2,1)})) %all-reduce.7.cloned.1.call-update) | async-done | bytes 8388624 | tf_op jit(solution)/shard_map/psum | solution.py:273
  2845.9 9.4 copy.207
  2855.3 39.4 %all-reduce = (f32[2048]{0:T(1024)}, f32[2048]{0:T(1024)}) all-reduce(f32[2048]{0:T(1024)S(1)} %get-tuple-element.66, f32[2048]{0:T(1024)S(1)} %copy-done.48), channel_id=1, replica_groups=mesh['expert'=8,'tensor'=4] {'expert','tensor'}, use_global_device_ids=true, to_apply=%region_31.32 | all-reduce | flops 4096 | bytes 32768 | tf_op jit(solution)/shard_map/psum | solution.py:277
  2894.7 79.8 %all-reduce.5.cloned.1.call-done = f32[2048,64]{0,1:T(8,128)} async-done(((f32[2048,64]{0,1:T(8,128)}), f32[2048,64]{0,1:T(8,128)}) %all-reduce.5.cloned.1.call-update) | async-done | bytes 524304 | tf_op jit(solution)/shard_map/psum | solution.py:277
  (244 shorter events, 104.5 us)
Async XLA Ops:
  7.2 93.3 %copy-start = (bf16[512,2048]{1,0:T(8,128)(2,1)S(1)}, bf16[512,2048]{1,0:T(8,128)(2,1)}, u32[]{:S(2)}) copy-start(bf16[512,2048]{1,0:T(8,128)(2,1)} %param.18) | copy-start | bytes 6291460
  7.2 42.7 %all-gather.7.cloned.1.call-start = ((), (), s32[]{:S(2)}) async-start(), calls=%async_computation.8 | async-start | bytes 5242880 | tf_op jit(solution)/shard_map/all_gather | solution.py:83
  12.6 167.0 %reduce-scatter.5.cloned.1.call-start = ((), (), s32[]{:S(2)}) async-start(), calls=%async_computation.9 | async-start | bytes 10485760 | tf_op jit(solution)/shard_map/reduce_scatter | solution.py:113
  13.4 59.7 %copy-start.51 = (f32[1,512]{1,0:T(1,128)}, f32[1,512]{1,0:T(1,128)S(1)}, u32[]{:S(2)}) copy-start(f32[1,512]{1,0:T(1,128)S(1)} %get-tuple-element.102) | copy-start | bytes 6148
  13.4 59.7 %copy-start.53 = (f32[1,512]{1,0:T(1,128)}, f32[1,512]{1,0:T(1,128)S(1)}, u32[]{:S(2)}) copy-start(f32[1,512]{1,0:T(1,128)S(1)} %get-tuple-element.103) | copy-start | bytes 6148
  17.2 73.9 %copy-start.11 = (pred[1024,1024]{0,1:T(8,128)(4,1)}, pred[1024,1024]{0,1:T(8,128)(4,1)S(1)}, u32[]{:S(2)}) copy-start(pred[1024,1024]{0,1:T(8,128)(4,1)S(1)} %fusion.44) | copy-start | bytes 3145732
  87.3 6.2 copy-start.1
  91.0 9.5 copy-start.40
  107.6 709.6 %all-gather.15.cloned.1.call-start = ((), (), s32[]{:S(2)}) async-start(), calls=%async_computation.17 | async-start | bytes 62914560 | tf_op jit(solution)/shard_map/all_gather | solution.py:139
  127.3 56.2 %copy-start.42 = (f32[2048]{0:T(1024)S(1)}, f32[2048]{0:T(1024)}, u32[]{:S(2)}) copy-start(f32[2048]{0:T(1024)} %param.19) | copy-start | bytes 24580
  128.5 373.7 %copy-start.49 = (s32[2048,1]{0,1:T(1,128)}, s32[2048,1]{0,1:T(1,128)S(1)}, u32[]{:S(2)}) copy-start(s32[2048,1]{0,1:T(1,128)S(1)} %compare_select_fusion) | copy-start | bytes 24580
  182.2 20.9 copy-start.61
  183.7 315.4 %copy-start.9 = (bf16[256,2048]{1,0:T(8,128)(2,1)}, bf16[256,2048]{1,0:T(8,128)(2,1)S(1)}, u32[]{:S(2)}) copy-start(bf16[256,2048]{1,0:T(8,128)(2,1)S(1)} %multiply_convert_fusion.3) | copy-start | bytes 3145732
  483.0 594.7 %all-gather.11.cloned.1.call-start = ((), (), s32[]{:S(2)}) async-start(), calls=%async_computation.12 | async-start | bytes 62914560 | tf_op jit(solution)/shard_map/all_gather | solution.py:186
  499.1 877.3 %all-gather.9.cloned.1.call-start = ((), (), s32[]{:S(2)}) async-start(), calls=%async_computation.11 | async-start | bytes 62914560 | tf_op jit(solution)/shard_map/all_gather | solution.py:187
  502.0 21.0 copy-start.26
  817.1 905.2 %reduce-scatter.7.cloned.1.call-start = ((), (), s32[]{:S(2)}) async-start(), calls=%async_computation.10 | async-start | bytes 62914560 | tf_op jit(solution)/shard_map/reduce_scatter | solution.py:145
  930.8 1137.3 %reduce-scatter.9.cloned.1.call-start = ((), (), s32[]{:S(2)}) async-start(), calls=%async_computation.13 | async-start | bytes 62914560 | tf_op jit(solution)/shard_map/reduce_scatter | solution.py:202
  1733.6 345.3 %all-to-all-start.1 = ((bf16[8,48,8,2048]{3,1,2,0:T(8,128)(2,1)}), bf16[8,48,8,2048]{3,1,2,0:T(8,128)(2,1)}, u32[]{:S(2)}, u32[]{:S(2)}) async-start(bf16[8,48,8,2048]{3,1,2,0:T(8,128)(2,1)} %copy.181), calls=%async_computation.3 | async-start | bytes 25165824 | tf_op jit(solution)/shard_map/all_to_all | solution.py:153
  2078.9 6.2 copy-start.50
  2078.9 279.1 %all-to-all-start.3 = ((bf16[8,48,8,2048]{3,1,2,0:T(8,128)(2,1)}), bf16[8,48,8,2048]{3,1,2,0:T(8,128)(2,1)}, u32[]{:S(2)}, u32[]{:S(2)}) async-start(bf16[8,48,8,2048]{3,1,2,0:T(8,128)(2,1)} %copy.190), calls=%async_computation.6 | async-start | bytes 25165824 | tf_op jit(solution)/shard_map/all_to_all | solution.py:210
  2085.0 361.5 %all-gather.13.cloned.1.call-start = ((), (), s32[]{:S(2)}) async-start(), calls=%async_computation.14 | async-start | bytes 5242880 | tf_op jit(solution)/shard_map/all_gather | solution.py:221
  2099.6 22.5 copy-start.27
  2122.2 9.8 copy-start.46
  2122.2 9.8 copy-start.25
  2122.2 9.8 copy-start.56
  2122.2 9.8 copy-start.58
  2132.1 274.4 %copy-start.34 = (bf16[256,64]{0,1:T(8,128)(2,1)}, bf16[256,64]{0,1:T(8,128)(2,1)S(1)}, u32[]{:S(2)}) copy-start(bf16[256,64]{0,1:T(8,128)(2,1)S(1)} %multiply_convert_fusion.5) | copy-start | bytes 98308
  2395.2 11.3 copy-start.31
  2395.2 11.3 copy-start.43
  2395.2 11.3 copy-start.62
  2413.8 37.3 %copy-start.12 = (pred[1024,1024]{0,1:T(8,128)(4,1)S(1)}, pred[1024,1024]{0,1:T(8,128)(4,1)}, u32[]{:S(2)}) copy-start(pred[1024,1024]{0,1:T(8,128)(4,1)} %copy-done.11) | copy-start | bytes 3145732
  2413.8 37.3 %copy-start.41 = (f32[4,1024]{1,0:T(4,128)S(1)}, f32[4,1024]{1,0:T(4,128)}, u32[]{:S(2)}) copy-start(f32[4,1024]{1,0:T(4,128)} %copy-done.40) | copy-start | bytes 49156
  2413.8 254.5 %reduce-scatter.11.cloned.1.call-start = ((), (), s32[]{:S(2)}) async-start(), calls=%async_computation.15 | async-start | bytes 5242880 | tf_op jit(solution)/shard_map/reduce_scatter | solution.py:262
  2451.1 9.6 copy-start.21
  2473.5 13.0 copy-start.32
  2473.5 13.0 copy-start.33
  2505.6 6.7 slice-start
  2521.1 320.6 %all-reduce.7.cloned.1.call-start = ((), (), s32[]{:S(2)}) async-start(), calls=%async_computation.18 | async-start | bytes 16777216 | tf_op jit(solution)/shard_map/psum | solution.py:273
  2521.1 6.3 copy-start.29
  2521.1 6.3 copy-start.64
  2521.2 6.3 copy-start.66
  2536.1 438.4 %all-reduce.5.cloned.1.call-start = ((), (), s32[]{:S(2)}) async-start(), calls=%async_computation.16 | async-start | bytes 1048576 | tf_op jit(solution)/shard_map/psum | solution.py:277
  2609.4 34.0 %copy-start.10 = (bf16[256,2048]{1,0:T(8,128)(2,1)S(1)}, bf16[256,2048]{1,0:T(8,128)(2,1)}, u32[]{:S(2)}) copy-start(bf16[256,2048]{1,0:T(8,128)(2,1)} %copy-done.9) | copy-start | bytes 3145732
  2609.4 34.0 %copy-start.35 = (bf16[256,64]{0,1:T(8,128)(2,1)S(1)}, bf16[256,64]{0,1:T(8,128)(2,1)}, u32[]{:S(2)}) copy-start(bf16[256,64]{0,1:T(8,128)(2,1)} %copy-done.34) | copy-start | bytes 98308
  2609.4 58.9 %copy-start.44 = (f32[2048]{0:T(1024)S(1)}, f32[2048]{0:T(1024)}, u32[]{:S(2)}) copy-start(f32[2048]{0:T(1024)} %param.15) | copy-start | bytes 24580
  2609.4 58.9 %copy-start.60 = (f32[256]{0:T(256)S(1)}, f32[256]{0:T(256)}, u32[]{:S(2)}) copy-start(f32[256]{0:T(256)} %copy-done.59) | copy-start | bytes 3076
  2845.9 9.5 copy-start.48
  (34 other events, 93.4 us)
Sparse Core Ops, SparseCore 0:
  12.7 37.1 all-gather.6
  107.7 71.9 reduce-scatter.4
  483.1 295.2 all-gather.14
  780.5 297.1 all-gather.10
  1079.2 297.1 all-gather.8
  1379.1 343.1 reduce-scatter.6
  1724.9 343.1 reduce-scatter.8
  2413.9 32.5 all-gather.12
  2521.2 44.4 reduce-scatter.10
  2570.2 271.4 all-reduce.6
  2847.6 126.8 all-reduce.4
where the time goes:
time: 2990 us; the launch traced here: 2980 us
  waiting for transfers between devices  1570 us (53%)
  blocking collectives  620 us (21%)
  matrix products  372 us (12%)
  local copies, waits for them, and re-layouts  264 us (9%)
  other arithmetic  125 us (4%)
    reduce_scatter x1, waiting for transfers between devices, shards(): lax.psum_scatter(jnp.einsum('recf,ecdf->red', grad_pair, expert_up, prefe...  329 us
    all_to_all x1, blocking collectives, shards(): lax.all_to_all(send, 'expert', split_axis=0, concat_axis=1, tiled=True)  280 us
    all_to_all x1, blocking collectives, shards(): lax.all_to_all(send_grads.reshape(n_expert, capacity, local_experts, widt...  278 us
    reduce_scatter x1, waiting for transfers between devices, shards(): lax.psum_scatter(jnp.einsum('ref,efd->red', active, expert_down, preferre...  256 us
    all_gather x1, waiting for transfers between devices, shards(): grad_piece = lax.all_gather(owner_grads, 'tensor', axis=0, tiled=True)  253 us
    all_to_all x1, waiting for transfers between devices, shards(): lax.all_to_all(row_sum.reshape(n_expert, capacity, local_experts, width),...  226 us
    psum x1, waiting for transfers between devices, shards(): lax.psum(qkv_grad.astype(jnp.bfloat16), 'expert').astype(jnp.float32)  167 us
    all_gather x1, waiting for transfers between devices, shards(): row_piece = lax.all_gather(own_rows, 'tensor', axis=0, tiled=True)  147 us
  transfers between devices with their start and end apart: 13, of which 10 were waited for; matrix products, arithmetic and copies ran while one was open for 18% of the time, Pallas kernels for 0%

commit v1 on v0

v1 whole, which is shorter than its diff:
```python
import functools
import math

import jax
import jax.numpy as jnp
from jax import lax
from jax.experimental import pallas as pl
from jax.experimental.pallas import tpu as pltpu
from jax.sharding import Mesh, PartitionSpec as P

HEAD_DIM = 128
ALL = ("z", "y", "x", "core")
EXPERT = ("z", "y")
TENSOR = ("x", "core")
LOW = jnp.bfloat16
WIDE = jnp.float32


EPSILON = 1e-05
THETA = 10000.0


def normalize(values, gain):
    inverse = lax.rsqrt(jnp.mean(values * values, axis=-1, keepdims=True) + EPSILON)
    return (values * inverse * gain, inverse)


def norm_back(grad_out, values, inverse, gain):
    scaled = values * inverse
    weighted = grad_out * gain
    grad_in = inverse * (weighted - scaled * jnp.mean(weighted * scaled, axis=-1, keepdims=True))
    return (grad_in, jnp.sum(grad_out * scaled, axis=0))


def doc_positions(segment_ids):
    index = jnp.arange(segment_ids.shape[0], dtype=jnp.int32)
    starts = jnp.concatenate([jnp.ones((1,), jnp.bool_), segment_ids[1:] != segment_ids[:-1]])
    first = lax.cummax(jnp.where(starts, index, 0), axis=0)
    return index - first


def rope_tables(positions, half):
    freq = jnp.exp(-math.log(THETA) * jnp.arange(half, dtype=jnp.float32) / half)
    angle = positions.astype(jnp.float32)[:, None] * freq[None, :]
    return (jnp.cos(angle)[:, None, :], jnp.sin(angle)[:, None, :])


def rotate(values, cosine, sine):
    half = values.shape[-1] // 2
    first = values[..., :half]
    second = values[..., half:]
    return jnp.concatenate(
        [first * cosine - second * sine, second * cosine + first * sine], axis=-1
    )


def add_low(*terms):
    total = terms[0].astype(WIDE)
    for term in terms[1:]:
        total = total + term.astype(WIDE)
    return total.astype(terms[0].dtype)


def swap(values, axis):
    return lax.ppermute(values, axis, [(0, 1), (1, 0)])


def pick(parts, index):
    last = parts.shape[0] - 1
    return lax.dynamic_index_in_dim(parts, jnp.clip(index, 0, last), 0, keepdims=False)


def line_scatter(parts, axis):
    n = lax.axis_size(axis)
    me = lax.axis_index(axis)
    up = down = None
    for step in range(1, n):
        block = pick(parts, me + n - step)
        block = block if up is None else add_low(block, up)
        up = lax.ppermute(block, axis, [(i, i + 1) for i in range(step)])
        block = pick(parts, me - n + step)
        block = block if down is None else add_low(block, down)
        down = lax.ppermute(block, axis, [(i, i - 1) for i in range(n - step, n)])
    return add_low(pick(parts, me), up, down)


def line_gather(values, axis):
    n = lax.axis_size(axis)
    me = lax.axis_index(axis)
    below, above = [], []
    up = down = values
    for step in range(1, n):
        up = lax.ppermute(up, axis, [(i, i + 1) for i in range(step - 1, n - 1)])
        down = lax.ppermute(down, axis, [(i, i - 1) for i in range(1, n - step + 1)])
        below.insert(0, up)
        above.append(down)
    return lax.dynamic_slice_in_dim(jnp.stack(below + [values] + above), n - 1 - me, n, 0)


def relative(axis):
    return lax.axis_size(axis) == 2


def coordinate(axis):
    places = jnp.arange(lax.axis_size(axis), dtype=jnp.int32)
    return places ^ lax.axis_index(axis) if relative(axis) else places


def block_order(axes):
    stride = {}
    step = 1
    for axis in reversed(ALL):
        stride[axis] = step
        step *= lax.axis_size(axis)
    order = jnp.zeros((1,), jnp.int32)
    for axis in axes:
        order = (order[:, None] + coordinate(axis)[None, :] * stride[axis]).reshape(-1)
    return order


def scatter_axis(parts, axis):
    if relative(axis):
        return add_low(parts[0], swap(parts[1], axis))
    return line_scatter(parts, axis)


def scatter_all(keep, send, axes):
    total = add_low(keep, swap(send, "core"))
    for axis in axes:
        total = scatter_axis(total, axis)
    return total


def sum_all(values):
    for axis in ("core", "x", "y", "z"):
        n = lax.axis_size(axis)
        step = 1
        while step < n:
            values = values + lax.ppermute(values, axis, [(i, i ^ step) for i in range(n)])
            step *= 2
    return values


def sum_expert(values):
    rows, columns = values.shape
    ny, nz = lax.axis_size("y"), lax.axis_size("z")
    parts = values.reshape(ny, nz, rows // (ny * nz), columns)
    if relative("y"):
        me = lax.axis_index("y")
        own = add_low(pick(parts, me), swap(pick(parts, 1 - me), "y"))
    else:
        own = line_scatter(parts, "y")
    own = line_gather(line_scatter(own, "z"), "z")
    if relative("y"):
        other = swap(own, "y")
        first = jnp.where(me == 0, own, other)
        second = jnp.where(me == 0, other, own)
        parts = jnp.stack([first, second])
    else:
        parts = line_gather(own, "y")
    return parts.reshape(rows, columns).astype(WIDE)


NT = (((1,), (1,)), ((), ()))
TN = (((0,), (0,)), ((), ()))


def dot(left, right, dims=None):
    if dims is None:
        return jnp.dot(left, right, preferred_element_type=WIDE)
    return lax.dot_general(left, right, dims, preferred_element_type=WIDE)


def params(megabytes):
    return pltpu.CompilerParams(vmem_limit_bytes=megabytes << 20)


def cost(flops, moved):
    return pl.CostEstimate(flops=int(flops), bytes_accessed=int(moved), transcendentals=0)


def dispatch_kernel(order_ref, select_ref, rows_ref, out_ref):
    experts, capacity, width = out_ref.shape
    picked = dot(select_ref[0], rows_ref[0])
    out_ref[...] = picked.astype(LOW).reshape(experts, capacity, width)


def dispatch(order, select, rows, experts):
    blocks, slots, tokens = select.shape
    width = rows.shape[-1]
    capacity = slots // experts
    return pl.pallas_call(
        dispatch_kernel,
        grid_spec=pltpu.PrefetchScalarGridSpec(
            num_scalar_prefetch=1,
            grid=(blocks,),
            in_specs=[
                pl.BlockSpec((1, slots, tokens), lambda b, order: (b, 0, 0)),
                pl.BlockSpec((1, tokens, width), lambda b, order: (order[b], 0, 0)),
            ],
            out_specs=pl.BlockSpec((experts, capacity, width), lambda b, order: (0, b, 0)),
        ),
        out_shape=jax.ShapeDtypeStruct((experts, blocks * capacity, width), LOW),
        compiler_params=params(32),
        cost_estimate=cost(2 * blocks * slots * tokens * width, 2 * blocks * (slots + tokens) * width),
        name="dispatch",
    )(order, select, rows.reshape(blocks, tokens, width))


def row_tile(rows):
    return max(t for t in range(128, 513, 128) if rows % t == 0)


def grad_active_kernel(rows_ref, down_ref, out_ref):
    out_ref[0] = dot(rows_ref[0], down_ref[0], NT)


def grad_active(rows, expert_down):
    experts, count, width = rows.shape
    units = expert_down.shape[1]
    tile = row_tile(count)
    return pl.pallas_call(
        grad_active_kernel,
        grid=(experts, count // tile),
        in_specs=[
            pl.BlockSpec((1, tile, width), lambda e, r: (e, r, 0)),
            pl.BlockSpec((1, units, width), lambda e, r: (e, 0, 0)),
        ],
        out_specs=pl.BlockSpec((1, tile, units), lambda e, r: (e, r, 0)),
        out_shape=jax.ShapeDtypeStruct((experts, count, units), WIDE),
        compiler_params=params(32),
        cost_estimate=cost(2 * rows.size * units, 2 * rows.size),
        name="grad_active",
    )(rows, expert_down)


def hidden_kernel(rows_ref, up_ref, grad_ref, gate_ref, act_ref, pair_ref, gate_grad_ref):
    rows = rows_ref[0]
    gate_pre = dot(rows, up_ref[0, 0])
    upper = dot(rows, up_ref[0, 1])
    gate = gate_ref[0]
    sigma = jax.nn.sigmoid(gate_pre)
    silu = gate_pre * sigma
    active = silu * upper
    grad = grad_ref[0]
    gated = gate * grad
    act_ref[0] = (gate * active).astype(LOW)
    pair_ref[0, 0] = (gated * upper * (sigma * (1.0 + gate_pre * (1.0 - sigma)))).astype(LOW)
    pair_ref[0, 1] = (gated * silu).astype(LOW)
    gate_grad_ref[0] = jnp.sum(active * grad, axis=-1, keepdims=True)


def hidden_units(rows, expert_up, grads, gates):
    experts, count, width = rows.shape
    units = expert_up.shape[-1]
    tile = row_tile(count)
    return pl.pallas_call(
        hidden_kernel,
        grid=(experts, count // tile),
        in_specs=[
            pl.BlockSpec((1, tile, width), lambda e, r: (e, r, 0)),
            pl.BlockSpec((1, 2, width, units), lambda e, r: (e, 0, 0, 0)),
            pl.BlockSpec((1, tile, units), lambda e, r: (e, r, 0)),
            pl.BlockSpec((1, tile, 1), lambda e, r: (e, r, 0)),
        ],
        out_specs=[
            pl.BlockSpec((1, tile, units), lambda e, r: (e, r, 0)),
            pl.BlockSpec((1, 2, tile, units), lambda e, r: (e, 0, r, 0)),
            pl.BlockSpec((1, tile, 1), lambda e, r: (e, r, 0)),
        ],
        out_shape=[
            jax.ShapeDtypeStruct((experts, count, units), LOW),
            jax.ShapeDtypeStruct((experts, 2, count, units), LOW),
            jax.ShapeDtypeStruct((experts, count, 1), WIDE),
        ],
        compiler_params=params(40),
        cost_estimate=cost(4 * rows.size * units, 2 * rows.size),
        name="hidden_units",
    )(rows, expert_up, grads, gates)


def combine_kernel(transposed, experts, lhs_ref, weight_ref, select_ref, keep_ref, send_ref, rows):
    step = pl.program_id(0)
    blocks, slots, columns = rows.shape
    capacity = slots // experts
    group = select_ref.shape[0]
    pairs = lhs_ref.shape[1]
    many = 8

    @pl.when(step < experts)
    def _():
        start = pl.multiple_of(step * capacity, capacity)
        for first in range(0, blocks, many):
            piece = pl.ds(first * capacity, many * capacity)
            total = None
            for i in range(pairs):
                term = dot(lhs_ref[0, i, piece, :], weight_ref[0, i], NT if transposed else None)
                total = term if total is None else total + term
            rows[first : first + many, pl.ds(start, capacity), :] = total.astype(LOW).reshape(
                many, capacity, columns
            )

    @pl.when(step >= experts)
    def _():
        at = (step - experts) * group
        half = (blocks // group) // 2

        def put(ref):
            for i in range(group):
                ref[0, i] = dot(select_ref[i], rows[at + i]).astype(LOW)

        pl.when(step - experts < half)(lambda: put(keep_ref))
        pl.when(step - experts >= half)(lambda: put(send_ref))


def combine(lhs, weight, select, first, columns, transposed, sizes, flip):
    experts, pairs, count, units = lhs.shape
    blocks, tokens, slots = select.shape
    nx, ny, nz = sizes
    half = nx * ny
    at = first // columns

    def place(group):
        return group % ny * nx + group // ny if flip else group

    def keep_map(s):
        return (place(jnp.clip(s - experts, 0, half - 1)), 0, 0, 0)

    def send_map(s):
        return (place(jnp.clip(s - experts - half, 0, half - 1)), 0, 0, 0)

    if transposed:
        weight_spec = pl.BlockSpec(
            (1, pairs, columns, units), lambda s: (jnp.minimum(s, experts - 1), 0, at, 0)
        )
    else:
        weight_spec = pl.BlockSpec(
            (1, pairs, units, columns), lambda s: (jnp.minimum(s, experts - 1), 0, 0, at)
        )
    keep, send = pl.pallas_call(
        functools.partial(combine_kernel, transposed, experts),
        grid=(experts + 2 * half,),
        in_specs=[
            pl.BlockSpec(
                (1, pairs, count, units), lambda s: (jnp.minimum(s, experts - 1), 0, 0, 0)
            ),
            weight_spec,
            pl.BlockSpec((nz, tokens, slots), lambda s: (jnp.clip(s - experts, 0, 2 * half - 1), 0, 0)),
        ],
        out_specs=[
            pl.BlockSpec((1, nz, tokens, columns), keep_map),
            pl.BlockSpec((1, nz, tokens, columns), send_map),
        ],
        out_shape=[jax.ShapeDtypeStruct((half, nz, tokens, columns), LOW)] * 2,
        scratch_shapes=[pltpu.VMEM((blocks, slots, columns), LOW)],
        compiler_params=params(48),
        cost_estimate=cost(
            2 * lhs.size * columns + 2 * select.size * columns,
            2 * lhs.size + 2 * select.size + 4 * half * nz * tokens * columns,
        ),
        name="combine",
    )(lhs, weight, select)
    shape = (ny, nx, nz, tokens, columns) if flip else (nx, ny, nz, tokens, columns)
    return keep.reshape(shape), send.reshape(shape)


def weight_grad_kernel(left_ref, right_ref, out_ref):
    out_ref[0, 0] = dot(left_ref[0, 0], right_ref[0, 0], TN)


def weight_grad(left, right, tile_left, tile_right):
    experts, left_pairs, count, left_width = left.shape
    _, right_pairs, _, right_width = right.shape
    pairs = max(left_pairs, right_pairs)

    def left_map(e, i, j, p):
        return (e, p if left_pairs > 1 else 0, 0, i)

    def right_map(e, i, j, p):
        return (e, p if right_pairs > 1 else 0, 0, j)

    return pl.pallas_call(
        weight_grad_kernel,
        grid=(experts, left_width // tile_left, right_width // tile_right, pairs),
        in_specs=[
            pl.BlockSpec((1, 1, count, tile_left), left_map),
            pl.BlockSpec((1, 1, count, tile_right), right_map),
        ],
        out_specs=pl.BlockSpec((1, 1, tile_left, tile_right), lambda e, i, j, p: (e, p, i, j)),
        out_shape=jax.ShapeDtypeStruct((experts, pairs, left_width, right_width), WIDE),
        compiler_params=params(48),
        cost_estimate=cost(
            2 * experts * pairs * count * left_width * right_width,
            2 * left.size + 2 * right.size + 4 * experts * pairs * left_width * right_width,
        ),
        name="weight_grad",
    )(left, right)


def shards(
    hidden,
    segments,
    routes,
    attn_gain,
    qkv_weight,
    qk_gain,
    out_weight,
    moe_gain,
    router_weight,
    expert_up,
    expert_down,
    cotangent,
):
    tok_rows, width = hidden.shape
    length = segments.shape[0]
    head_width = out_weight.shape[0]
    local_heads = head_width // HEAD_DIM
    local_experts = expert_up.shape[0]
    all_experts = router_weight.shape[1]
    nz, ny, nx, ncore = (lax.axis_size(axis) for axis in ALL)
    n_tensor = nx * ncore
    blocks = nz * ny * n_tensor
    capacity = max(2, 3 * length // (16 * n_tensor))
    capacity = -(-capacity // 16) * 16
    slots = local_experts * capacity
    scale = HEAD_DIM ** (-0.5)
    expert_index = lax.axis_index("z") * ny + lax.axis_index("y")
    normed, inverse_attn = normalize(hidden, attn_gain)
    normed_all = lax.all_gather(normed.astype(LOW), TENSOR, axis=0, tiled=True)
    cotangent_all = lax.all_gather(cotangent.astype(LOW), ALL, axis=0, tiled=True)
    routes_all = lax.all_gather(routes, ALL, axis=0, tiled=True)

    order = block_order(("core", "x", "y", "z"))
    own_experts = expert_index * local_experts + jnp.arange(local_experts, dtype=jnp.int32)
    named = routes_all.reshape(blocks, tok_rows, -1)[order]
    member = jnp.any(named[:, None, :, :] == own_experts[None, :, None, None], axis=-1)
    token = jnp.arange(tok_rows, dtype=jnp.int32)
    earlier = (token[:, None] < token[None, :]).astype(LOW)
    rank = jnp.einsum("beu,ut->bet", member.astype(LOW), earlier, preferred_element_type=WIDE)
    rank = jnp.where(member, rank.astype(jnp.int32), -1)
    slot = jnp.arange(capacity, dtype=jnp.int32)
    chosen = rank[:, :, None, :] == slot[None, None, :, None]
    select = chosen.reshape(blocks, slots, tok_rows).astype(LOW)
    rank_back = jnp.swapaxes(rank, 1, 2)
    select_back = (rank_back[:, :, :, None] == slot).reshape(blocks, tok_rows, slots).astype(LOW)

    projected = jnp.einsum("td,cdf->tcf", normed_all, qkv_weight, preferred_element_type=WIDE)
    head_shape = (length, local_heads, HEAD_DIM)
    gains = qk_gain.reshape(2, local_heads, HEAD_DIM)
    cosine, sine = rope_tables(doc_positions(segments), HEAD_DIM // 2)
    query_pre = projected[:, 0].reshape(head_shape)
    key_pre = projected[:, 1].reshape(head_shape)
    query_normed, query_inverse = normalize(query_pre, gains[0])
    key_normed, key_inverse = normalize(key_pre, gains[1])
    queries = rotate(query_normed, cosine, sine).astype(LOW)
    keys_low = rotate(key_normed, cosine, sine).astype(LOW)
    values_low = projected[:, 2].reshape(head_shape).astype(LOW)
    index = jnp.arange(length, dtype=jnp.int32)
    allowed = ((segments[:, None] == segments[None, :]) & (index[:, None] >= index[None, :]))[None]

    def masked_scores():
        scores = jnp.einsum("qhd,khd->hqk", queries, keys_low, preferred_element_type=WIDE) * scale
        return jnp.where(allowed, scores, -1e30)

    masked = masked_scores()
    top = jnp.max(masked, axis=-1, keepdims=True)
    total = jnp.log(jnp.sum(jnp.exp(masked - top), axis=-1, keepdims=True)) + top
    weights_low = jnp.exp(masked - total).astype(LOW)
    mixed = jnp.einsum("hqk,khd->qhd", weights_low, values_low, preferred_element_type=WIDE)
    mixed = mixed.reshape(length, head_width).astype(LOW)

    def scatter_tensor(partial):
        parts = partial.reshape(nx, ncore, tok_rows, width)
        core = lax.axis_index("core")
        own = lax.dynamic_index_in_dim(parts, core, 1, keepdims=False)
        other = lax.dynamic_index_in_dim(parts, 1 - core, 1, keepdims=False)
        parts = add_low(own, swap(other, "core"))
        return line_scatter(parts, "x")

    attended = hidden + scatter_tensor(
        jnp.dot(mixed, out_weight, preferred_element_type=WIDE).astype(LOW)
    ).astype(WIDE)
    moe_normed, inverse_moe = normalize(attended, moe_gain)
    routed_low = moe_normed.astype(LOW)
    routed_all = lax.all_gather(routed_low, ALL, axis=0, tiled=True)
    logits = jnp.dot(routed_low, router_weight, preferred_element_type=WIDE)
    shifted = jnp.exp(logits - jnp.max(logits, axis=-1, keepdims=True))
    probs = shifted / jnp.sum(shifted, axis=-1, keepdims=True)
    probs_all = lax.all_gather(probs, ALL, axis=0, tiled=True)

    grad_slots = dispatch(order, select, cotangent_all, local_experts)
    grad_units = grad_active(grad_slots, expert_down)
    own_probs = lax.dynamic_slice_in_dim(
        probs_all.reshape(blocks, tok_rows, all_experts)[order],
        expert_index * local_experts,
        local_experts,
        axis=2,
    )
    slot_gates = jnp.sum(
        jnp.where(chosen, jnp.swapaxes(own_probs, 1, 2)[:, :, None, :], 0.0), axis=-1
    )
    slot_gates = jnp.swapaxes(slot_gates, 0, 1).reshape(local_experts, blocks * capacity, 1)
    row_slots = dispatch(order, select, routed_all, local_experts)
    gated_act, grad_pair, gate_grads = hidden_units(row_slots, expert_up, grad_units, slot_gates)

    gate_grads = jnp.swapaxes(gate_grads.reshape(local_experts, blocks, capacity), 0, 1)
    own_grads = jnp.sum(jnp.where(chosen, gate_grads[:, :, :, None], 0.0), axis=2)
    placed = lax.dynamic_update_slice_in_dim(
        jnp.zeros((blocks, tok_rows, all_experts), WIDE),
        jnp.swapaxes(own_grads, 1, 2),
        expert_index * local_experts,
        axis=2,
    ).reshape(ncore, nx, ny, nz, tok_rows, all_experts)
    grad_probs = scatter_all(placed[0], placed[1], ("x", "y", "z"))

    sizes = (nx, ny, nz)
    chunk = 512

    def sums(lhs, weight, transposed):
        pieces = []
        for first in range(0, width, chunk):
            flip = first // chunk % 2 == 1
            keep, send = combine(lhs, weight, select_back, first, chunk, transposed, sizes, flip)
            pieces.append(scatter_all(keep, send, ("y", "x", "z") if flip else ("x", "y", "z")))
        return jnp.concatenate(pieces, axis=-1).astype(WIDE)

    rows_back = sums(grad_pair, expert_up, True)
    outputs = sums(gated_act[:, None], expert_down[:, None], False)
    output = attended + outputs

    chose = jnp.any(routes[:, :, None] == jnp.arange(all_experts, dtype=jnp.int32), axis=1)
    grad_probs = jnp.where(chose, grad_probs, 0.0)
    grad_logits = probs * (grad_probs - jnp.sum(probs * grad_probs, axis=-1, keepdims=True))
    logits_low = grad_logits.astype(LOW)
    router_grad = jnp.einsum("td,te->de", routed_low, logits_low, preferred_element_type=WIDE)
    grad_moe = jnp.einsum("te,de->td", logits_low, router_weight, preferred_element_type=WIDE)
    grad_moe = grad_moe + rows_back
    grad_attended, moe_gain_grad = norm_back(grad_moe, attended, inverse_moe, moe_gain)
    grad_attended = grad_attended + cotangent
    piece = lax.all_gather(grad_attended.astype(LOW), TENSOR, axis=0, tiled=True)

    up_grad = weight_grad(row_slots[:, None], grad_pair, 512, expert_up.shape[-1])
    down_grad = weight_grad(gated_act[:, None], grad_slots[:, None], expert_up.shape[-1], 512)
    down_grad = down_grad.reshape(expert_down.shape)

    out_acc = jnp.einsum("tf,td->fd", mixed, piece, preferred_element_type=WIDE).astype(LOW)
    out_grad = sum_expert(out_acc)
    grad_mixed = jnp.einsum("td,fd->tf", piece, out_weight, preferred_element_type=WIDE).astype(LOW)
    grad_heads = grad_mixed.reshape(head_shape)
    recomputed = masked_scores()
    weights_wide = jnp.exp(recomputed - total)
    grad_weights = jnp.einsum("qhd,khd->hqk", grad_heads, values_low, preferred_element_type=WIDE)
    grad_scores = (
        weights_wide * (grad_weights - jnp.sum(grad_weights * weights_wide, axis=-1, keepdims=True))
    ).astype(LOW)
    grad_values = jnp.einsum("hqk,qhd->khd", weights_low, grad_heads, preferred_element_type=WIDE)
    grad_queries = jnp.einsum("hqk,khd->qhd", grad_scores, keys_low, preferred_element_type=WIDE)
    grad_keys = jnp.einsum("hqk,qhd->khd", grad_scores, queries, preferred_element_type=WIDE)
    grad_query_pre, query_gain_grad = norm_back(
        rotate(grad_queries * scale, cosine, -sine), query_pre, query_inverse, gains[0]
    )
    grad_key_pre, key_gain_grad = norm_back(
        rotate(grad_keys * scale, cosine, -sine), key_pre, key_inverse, gains[1]
    )
    grad_proj = [
        grad.reshape(length, head_width).astype(LOW)
        for grad in (grad_query_pre, grad_key_pre, grad_values)
    ]
    qk_gain_grad = jnp.stack([query_gain_grad.reshape(-1), key_gain_grad.reshape(-1)])
    grad_normed = sum(
        jnp.einsum("tf,df->td", grad, weight, preferred_element_type=WIDE)
        for grad, weight in zip(grad_proj, qkv_weight)
    ).astype(LOW)
    grad_normed = scatter_tensor(grad_normed).astype(WIDE)
    qkv_grad = jnp.stack(
        [
            sum_expert(
                jnp.einsum("td,tf->df", normed_all, grad, preferred_element_type=WIDE).astype(LOW)
            )
            for grad in grad_proj
        ]
    )
    grad_hidden, attn_gain_grad = norm_back(grad_normed, hidden, inverse_attn, attn_gain)
    grad_hidden = grad_hidden + grad_attended
    qk_gain_grad = lax.psum(qk_gain_grad, EXPERT)
    router_grad = lax.psum(router_grad, ALL)
    attn_gain_grad, moe_gain_grad = sum_all(jnp.stack([attn_gain_grad, moe_gain_grad]))
    return (
        output,
        grad_hidden,
        attn_gain_grad,
        qkv_grad,
        qk_gain_grad,
        out_grad,
        moe_gain_grad,
        router_grad,
        up_grad,
        down_grad,
    )


def solution(mesh):
    expert, tensor = (mesh.shape[name] for name in ("expert", "tensor"))
    grid = Mesh(mesh.devices.reshape(4, expert // 4, tensor // 2, 2), ALL)
    return jax.shard_map(
        shards,
        mesh=grid,
        in_specs=(
            P(ALL, None),
            P(EXPERT),
            P(ALL, None),
            P(),
            P(None, None, TENSOR),
            P(None, TENSOR),
            P(TENSOR, None),
            P(),
            P(),
            P(EXPERT, None, None, TENSOR),
            P(EXPERT, TENSOR, None),
            P(ALL, None),
        ),
        out_specs=(
            P(ALL, None),
            P(ALL, None),
            P(),
            P(None, None, TENSOR),
            P(None, TENSOR),
            P(TENSOR, None),
            P(),
            P(),
            P(EXPERT, None, None, TENSOR),
            P(EXPERT, TENSOR, None),
        ),
        check_vma=False,
    )
```

time: 2990 us -> 2010 us (0.67)
  waiting for transfers between devices: 1570 us -> 665 us
  blocking collectives: 620 us -> 76.3 us
  Pallas kernels: 0 us -> 447 us
  starting transfers between devices: 12.5 us -> 372 us
  matrix products: 372 us -> 100 us
  local copies, waits for them, and re-layouts: 264 us -> 134 us
  other arithmetic: 125 us -> 177 us
    reduce_scatter x4 -> x0, waiting for transfers between devices: 636 us -> none  [the longest x1 329 us: shards(): lax.psum_scatter(jnp.einsum('recf,ecdf->red', grad_pair, expert_up, prefe...]
    all_to_all x2 -> x0, blocking collectives: 557 us -> none  [the longest x1 280 us: shards(): lax.all_to_all(send, 'expert', split_axis=0, concat_axis=1, tiled=True)]
    pallas_call x0 -> x14, Pallas kernels: none -> 447 us  [the longest x8 155 us: combine(): pl.pallas_call(functools.partial(combine_kernel, transposed, experts), gr...]
    ppermute x0 -> x148, starting transfers between devices: none -> 372 us  [the longest x41 188 us: line_scatter(): up = lax.ppermute(block, axis, [(i, i + 1) for i in range(step)])]
    ppermute x0 -> x148, waiting for transfers between devices: none -> 354 us  [the longest x37 190 us: swap(): return lax.ppermute(values, axis, [(0, 1), (1, 0)])]
    dot_general x16 -> x14, matrix products: 326 us -> 55.5 us  [the longest x3 24.4 us: shards(): jnp.einsum('tf,df->td', grad, weight, preferred_element_type=WIDE)]
    psum x2 -> x1, waiting for transfers between devices: 247 us -> 0.01 us  [shards(): router_grad = lax.psum(router_grad, ALL)]
    all_to_all x2 -> x0, waiting for transfers between devices: 226 us -> none  [the longest x1 226 us: shards(): lax.all_to_all(row_sum.reshape(n_expert, capacity, local_experts, width),...]
  transfers between devices with their start and end apart: 13 -> 154, of which waited for: 10 -> 54; matrix products, arithmetic and copies ran while one was open for 18% -> 14% of each run, Pallas kernels for 0% -> 18%
where the time goes in v1:
time: 2010 us; the launch traced here: 1990 us
  waiting for transfers between devices  665 us (33%)
  Pallas kernels  447 us (22%)
  starting transfers between devices  372 us (19%)
  other arithmetic  177 us (9%)
  local copies, waits for them, and re-layouts  134 us (7%)
  matrix products  100 us (5%)
  blocking collectives  76.3 us (4%)
    ppermute x37, waiting for transfers between devices, swap(): return lax.ppermute(values, axis, [(0, 1), (1, 0)])  190 us
    ppermute x41, starting transfers between devices, line_scatter(): up = lax.ppermute(block, axis, [(i, i + 1) for i in range(step)])  188 us
    all_gather x1, waiting for transfers between devices, shards(): lax.all_gather(cotangent.astype(LOW), ALL, axis=0, tiled=True)  167 us
    pallas_call x8, Pallas kernels, combine(): pl.pallas_call(functools.partial(combine_kernel, transposed, experts), gr...  155 us
    pallas_call x2, Pallas kernels, weight_grad(): pl.pallas_call(weight_grad_kernel, grid=(experts, left_width // tile_left...  127 us
    all_gather x1, waiting for transfers between devices, shards(): routed_all = lax.all_gather(routed_low, ALL, axis=0, tiled=True)  110 us
    pallas_call x2, Pallas kernels, dispatch(): pl.pallas_call(dispatch_kernel, grid_spec=pltpu.PrefetchScalarGridSpec(nu...  87.7 us
    convert_element_type x78, other arithmetic, add_low(): return total.astype(terms[0].dtype)  75.8 us
  transfers between devices with their start and end apart: 154, of which 54 were waited for; matrix products, arithmetic and copies ran while one was open for 14% of the time, Pallas kernels for 18%

profile of v1, /device:TPU:0, one launch (start us, length us, event | category | flops | bytes accessed | tf_op | source)
XLA Modules:
  0.0 1989.6 jit_solution(17841171593277574160)
XLA Ops:
  16.4 32.8 %all-gather.6.cloned.1.call-done = bf16[1024,2048]{1,0:T(8,128)(2,1)} async-done(((bf16[256,2048]{1,0:T(8,128)(2,1)}), bf16[1024,2048]{1,0:T(8,128)(2,1)}) %all-gather.6.cloned.1.call-update) | async-done | bytes 4194320 | tf_op jit(solution)/shard_map/all_gather | solution.py:429
  49.1 10.1 fusion.21
  94.0 7.4 convolution_convert_fusion.7
  121.4 20.9 %collective-permute-done.1 = bf16[256,2048]{1,0:T(8,128)(2,1)} collective-permute-done((bf16[256,2048]{1,0:T(8,128)(2,1)}, bf16[256,2048]{1,0:T(8,128)(2,1)}, u32[]{:S(2)}, u32[]{:S(2)}) %collective-permute-start.1) | collective-permute-done | bytes 1048608 | tf_op jit(solution)/shard_map/ppermute | solution.py:80
  158.3 40.5 %all_gather.19 = s32[8192,8]{0,1:T(8,128)S(1)} all-gather(s32[256,8]{0,1:T(8,128)S(1)} %copy-done.90), channel_id=1, replica_groups=mesh['z'=4,'y'=2,'x'=2,'core'=2] {'z','y','x','core'}, dimensions={0}, use_global_device_ids=true | all-gather | bytes 270336 | tf_op jit(solution)/shard_map/all_gather | solution.py:431
  210.5 13.0 copy.125
  239.7 167.1 %all-gather.10.cloned.1.call-done = bf16[8192,2048]{1,0:T(8,128)(2,1)} async-done(((bf16[256,2048]{1,0:T(8,128)(2,1)}), bf16[8192,2048]{1,0:T(8,128)(2,1)}) %all-gather.10.cloned.1.call-update) | async-done | bytes 33554448 | tf_op jit(solution)/shard_map/all_gather | solution.py:430
  409.6 44.0 %dispatch.3.rows_ref = bf16[8,1536,2048]{2,1,0:T(8,128)(2,1)} custom-call(s32[32]{0:T(128)S(1)} %add.797.order_ref, bf16[32,384,256]{2,1,0:T(8,128)(2,1)S(1)} %copy-done.1, bf16[32,256,2048]{2,1,0:T(8,128)(2,1)} %bitcast.712), custom_call_target="tpu_custom_call" | custom-call | flops 12884901888 | bytes 83886080 | tf_op jit(solution)/shard_map/dispatch/pallas_call | solution.py:192
  457.0 30.5 %grad_active.1.grad_ref = f32[8,1536,256]{2,1,0:T(8,128)S(1)} custom-call(bf16[8,1536,2048]{2,1,0:T(8,128)(2,1)} %dispatch.3.rows_ref, bf16[8,256,2048]{2,1,0:T(8,128)(2,1)S(1)} %copy-done.4), custom_call_target="tpu_custom_call" | custom-call | flops 12884901888 | bytes 50331648 | tf_op jit(solution)/shard_map/grad_active/pallas_call | solution.py:222
  492.3 110.2 %all-gather.8.cloned.1.call-done = bf16[8192,2048]{1,0:T(8,128)(2,1)} async-done(((bf16[256,2048]{1,0:T(8,128)(2,1)}), bf16[8192,2048]{1,0:T(8,128)(2,1)}) %all-gather.8.cloned.1.call-update) | async-done | bytes 33554448 | tf_op jit(solution)/shard_map/all_gather | solution.py:485
  605.3 43.6 %dispatch.2.rows_ref = bf16[8,1536,2048]{2,1,0:T(8,128)(2,1)} custom-call(s32[32]{0:T(128)S(1)} %add.797.order_ref, bf16[32,384,256]{2,1,0:T(8,128)(2,1)S(1)} %copy-done.2, bf16[32,256,2048]{2,1,0:T(8,128)(2,1)} %bitcast.713), custom_call_target="tpu_custom_call" | custom-call | flops 12884901888 | bytes 83886080 | tf_op jit(solution)/shard_map/dispatch/pallas_call | solution.py:192
  649.0 47.3 %hidden_units.1 = (bf16[8,1536,256]{2,1,0:T(8,128)(2,1)S(1)}, bf16[8,2,1536,256]{3,2,1,0:T(8,128)(2,1)}, f32[8,1536,1]{2,1,0:T(8,128)S(1)}) custom-call(bf16[8,1536,2048]{2,1,0:T(8,128)(2,1)} %dispatch.2.rows_ref, bf16[8,2,2048,256]{3,2,1,0:T(8,128)(2,1)} %weight_ref.7, f32[8,1536,256]{2,1,0:T(8,128)} %copy-done.3, f32[8,1536,1]{2,1,0:T(8,128)} %reshape.924.gate_ref), custom_call_target="tpu_custom_call" | custom-call | flops 25769803776 | bytes 50331648 | tf_op jit(solution)/shard_map/hidden_units/pallas_call | solution.py:257
  710.1 9.0 compare_convert_fusion.select_ref
  719.0 17.8 combine.8
  738.8 17.4 combine.9
  757.0 21.6 %combine.12 = (bf16[4,4,256,512]{3,2,1,0:T(8,128)(2,1)S(1)}, bf16[4,4,256,512]{3,2,1,0:T(8,128)(2,1)}) custom-call(bf16[8,2,1536,256]{3,2,1,0:T(8,128)(2,1)} %get-tuple-element.39.lhs_ref.right_ref, bf16[8,2,2048,256]{3,2,1,0:T(8,128)(2,1)} %weight_ref.7, bf16[32,256,384]{2,1,0:T(8,128)(2,1)} %compare_convert_fusion.select_ref), custom_call_target="tpu_custom_call" | custom-call | flops 9663676416 | bytes 27262976 | tf_op jit(solution)/shard_map/combine/pallas_call | solution.py:340
  780.2 21.0 %combine.13 = (bf16[4,4,256,512]{3,2,1,0:T(8,128)(2,1)S(1)}, bf16[4,4,256,512]{3,2,1,0:T(8,128)(2,1)}) custom-call(bf16[8,2,1536,256]{3,2,1,0:T(8,128)(2,1)} %get-tuple-element.39.lhs_ref.right_ref, bf16[8,2,2048,256]{3,2,1,0:T(8,128)(2,1)} %weight_ref.7, bf16[32,256,384]{2,1,0:T(8,128)(2,1)} %compare_convert_fusion.select_ref), custom_call_target="tpu_custom_call" | custom-call | flops 9663676416 | bytes 27262976 | tf_op jit(solution)/shard_map/combine/pallas_call | solution.py:340
  805.2 17.4 combine.10
  825.2 17.4 combine.11
  857.8 20.9 %combine.14 = (bf16[4,4,256,512]{3,2,1,0:T(8,128)(2,1)S(1)}, bf16[4,4,256,512]{3,2,1,0:T(8,128)(2,1)}) custom-call(bf16[8,2,1536,256]{3,2,1,0:T(8,128)(2,1)} %get-tuple-element.39.lhs_ref.right_ref, bf16[8,2,2048,256]{3,2,1,0:T(8,128)(2,1)} %weight_ref.7, bf16[32,256,384]{2,1,0:T(8,128)(2,1)} %compare_convert_fusion.select_ref), custom_call_target="tpu_custom_call" | custom-call | flops 9663676416 | bytes 27262976 | tf_op jit(solution)/shard_map/combine/pallas_call | solution.py:340
  880.8 7.3 collective-permute-start.48
  888.1 21.1 %combine.15 = (bf16[4,4,256,512]{3,2,1,0:T(8,128)(2,1)S(1)}, bf16[4,4,256,512]{3,2,1,0:T(8,128)(2,1)}) custom-call(bf16[8,2,1536,256]{3,2,1,0:T(8,128)(2,1)} %get-tuple-element.39.lhs_ref.right_ref, bf16[8,2,2048,256]{3,2,1,0:T(8,128)(2,1)} %weight_ref.7, bf16[32,256,384]{2,1,0:T(8,128)(2,1)} %compare_convert_fusion.select_ref), custom_call_target="tpu_custom_call" | custom-call | flops 9663676416 | bytes 27262976 | tf_op jit(solution)/shard_map/combine/pallas_call | solution.py:340
  996.8 29.7 %collective-permute-done.22 = bf16[2,4,256,512]{3,2,1,0:T(8,128)(2,1)} collective-permute-done((bf16[2,4,256,512]{3,2,1,0:T(8,128)(2,1)}, bf16[2,4,256,512]{3,2,1,0:T(8,128)(2,1)}, u32[]{:S(2)}, u32[]{:S(2)}) %collective-permute-start.22) | collective-permute-done | bytes 2097184 | tf_op jit(solution)/shard_map/ppermute | solution.py:65
  1039.0 32.4 %collective-permute-done.49 = bf16[2,4,256,512]{3,2,1,0:T(8,128)(2,1)} collective-permute-done((bf16[2,4,256,512]{3,2,1,0:T(8,128)(2,1)}, bf16[2,4,256,512]{3,2,1,0:T(8,128)(2,1)}, u32[]{:S(2)}, u32[]{:S(2)}) %collective-permute-start.49) | collective-permute-done | bytes 2097184 | tf_op jit(solution)/shard_map/ppermute | solution.py:65
  1081.3 35.0 %collective-permute-done.67 = bf16[2,4,256,512]{3,2,1,0:T(8,128)(2,1)S(1)} collective-permute-done((bf16[2,4,256,512]{3,2,1,0:T(8,128)(2,1)}, bf16[2,4,256,512]{3,2,1,0:T(8,128)(2,1)S(1)}, u32[]{:S(2)}, u32[]{:S(2)}) %collective-permute-start.67) | collective-permute-done | bytes 2097184 | tf_op jit(solution)/shard_map/ppermute | solution.py:65
  1128.0 18.6 collective-permute-done.5
  1152.7 16.3 collective-permute-done.23
  1174.6 16.9 collective-permute-done.50
  1196.2 16.9 collective-permute-done.68
  1292.9 7.9 collective-permute-start.28
  1300.9 7.0 collective-permute-start.37
  1325.4 20.2 %collective-permute-start.71 = (bf16[256,512]{1,0:T(8,128)(2,1)S(1)}, bf16[256,512]{1,0:T(8,128)(2,1)S(1)}, u32[]{:S(2)}, u32[]{:S(2)}) collective-permute-start(bf16[256,512]{1,0:T(8,128)(2,1)S(1)} %get-tuple-element.118), channel_id=1, source_target_pairs={{0,8},{8,16},{16,24},{1,9},{9,17},{17,25},{2,10},{10,18},{18,26},{... | collective-permute-start | bytes 786440 | tf_op jit(solution)/shard_map/ppermute | solution.py:80
  1347.0 8.3 collective-permute-start.80
  1394.8 41.5 %weight_grad.3 = f32[8,1,256,2048]{3,2,1,0:T(8,128)} custom-call(bf16[8,1,1536,256]{3,2,1,0:T(8,128)(2,1)} %bitcast.699, bf16[8,1,1536,2048]{3,2,1,0:T(8,128)(2,1)} %bitcast.708), custom_call_target="tpu_custom_call" | custom-call | flops 12884901888 | bytes 73400320 | tf_op jit(solution)/shard_map/weight_grad/pallas_call | solution.py:382
  1436.3 85.4 %weight_grad.2 = f32[8,2,2048,256]{3,2,1,0:T(8,128)} custom-call(bf16[8,1,1536,2048]{3,2,1,0:T(8,128)(2,1)} %bitcast.709, bf16[8,2,1536,256]{3,2,1,0:T(8,128)(2,1)} %get-tuple-element.39.lhs_ref.right_ref), custom_call_target="tpu_custom_call" | custom-call | flops 25769803776 | bytes 96468992 | tf_op jit(solution)/shard_map/weight_grad/pallas_call | solution.py:382
  1527.6 12.6 multiply_reduce_fusion
  1540.2 13.3 multiply_convert_fusion
  1559.5 9.6 convolution_convert_fusion.5
  1619.2 7.6 fusion.57
  1628.3 7.8 fusion.59
  1636.2 9.0 add_convert_fusion
  1650.7 35.9 %psum.14 = f32[2,512]{1,0:T(2,128)} all-reduce(f32[2,512]{1,0:T(2,128)S(1)} %pad_maximum_fusion.13), channel_id=1, replica_groups=mesh['z'=4,'y'=2,'x'=2,'core'=2] {'z','y'}, use_global_device_ids=true, to_apply=%region_24.25 | all-reduce | flops 1024 | bytes 8192 | tf_op jit(solution)/shard_map/psum | solution.py:585
  1743.2 14.8 collective-permute-start.109
  1791.9 19.5 collective-permute-start.127
  1814.3 10.8 collective-permute-done.145
  1833.2 8.1 collective-permute-done.146
  1841.3 11.3 collective-permute-start.117
  1893.9 59.1 %collective-permute-done.89 = f32[2,2048]{1,0:T(2,128)S(1)} collective-permute-done((f32[2,2048]{1,0:T(2,128)S(1)}, f32[2,2048]{1,0:T(2,128)S(1)}, u32[]{:S(2)}, u32[]{:S(2)}) %collective-permute-start.89) | collective-permute-done | bytes 16416 | tf_op jit(solution)/shard_map/ppermute | solution.py:139
  (775 shorter events, 677.4 us)
Async XLA Ops:
  7.2 41.9 %all-gather.6.cloned.1.call-start = ((), (), s32[]{:S(2)}) async-start(), calls=%async_computation | async-start | bytes 5242880 | tf_op jit(solution)/shard_map/all_gather | solution.py:429
  11.8 212.4 %all-gather.12.cloned.1.call-start = ((), (), s32[]{:S(2)}) async-start(), calls=%async_computation.3 | async-start | bytes 2162688 | tf_op jit(solution)/shard_map/all_gather | solution.py:489
  154.2 252.6 %all-gather.10.cloned.1.call-start = ((), (), s32[]{:S(2)}) async-start(), calls=%async_computation.2 | async-start | bytes 34603008 | tf_op jit(solution)/shard_map/all_gather | solution.py:430
  157.0 445.6 %all-gather.8.cloned.1.call-start = ((), (), s32[]{:S(2)}) async-start(), calls=%async_computation.1 | async-start | bytes 34603008 | tf_op jit(solution)/shard_map/all_gather | solution.py:485
  157.5 1365.3 %all-gather.14.cloned.1.call-start = ((), (), s32[]{:S(2)}) async-start(), calls=%async_computation.4 | async-start | bytes 5242880 | tf_op jit(solution)/shard_map/all_gather | solution.py:540
  736.8 172.5 %collective-permute-start.3 = (bf16[2,2,4,256,512]{4,3,2,1,0:T(8,128)(2,1)}, bf16[2,2,4,256,512]{4,3,2,1,0:T(8,128)(2,1)}, u32[]{:S(2)}, u32[]{:S(2)}) collective-permute-start(bf16[2,2,4,256,512]{4,3,2,1,0:T(8,128)(2,1)} %bitcast.775), channel_id=1, source_target_pairs={{0,1},{1,0},{2,3},{3,2},{4,5},{5,4},{6,7},{7,6},{8,9},{9,8},{10,11... | collective-permute-start | bytes 12582920 | tf_op jit(solution)/shard_map/ppermute | solution.py:65
  756.2 153.6 %collective-permute-start.12 = (bf16[2,2,4,256,512]{4,3,2,1,0:T(8,128)(2,1)}, bf16[2,2,4,256,512]{4,3,2,1,0:T(8,128)(2,1)}, u32[]{:S(2)}, u32[]{:S(2)}) collective-permute-start(bf16[2,2,4,256,512]{4,3,2,1,0:T(8,128)(2,1)} %bitcast.776), channel_id=1, source_target_pairs={{0,1},{1,0},{2,3},{3,2},{4,5},{5,4},{6,7},{7,6},{8,9},{9,8},{10,11... | collective-permute-start | bytes 12582920 | tf_op jit(solution)/shard_map/ppermute | solution.py:65
  824.5 96.8 %collective-permute-start.21 = (bf16[2,2,4,256,512]{4,3,2,1,0:T(8,128)(2,1)}, bf16[2,2,4,256,512]{4,3,2,1,0:T(8,128)(2,1)}, u32[]{:S(2)}, u32[]{:S(2)}) collective-permute-start(bf16[2,2,4,256,512]{4,3,2,1,0:T(8,128)(2,1)} %bitcast.779), channel_id=1, source_target_pairs={{0,1},{1,0},{2,3},{3,2},{4,5},{5,4},{6,7},{7,6},{8,9},{9,8},{10,11... | collective-permute-start | bytes 12582920 | tf_op jit(solution)/shard_map/ppermute | solution.py:65
  844.6 88.2 %collective-permute-start.30 = (bf16[2,2,4,256,512]{4,3,2,1,0:T(8,128)(2,1)}, bf16[2,2,4,256,512]{4,3,2,1,0:T(8,128)(2,1)}, u32[]{:S(2)}, u32[]{:S(2)}) collective-permute-start(bf16[2,2,4,256,512]{4,3,2,1,0:T(8,128)(2,1)} %bitcast.780), channel_id=1, source_target_pairs={{0,1},{1,0},{2,3},{3,2},{4,5},{5,4},{6,7},{7,6},{8,9},{9,8},{10,11... | collective-permute-start | bytes 12582920 | tf_op jit(solution)/shard_map/ppermute | solution.py:65
  880.8 59.8 %collective-permute-start.48 = (bf16[2,2,4,256,512]{4,3,2,1,0:T(8,128)(2,1)}, bf16[2,2,4,256,512]{4,3,2,1,0:T(8,128)(2,1)}, u32[]{:S(2)}, u32[]{:S(2)}) collective-permute-start(bf16[2,2,4,256,512]{4,3,2,1,0:T(8,128)(2,1)} %bitcast.773), channel_id=1, source_target_pairs={{0,1},{1,0},{2,3},{3,2},{4,5},{5,4},{6,7},{7,6},{8,9},{9,8},{10,11... | collective-permute-start | bytes 12582920 | tf_op jit(solution)/shard_map/ppermute | solution.py:65
  909.8 45.2 %collective-permute-start.66 = (bf16[2,2,4,256,512]{4,3,2,1,0:T(8,128)(2,1)}, bf16[2,2,4,256,512]{4,3,2,1,0:T(8,128)(2,1)}, u32[]{:S(2)}, u32[]{:S(2)}) collective-permute-start(bf16[2,2,4,256,512]{4,3,2,1,0:T(8,128)(2,1)} %bitcast.778), channel_id=1, source_target_pairs={{0,1},{1,0},{2,3},{3,2},{4,5},{5,4},{6,7},{7,6},{8,9},{9,8},{10,11... | collective-permute-start | bytes 12582920 | tf_op jit(solution)/shard_map/ppermute | solution.py:65
  921.3 43.8 %collective-permute-start.75 = (bf16[2,2,4,256,512]{4,3,2,1,0:T(8,128)(2,1)}, bf16[2,2,4,256,512]{4,3,2,1,0:T(8,128)(2,1)}, u32[]{:S(2)}, u32[]{:S(2)}) collective-permute-start(bf16[2,2,4,256,512]{4,3,2,1,0:T(8,128)(2,1)} %bitcast.777), channel_id=1, source_target_pairs={{0,1},{1,0},{2,3},{3,2},{4,5},{5,4},{6,7},{7,6},{8,9},{9,8},{10,11... | collective-permute-start | bytes 12582920 | tf_op jit(solution)/shard_map/ppermute | solution.py:65
  932.8 48.8 %collective-permute-start.4 = (bf16[2,4,256,512]{3,2,1,0:T(8,128)(2,1)}, bf16[2,4,256,512]{3,2,1,0:T(8,128)(2,1)}, u32[]{:S(2)}, u32[]{:S(2)}) collective-permute-start(bf16[2,4,256,512]{3,2,1,0:T(8,128)(2,1)} %slice_bitcast_fusion.14), channel_id=1, source_target_pairs={{0,2},{2,0},{1,3},{3,1},{4,6},{6,4},{5,7},{7,5},{8,10},{10,8},{9,1... | collective-permute-start | bytes 6291464 | tf_op jit(solution)/shard_map/ppermute | solution.py:65
  940.6 48.8 %collective-permute-start.13 = (bf16[2,4,256,512]{3,2,1,0:T(8,128)(2,1)}, bf16[2,4,256,512]{3,2,1,0:T(8,128)(2,1)}, u32[]{:S(2)}, u32[]{:S(2)}) collective-permute-start(bf16[2,4,256,512]{3,2,1,0:T(8,128)(2,1)} %slice_bitcast_fusion.12), channel_id=1, source_target_pairs={{0,4},{4,0},{1,5},{5,1},{2,6},{6,2},{3,7},{7,3},{8,12},{12,8},{9,1... | collective-permute-start | bytes 6291464 | tf_op jit(solution)/shard_map/ppermute | solution.py:65
  947.7 78.8 %collective-permute-start.22 = (bf16[2,4,256,512]{3,2,1,0:T(8,128)(2,1)}, bf16[2,4,256,512]{3,2,1,0:T(8,128)(2,1)}, u32[]{:S(2)}, u32[]{:S(2)}) collective-permute-start(bf16[2,4,256,512]{3,2,1,0:T(8,128)(2,1)} %slice_bitcast_fusion.10), channel_id=1, source_target_pairs={{0,2},{2,0},{1,3},{3,1},{4,6},{6,4},{5,7},{7,5},{8,10},{10,8},{9,1... | collective-permute-start | bytes 6291464 | tf_op jit(solution)/shard_map/ppermute | solution.py:65
  954.9 79.4 %collective-permute-start.31 = (bf16[2,4,256,512]{3,2,1,0:T(8,128)(2,1)}, bf16[2,4,256,512]{3,2,1,0:T(8,128)(2,1)}, u32[]{:S(2)}, u32[]{:S(2)}) collective-permute-start(bf16[2,4,256,512]{3,2,1,0:T(8,128)(2,1)} %slice_bitcast_fusion.8), channel_id=1, source_target_pairs={{0,4},{4,0},{1,5},{5,1},{2,6},{6,2},{3,7},{7,3},{8,12},{12,8},{9,1... | collective-permute-start | bytes 6291464 | tf_op jit(solution)/shard_map/ppermute | solution.py:65
  965.1 106.3 %collective-permute-start.49 = (bf16[2,4,256,512]{3,2,1,0:T(8,128)(2,1)}, bf16[2,4,256,512]{3,2,1,0:T(8,128)(2,1)}, u32[]{:S(2)}, u32[]{:S(2)}) collective-permute-start(bf16[2,4,256,512]{3,2,1,0:T(8,128)(2,1)} %slice_bitcast_fusion.6), channel_id=1, source_target_pairs={{0,2},{2,0},{1,3},{3,1},{4,6},{6,4},{5,7},{7,5},{8,10},{10,8},{9,1... | collective-permute-start | bytes 6291464 | tf_op jit(solution)/shard_map/ppermute | solution.py:65
  981.5 97.6 %collective-permute-start.58 = (bf16[2,4,256,512]{3,2,1,0:T(8,128)(2,1)}, bf16[2,4,256,512]{3,2,1,0:T(8,128)(2,1)S(1)}, u32[]{:S(2)}, u32[]{:S(2)}) collective-permute-start(bf16[2,4,256,512]{3,2,1,0:T(8,128)(2,1)} %slice_bitcast_fusion.4), channel_id=1, source_target_pairs={{0,4},{4,0},{1,5},{5,1},{2,6},{6,2},{3,7},{7,3},{8,12},{12,8},{9,1... | collective-permute-start | bytes 6291464 | tf_op jit(solution)/shard_map/ppermute | solution.py:65
  989.3 126.9 %collective-permute-start.67 = (bf16[2,4,256,512]{3,2,1,0:T(8,128)(2,1)}, bf16[2,4,256,512]{3,2,1,0:T(8,128)(2,1)S(1)}, u32[]{:S(2)}, u32[]{:S(2)}) collective-permute-start(bf16[2,4,256,512]{3,2,1,0:T(8,128)(2,1)} %slice_bitcast_fusion.2), channel_id=1, source_target_pairs={{0,2},{2,0},{1,3},{3,1},{4,6},{6,4},{5,7},{7,5},{8,10},{10,8},{9,1... | collective-permute-start | bytes 6291464 | tf_op jit(solution)/shard_map/ppermute | solution.py:65
  1026.5 97.7 %collective-permute-start.76 = (bf16[2,4,256,512]{3,2,1,0:T(8,128)(2,1)}, bf16[2,4,256,512]{3,2,1,0:T(8,128)(2,1)}, u32[]{:S(2)}, u32[]{:S(2)}) collective-permute-start(bf16[2,4,256,512]{3,2,1,0:T(8,128)(2,1)} %slice_bitcast_fusion), channel_id=1, source_target_pairs={{0,4},{4,0},{1,5},{5,1},{2,6},{6,2},{3,7},{7,3},{8,12},{12,8},{9,1... | collective-permute-start | bytes 6291464 | tf_op jit(solution)/shard_map/ppermute | solution.py:65
  1034.3 112.4 %collective-permute-start.5 = (bf16[4,256,512]{2,1,0:T(8,128)(2,1)}, bf16[4,256,512]{2,1,0:T(8,128)(2,1)}, u32[]{:S(2)}, u32[]{:S(2)}) collective-permute-start(bf16[4,256,512]{2,1,0:T(8,128)(2,1)} %slice_bitcast_fusion.30), channel_id=1, source_target_pairs={{0,4},{4,0},{1,5},{5,1},{2,6},{6,2},{3,7},{7,3},{8,12},{12,8},{9,1... | collective-permute-start | bytes 3145736 | tf_op jit(solution)/shard_map/ppermute | solution.py:65
  1071.4 78.2 %collective-permute-start.14 = (bf16[4,256,512]{2,1,0:T(8,128)(2,1)}, bf16[4,256,512]{2,1,0:T(8,128)(2,1)}, u32[]{:S(2)}, u32[]{:S(2)}) collective-permute-start(bf16[4,256,512]{2,1,0:T(8,128)(2,1)} %slice_bitcast_fusion.28), channel_id=1, source_target_pairs={{0,2},{2,0},{1,3},{3,1},{4,6},{6,4},{5,7},{7,5},{8,10},{10,8},{9,1... | collective-permute-start | bytes 3145736 | tf_op jit(solution)/shard_map/ppermute | solution.py:65
  1079.1 89.9 %collective-permute-start.23 = (bf16[4,256,512]{2,1,0:T(8,128)(2,1)}, bf16[4,256,512]{2,1,0:T(8,128)(2,1)S(1)}, u32[]{:S(2)}, u32[]{:S(2)}) collective-permute-start(bf16[4,256,512]{2,1,0:T(8,128)(2,1)} %slice_bitcast_fusion.26), channel_id=1, source_target_pairs={{0,4},{4,0},{1,5},{5,1},{2,6},{6,2},{3,7},{7,3},{8,12},{12,8},{9,1... | collective-permute-start | bytes 3145736 | tf_op jit(solution)/shard_map/ppermute | solution.py:65
  1116.3 54.5 %collective-permute-start.32 = (bf16[4,256,512]{2,1,0:T(8,128)(2,1)}, bf16[4,256,512]{2,1,0:T(8,128)(2,1)S(1)}, u32[]{:S(2)}, u32[]{:S(2)}) collective-permute-start(bf16[4,256,512]{2,1,0:T(8,128)(2,1)} %slice_bitcast_fusion.24), channel_id=1, source_target_pairs={{0,2},{2,0},{1,3},{3,1},{4,6},{6,4},{5,7},{7,5},{8,10},{10,8},{9,1... | collective-permute-start | bytes 3145736 | tf_op jit(solution)/shard_map/ppermute | solution.py:65
  1124.2 67.3 %collective-permute-start.50 = (bf16[4,256,512]{2,1,0:T(8,128)(2,1)}, bf16[4,256,512]{2,1,0:T(8,128)(2,1)S(1)}, u32[]{:S(2)}, u32[]{:S(2)}) collective-permute-start(bf16[4,256,512]{2,1,0:T(8,128)(2,1)} %slice_bitcast_fusion.22), channel_id=1, source_target_pairs={{0,4},{4,0},{1,5},{5,1},{2,6},{6,2},{3,7},{7,3},{8,12},{12,8},{9,1... | collective-permute-start | bytes 3145736 | tf_op jit(solution)/shard_map/ppermute | solution.py:65
  1146.6 45.9 %collective-permute-start.59 = (bf16[4,256,512]{2,1,0:T(8,128)(2,1)S(1)}, bf16[4,256,512]{2,1,0:T(8,128)(2,1)S(1)}, u32[]{:S(2)}, u32[]{:S(2)}) collective-permute-start(bf16[4,256,512]{2,1,0:T(8,128)(2,1)S(1)} %slice_bitcast_fusion.20), channel_id=1, source_target_pairs={{0,2},{2,0},{1,3},{3,1},{4,6},{6,4},{5,7},{7,5},{8,10},{10,8},{9,1... | collective-permute-start | bytes 3145736 | tf_op jit(solution)/shard_map/ppermute | solution.py:65
  1149.6 63.5 %collective-permute-start.68 = (bf16[4,256,512]{2,1,0:T(8,128)(2,1)S(1)}, bf16[4,256,512]{2,1,0:T(8,128)(2,1)S(1)}, u32[]{:S(2)}, u32[]{:S(2)}) collective-permute-start(bf16[4,256,512]{2,1,0:T(8,128)(2,1)S(1)} %slice_bitcast_fusion.18), channel_id=1, source_target_pairs={{0,4},{4,0},{1,5},{5,1},{2,6},{6,2},{3,7},{7,3},{8,12},{12,8},{9,1... | collective-permute-start | bytes 3145736 | tf_op jit(solution)/shard_map/ppermute | solution.py:65
  1169.0 45.1 %collective-permute-start.77 = (bf16[4,256,512]{2,1,0:T(8,128)(2,1)S(1)}, bf16[4,256,512]{2,1,0:T(8,128)(2,1)S(1)}, u32[]{:S(2)}, u32[]{:S(2)}) collective-permute-start(bf16[4,256,512]{2,1,0:T(8,128)(2,1)S(1)} %slice_bitcast_fusion.16), channel_id=1, source_target_pairs={{0,2},{2,0},{1,3},{3,1},{4,6},{6,4},{5,7},{7,5},{8,10},{10,8},{9,1... | collective-permute-start | bytes 3145736 | tf_op jit(solution)/shard_map/ppermute | solution.py:65
  1170.8 47.4 %collective-permute-start.6 = (bf16[256,512]{1,0:T(8,128)(2,1)S(1)}, bf16[256,512]{1,0:T(8,128)(2,1)S(1)}, u32[]{:S(2)}, u32[]{:S(2)}) collective-permute-start(bf16[256,512]{1,0:T(8,128)(2,1)S(1)} %get-tuple-element.128), channel_id=1, source_target_pairs={{0,8},{1,9},{2,10},{3,11},{4,12},{5,13},{6,14},{7,15}} | collective-permute-start | bytes 786440 | tf_op jit(solution)/shard_map/ppermute | solution.py:80
  1191.5 65.5 %collective-permute-start.9 = (bf16[256,512]{1,0:T(8,128)(2,1)S(1)}, bf16[256,512]{1,0:T(8,128)(2,1)S(1)}, u32[]{:S(2)}, u32[]{:S(2)}) collective-permute-start(bf16[256,512]{1,0:T(8,128)(2,1)S(1)} %get-tuple-element.129), channel_id=1, source_target_pairs={{24,16},{25,17},{26,18},{27,19},{28,20},{29,21},{30,22},{31,23}} | collective-permute-start | bytes 786440 | tf_op jit(solution)/shard_map/ppermute | solution.py:83
  1213.1 49.8 %collective-permute-start.18 = (bf16[256,512]{1,0:T(8,128)(2,1)S(1)}, bf16[256,512]{1,0:T(8,128)(2,1)S(1)}, u32[]{:S(2)}, u32[]{:S(2)}) collective-permute-start(bf16[256,512]{1,0:T(8,128)(2,1)S(1)} %get-tuple-element.133), channel_id=1, source_target_pairs={{24,16},{25,17},{26,18},{27,19},{28,20},{29,21},{30,22},{31,23}} | collective-permute-start | bytes 786440 | tf_op jit(solution)/shard_map/ppermute | solution.py:83
  1218.2 50.1 %collective-permute-start.27 = (bf16[256,512]{1,0:T(8,128)(2,1)S(1)}, bf16[256,512]{1,0:T(8,128)(2,1)S(1)}, u32[]{:S(2)}, u32[]{:S(2)}) collective-permute-start(bf16[256,512]{1,0:T(8,128)(2,1)S(1)} %get-tuple-element.137), channel_id=1, source_target_pairs={{24,16},{25,17},{26,18},{27,19},{28,20},{29,21},{30,22},{31,23}} | collective-permute-start | bytes 786440 | tf_op jit(solution)/shard_map/ppermute | solution.py:83
  1288.0 81.5 %collective-permute-start.8 = (bf16[256,512]{1,0:T(8,128)(2,1)S(1)}, bf16[256,512]{1,0:T(8,128)(2,1)S(1)}, u32[]{:S(2)}, u32[]{:S(2)}) collective-permute-start(bf16[256,512]{1,0:T(8,128)(2,1)S(1)} %get-tuple-element.126), channel_id=1, source_target_pairs={{0,8},{8,16},{16,24},{1,9},{9,17},{17,25},{2,10},{10,18},{18,26},{... | collective-permute-start | bytes 786440 | tf_op jit(solution)/shard_map/ppermute | solution.py:80
  1394.7 585.7 %all-reduce.2.cloned.1.call-start = ((), (), s32[]{:S(2)}) async-start(), calls=%async_computation.5 | async-start | bytes 1048576 | tf_op jit(solution)/shard_map/psum | solution.py:586
  1574.8 111.8 %collective-permute-start.134 = (bf16[4,64,2048]{2,1,0:T(8,128)(2,1)}, bf16[4,64,2048]{2,1,0:T(8,128)(2,1)}, u32[]{:S(2)}, u32[]{:S(2)}) collective-permute-start(bf16[4,64,2048]{2,1,0:T(8,128)(2,1)} %dynamic-slice_bitcast_fusion.2), channel_id=1, source_target_pairs={{0,4},{4,0},{1,5},{5,1},{2,6},{6,2},{3,7},{7,3},{8,12},{12,8},{9,1... | collective-permute-start | bytes 3145736 | tf_op jit(solution)/shard_map/ppermute | solution.py:65
  1605.4 84.9 %collective-permute-start.92 = (bf16[4,256,512]{2,1,0:T(8,128)(2,1)}, bf16[4,256,512]{2,1,0:T(8,128)(2,1)}, u32[]{:S(2)}, u32[]{:S(2)}) collective-permute-start(bf16[4,256,512]{2,1,0:T(8,128)(2,1)} %dynamic-slice_bitcast_fusion.5), channel_id=1, source_target_pairs={{0,4},{4,0},{1,5},{5,1},{2,6},{6,2},{3,7},{7,3},{8,12},{12,8},{9,1... | collective-permute-start | bytes 3145736 | tf_op jit(solution)/shard_map/ppermute | solution.py:65
  1609.8 83.0 %collective-permute-start.106 = (bf16[4,256,512]{2,1,0:T(8,128)(2,1)}, bf16[4,256,512]{2,1,0:T(8,128)(2,1)}, u32[]{:S(2)}, u32[]{:S(2)}) collective-permute-start(bf16[4,256,512]{2,1,0:T(8,128)(2,1)} %dynamic-slice_bitcast_fusion.4), channel_id=1, source_target_pairs={{0,4},{4,0},{1,5},{5,1},{2,6},{6,2},{3,7},{7,3},{8,12},{12,8},{9,1... | collective-permute-start | bytes 3145736 | tf_op jit(solution)/shard_map/ppermute | solution.py:65
  1616.0 79.8 %collective-permute-start.120 = (bf16[4,256,512]{2,1,0:T(8,128)(2,1)}, bf16[4,256,512]{2,1,0:T(8,128)(2,1)}, u32[]{:S(2)}, u32[]{:S(2)}) collective-permute-start(bf16[4,256,512]{2,1,0:T(8,128)(2,1)} %dynamic-slice_bitcast_fusion.3), channel_id=1, source_target_pairs={{0,4},{4,0},{1,5},{5,1},{2,6},{6,2},{3,7},{7,3},{8,12},{12,8},{9,1... | collective-permute-start | bytes 3145736 | tf_op jit(solution)/shard_map/ppermute | solution.py:65
  1647.8 133.2 %collective-permute-start.84 = (bf16[2,256,2048]{2,1,0:T(8,128)(2,1)}, bf16[2,256,2048]{2,1,0:T(8,128)(2,1)}, u32[]{:S(2)}, u32[]{:S(2)}) collective-permute-start(bf16[2,256,2048]{2,1,0:T(8,128)(2,1)} %dynamic-slice_bitcast_fusion), channel_id=1, source_target_pairs={{0,1},{1,0},{2,3},{3,2},{4,5},{5,4},{6,7},{7,6},{8,9},{9,8},{10,11... | collective-permute-start | bytes 6291464 | tf_op jit(solution)/shard_map/ppermute | solution.py:65
  1779.6 48.9 %collective-permute-start.102 = (bf16[256,512]{1,0:T(8,128)(2,1)S(1)}, bf16[256,512]{1,0:T(8,128)(2,1)S(1)}, u32[]{:S(2)}, u32[]{:S(2)}) collective-permute-start(bf16[256,512]{1,0:T(8,128)(2,1)S(1)} %fusion.89), channel_id=1, source_target_pairs={{8,0},{16,8},{24,16},{9,1},{17,9},{25,17},{10,2},{18,10},{26,18},{... | collective-permute-start | bytes 786440 | tf_op jit(solution)/shard_map/ppermute | solution.py:94
  1789.8 42.0 %collective-permute-start.116 = (bf16[256,512]{1,0:T(8,128)(2,1)S(1)}, bf16[256,512]{1,0:T(8,128)(2,1)S(1)}, u32[]{:S(2)}, u32[]{:S(2)}) collective-permute-start(bf16[256,512]{1,0:T(8,128)(2,1)S(1)} %fusion.83), channel_id=1, source_target_pairs={{8,0},{16,8},{24,16},{9,1},{17,9},{25,17},{10,2},{18,10},{26,18},{... | collective-permute-start | bytes 786440 | tf_op jit(solution)/shard_map/ppermute | solution.py:94
  1791.9 60.7 %collective-permute-start.127 = (bf16[256,512]{1,0:T(8,128)(2,1)S(1)}, bf16[256,512]{1,0:T(8,128)(2,1)S(1)}, u32[]{:S(2)}, u32[]{:S(2)}) collective-permute-start(bf16[256,512]{1,0:T(8,128)(2,1)S(1)} %fusion.77), channel_id=1, source_target_pairs={{0,8},{8,16},{16,24},{1,9},{9,17},{17,25},{2,10},{10,18},{18,26},{... | collective-permute-start | bytes 786440 | tf_op jit(solution)/shard_map/ppermute | solution.py:93
  1828.5 55.7 %collective-permute-start.85 = (bf16[256,2048]{1,0:T(8,128)(2,1)S(1)}, bf16[256,2048]{1,0:T(8,128)(2,1)S(1)}, u32[]{:S(2)}, u32[]{:S(2)}) collective-permute-start(bf16[256,2048]{1,0:T(8,128)(2,1)S(1)} %get-tuple-element.85), channel_id=1, source_target_pairs={{0,2},{1,3},{4,6},{5,7},{8,10},{9,11},{12,14},{13,15},{16,18},{17,... | collective-permute-start | bytes 3145736 | tf_op jit(solution)/shard_map/ppermute | solution.py:80
  1876.0 95.1 %collective-permute-start.147 = (bf16[4,64,2048]{2,1,0:T(8,128)(2,1)S(1)}, bf16[4,64,2048]{2,1,0:T(8,128)(2,1)S(1)}, u32[]{:S(2)}, u32[]{:S(2)}) collective-permute-start(bf16[4,64,2048]{2,1,0:T(8,128)(2,1)S(1)} %constant_dynamic-slice_fusion), channel_id=1, source_target_pairs={{0,4},{4,0},{1,5},{5,1},{2,6},{6,2},{3,7},{7,3},{8,12},{12,8},{9,1... | collective-permute-start | bytes 3145736 | tf_op jit(solution)/shard_map/ppermute | solution.py:65
  1882.0 88.8 %collective-permute-start.105 = (bf16[4,256,512]{2,1,0:T(8,128)(2,1)S(1)}, bf16[4,256,512]{2,1,0:T(8,128)(2,1)S(1)}, u32[]{:S(2)}, u32[]{:S(2)}) collective-permute-start(bf16[4,256,512]{2,1,0:T(8,128)(2,1)S(1)} %constant_dynamic-slice_fusion.3), channel_id=1, source_target_pairs={{0,4},{4,0},{1,5},{5,1},{2,6},{6,2},{3,7},{7,3},{8,12},{12,8},{9,1... | collective-permute-start | bytes 3145736 | tf_op jit(solution)/shard_map/ppermute | solution.py:65
  1884.2 87.1 %collective-permute-start.119 = (bf16[4,256,512]{2,1,0:T(8,128)(2,1)S(1)}, bf16[4,256,512]{2,1,0:T(8,128)(2,1)S(1)}, u32[]{:S(2)}, u32[]{:S(2)}) collective-permute-start(bf16[4,256,512]{2,1,0:T(8,128)(2,1)S(1)} %constant_dynamic-slice_fusion.2), channel_id=1, source_target_pairs={{0,4},{4,0},{1,5},{5,1},{2,6},{6,2},{3,7},{7,3},{8,12},{12,8},{9,1... | collective-permute-start | bytes 3145736 | tf_op jit(solution)/shard_map/ppermute | solution.py:65
  1891.7 61.4 %collective-permute-start.89 = (f32[2,2048]{1,0:T(2,128)S(1)}, f32[2,2048]{1,0:T(2,128)S(1)}, u32[]{:S(2)}, u32[]{:S(2)}) collective-permute-start(f32[2,2048]{1,0:T(2,128)S(1)} %fusion.194), channel_id=1, source_target_pairs={{0,4},{4,0},{1,5},{5,1},{2,6},{6,2},{3,7},{7,3},{8,12},{12,8},{9,1... | collective-permute-start | bytes 49160 | tf_op jit(solution)/shard_map/ppermute | solution.py:139
  1892.6 82.5 %collective-permute-start.133 = (bf16[4,256,512]{2,1,0:T(8,128)(2,1)S(1)}, bf16[4,256,512]{2,1,0:T(8,128)(2,1)S(1)}, u32[]{:S(2)}, u32[]{:S(2)}) collective-permute-start(bf16[4,256,512]{2,1,0:T(8,128)(2,1)S(1)} %constant_dynamic-slice_fusion.1), channel_id=1, source_target_pairs={{0,4},{4,0},{1,5},{5,1},{2,6},{6,2},{3,7},{7,3},{8,12},{12,8},{9,1... | collective-permute-start | bytes 3145736 | tf_op jit(solution)/shard_map/ppermute | solution.py:65
  (210 other events, 2903.3 us)
Sparse Core Ops, SparseCore 0:
  11.9 37.1 all-gather.5
  154.3 55.2 all-gather.11
  212.5 194.2 all-gather.9
  409.5 192.9 all-gather.7
  1394.9 33.5 all-gather.13
  1523.0 127.4 all-reduce.1

commit v2 on v1

v2 whole, which is shorter than its diff:
```python
import functools
import math

import jax
import jax.numpy as jnp
from jax import lax
from jax.experimental import pallas as pl
from jax.experimental.pallas import tpu as pltpu
from jax.sharding import Mesh, PartitionSpec as P

HEAD_DIM = 128
LOW = jnp.bfloat16
WIDE = jnp.float32


EPSILON = 1e-05
THETA = 10000.0


def normalize(values, gain):
    inverse = lax.rsqrt(jnp.mean(values * values, axis=-1, keepdims=True) + EPSILON)
    return (values * inverse * gain, inverse)


def norm_back(grad_out, values, inverse, gain):
    scaled = values * inverse
    weighted = grad_out * gain
    grad_in = inverse * (weighted - scaled * jnp.mean(weighted * scaled, axis=-1, keepdims=True))
    return (grad_in, jnp.sum(grad_out * scaled, axis=0))


def doc_starts(segment_ids):
    index = jnp.arange(segment_ids.shape[0], dtype=jnp.int32)
    starts = jnp.concatenate([jnp.ones((1,), jnp.bool_), segment_ids[1:] != segment_ids[:-1]])
    return lax.cummax(jnp.where(starts, index, 0), axis=0)


def rope_tables(positions, half):
    freq = jnp.exp(-math.log(THETA) * jnp.arange(half, dtype=jnp.float32) / half)
    angle = positions.astype(jnp.float32)[:, None] * freq[None, :]
    cosine, sine = jnp.cos(angle), jnp.sin(angle)
    return (
        jnp.concatenate([cosine, cosine], axis=-1),
        jnp.concatenate([-sine, sine], axis=-1),
    )


def add_low(*terms):
    total = terms[0].astype(WIDE)
    for term in terms[1:]:
        total = total + term.astype(WIDE)
    return total.astype(terms[0].dtype)


def tie(values, *before):
    return lax.optimization_barrier((values,) + before)[0]


class Grid:
    def __init__(self, expert, tensor):
        y_bits, x_bits = (expert // 4).bit_length() - 1, (tensor // 2).bit_length() - 1
        self.z = ("z1", "z0")
        self.y = tuple(f"y{i}" for i in reversed(range(y_bits)))
        self.x = tuple(f"x{i}" for i in reversed(range(x_bits)))
        self.core = ("core",)
        self.expert = self.z + self.y
        self.tensor = self.x + self.core
        self.all = self.expert + self.tensor


def swap(values, axis):
    return lax.ppermute(values, axis, [(0, 1), (1, 0)])


def pick(parts, index):
    return lax.dynamic_index_in_dim(parts, index, 0, keepdims=False)


def index_of(axes):
    index = jnp.int32(0)
    for axis in axes:
        index = index * 2 + lax.axis_index(axis)
    return index


def block_order(grid, axes):
    order = jnp.zeros((1,), jnp.int32)
    for axis in axes:
        stride = 1 << (len(grid.all) - 1 - grid.all.index(axis))
        own = lax.axis_index(axis)
        order = (order[:, None] + jnp.stack([own, 1 - own])[None, :] * stride).reshape(-1)
    return order


def halves(total):
    return total.reshape((2, total.shape[0] // 2) + total.shape[1:])


def scatter(total, axes):
    for axis in axes:
        parts = halves(total)
        total = add_low(parts[0], swap(parts[1], axis))
    return total


def scatter_rows(total, axes):
    for axis in axes:
        me = lax.axis_index(axis)
        parts = halves(total)
        total = add_low(pick(parts, me), swap(pick(parts, 1 - me), axis))
    return total


def gather_rows(values, axes):
    for axis in reversed(axes):
        me = lax.axis_index(axis)
        other = swap(values, axis)
        values = jnp.concatenate(
            [jnp.where(me == 0, values, other), jnp.where(me == 0, other, values)]
        )
    return values


def gather_relative(values, axes):
    for axis in axes:
        values = jnp.concatenate([values, swap(values, axis)])
    return values


def gather_tensor(values, grid):
    rows, width = values.shape
    pieces = gather_rows(gather_rows(values, grid.x), grid.core)
    return jnp.swapaxes(pieces.reshape(2, -1, rows, width), 0, 1).reshape(-1, width)


def scatter_tensor(partial, grid):
    rows, width = partial.shape
    parts = jnp.swapaxes(partial.reshape(1 << len(grid.x), 2, -1, width), 0, 1)
    return scatter_rows(parts.reshape(rows, width), grid.core + grid.x)


def sum_over(values, axes):
    for axis in axes:
        values = values + swap(values, axis)
    return values


def sum_expert(values, grid):
    axes = grid.y + grid.z[::-1]
    return gather_rows(scatter_rows(values, axes), axes).astype(WIDE)


NT = (((1,), (1,)), ((), ()))
TN = (((0,), (0,)), ((), ()))


def dot(left, right, dims=None):
    if dims is None:
        return jnp.dot(left, right, preferred_element_type=WIDE)
    return lax.dot_general(left, right, dims, preferred_element_type=WIDE)


def params(megabytes):
    return pltpu.CompilerParams(vmem_limit_bytes=megabytes << 20)


def cost(flops, moved):
    return pl.CostEstimate(flops=int(2 * flops), bytes_accessed=int(2 * moved), transcendentals=0)


def dispatch_kernel(order_ref, select_ref, rows_ref, out_ref):
    experts, capacity, width = out_ref.shape
    picked = dot(select_ref[0], rows_ref[0])
    out_ref[...] = picked.astype(LOW).reshape(experts, capacity, width)


def dispatch(order, select, rows, experts):
    blocks, slots, tokens = select.shape
    width = rows.shape[-1]
    capacity = slots // experts
    return pl.pallas_call(
        dispatch_kernel,
        grid_spec=pltpu.PrefetchScalarGridSpec(
            num_scalar_prefetch=1,
            grid=(blocks,),
            in_specs=[
                pl.BlockSpec((1, slots, tokens), lambda b, order: (b, 0, 0)),
                pl.BlockSpec((1, tokens, width), lambda b, order: (order[b], 0, 0)),
            ],
            out_specs=pl.BlockSpec((experts, capacity, width), lambda b, order: (0, b, 0)),
        ),
        out_shape=jax.ShapeDtypeStruct((experts, blocks * capacity, width), LOW),
        compiler_params=params(32),
        cost_estimate=cost(2 * blocks * slots * tokens * width, 2 * blocks * (slots + tokens) * width),
        name="dispatch",
    )(order, select, rows.reshape(blocks, tokens, width))


def row_tile(rows):
    return max(t for t in range(128, 513, 128) if rows % t == 0)


def grad_active_kernel(rows_ref, down_ref, out_ref):
    out_ref[0] = dot(rows_ref[0], down_ref[0], NT)


def grad_active(rows, expert_down):
    experts, count, width = rows.shape
    units = expert_down.shape[1]
    tile = row_tile(count)
    return pl.pallas_call(
        grad_active_kernel,
        grid=(experts, count // tile),
        in_specs=[
            pl.BlockSpec((1, tile, width), lambda e, r: (e, r, 0)),
            pl.BlockSpec((1, units, width), lambda e, r: (e, 0, 0)),
        ],
        out_specs=pl.BlockSpec((1, tile, units), lambda e, r: (e, r, 0)),
        out_shape=jax.ShapeDtypeStruct((experts, count, units), WIDE),
        compiler_params=params(32),
        cost_estimate=cost(2 * rows.size * units, 2 * rows.size),
        name="grad_active",
    )(rows, expert_down)


def hidden_kernel(rows_ref, up_ref, grad_ref, gate_ref, act_ref, pair_ref, gate_grad_ref):
    rows = rows_ref[0]
    gate_pre = dot(rows, up_ref[0, 0])
    upper = dot(rows, up_ref[0, 1])
    gate = gate_ref[0]
    sigma = jax.nn.sigmoid(gate_pre)
    silu = gate_pre * sigma
    active = silu * upper
    grad = grad_ref[0]
    gated = gate * grad
    act_ref[0] = (gate * active).astype(LOW)
    pair_ref[0, 0] = (gated * upper * (sigma * (1.0 + gate_pre * (1.0 - sigma)))).astype(LOW)
    pair_ref[0, 1] = (gated * silu).astype(LOW)
    gate_grad_ref[0] = jnp.sum(active * grad, axis=-1, keepdims=True)


def hidden_units(rows, expert_up, grads, gates):
    experts, count, width = rows.shape
    units = expert_up.shape[-1]
    tile = row_tile(count)
    return pl.pallas_call(
        hidden_kernel,
        grid=(experts, count // tile),
        in_specs=[
            pl.BlockSpec((1, tile, width), lambda e, r: (e, r, 0)),
            pl.BlockSpec((1, 2, width, units), lambda e, r: (e, 0, 0, 0)),
            pl.BlockSpec((1, tile, units), lambda e, r: (e, r, 0)),
            pl.BlockSpec((1, tile, 1), lambda e, r: (e, r, 0)),
        ],
        out_specs=[
            pl.BlockSpec((1, tile, units), lambda e, r: (e, r, 0)),
            pl.BlockSpec((1, 2, tile, units), lambda e, r: (e, 0, r, 0)),
            pl.BlockSpec((1, tile, 1), lambda e, r: (e, r, 0)),
        ],
        out_shape=[
            jax.ShapeDtypeStruct((experts, count, units), LOW),
            jax.ShapeDtypeStruct((experts, 2, count, units), LOW),
            jax.ShapeDtypeStruct((experts, count, 1), WIDE),
        ],
        compiler_params=params(40),
        cost_estimate=cost(4 * rows.size * units, 2 * rows.size),
        name="hidden_units",
    )(rows, expert_up, grads, gates)


def combine_kernel(transposed, experts, adds, group_of, *refs):
    lhs_ref, weight_ref, select_ref = refs[:3]
    received = refs[3] if adds else None
    outs, rows = refs[3 + adds : -1], refs[-1]
    step = pl.program_id(0)
    blocks, slots, columns = rows.shape
    capacity = slots // experts
    group = select_ref.shape[0]
    pairs = lhs_ref.shape[1]
    many = math.gcd(blocks, 8)

    @pl.when(step < experts)
    def _():
        start = pl.multiple_of(step * capacity, capacity)
        for first in range(0, blocks, many):
            piece = pl.ds(first * capacity, many * capacity)
            total = None
            for i in range(pairs):
                term = dot(lhs_ref[0, i, piece, :], weight_ref[0, i], NT if transposed else None)
                total = term if total is None else total + term
            rows[first : first + many, pl.ds(start, capacity), :] = total.astype(LOW).reshape(
                many, capacity, columns
            )

    @pl.when(step >= experts)
    def _():
        at = group_of(step) * group

        def put(ref):
            for i in range(group):
                total = dot(select_ref[i], rows[at + i])
                if adds:
                    total = total + received[0, i].astype(WIDE)
                ref[0, i] = total.astype(LOW)

        if adds:
            half = blocks // group // 2
            pl.when(step - experts < half)(lambda: put(outs[0]))
            pl.when(step - experts >= half)(lambda: put(outs[1]))
        else:
            put(outs[0])


def combine(lhs, weight, select, received, at, columns, transposed, sizes, flip, after=()):
    experts, pairs, count, units = lhs.shape
    blocks, tokens, slots = select.shape
    nx, ny, nz = sizes
    groups = nx * ny
    blocks //= 2
    count //= 2
    adds = received is not None
    part = 0 if adds else 1

    def group_of(s):
        place = jnp.clip(s - experts, 0, groups - 1)
        return place % nx * ny + place // nx if flip else place

    def expert_of(s):
        return jnp.minimum(s, experts - 1)

    if transposed:
        weight_spec = pl.BlockSpec((1, pairs, columns, units), lambda s: (expert_of(s), 0, at, 0))
    else:
        weight_spec = pl.BlockSpec((1, pairs, units, columns), lambda s: (expert_of(s), 0, 0, at))
    in_specs = [
        pl.BlockSpec((1, pairs, count, units), lambda s: (expert_of(s), 0, part, 0)),
        weight_spec,
        pl.BlockSpec((nz, tokens, slots), lambda s: (part * groups + group_of(s), 0, 0)),
    ]
    operands = [lhs, weight, select]
    if adds:
        in_specs.append(
            pl.BlockSpec((1, nz, tokens, columns), lambda s: (jnp.clip(s - experts, 0, groups - 1), 0, 0, 0))
        )
        operands.append(received)
        half = groups // 2
        out_specs = [
            pl.BlockSpec(
                (1, nz, tokens, columns), lambda s: (jnp.clip(s - experts, 0, half - 1), 0, 0, 0)
            ),
            pl.BlockSpec(
                (1, nz, tokens, columns), lambda s: (jnp.clip(s - experts - half, 0, half - 1), 0, 0, 0)
            ),
        ]
        out_shape = [jax.ShapeDtypeStruct((half, nz, tokens, columns), LOW)] * 2
    else:
        out_specs = [
            pl.BlockSpec(
                (1, nz, tokens, columns), lambda s: (jnp.clip(s - experts, 0, groups - 1), 0, 0, 0)
            )
        ]
        out_shape = [jax.ShapeDtypeStruct((groups, nz, tokens, columns), LOW)]
    return pl.pallas_call(
        without(len(operands), len(after), functools.partial(combine_kernel, transposed, experts, adds, group_of)),
        grid=(experts + groups,),
        in_specs=in_specs + [pl.BlockSpec(memory_space=pl.ANY)] * len(after),
        out_specs=out_specs,
        out_shape=out_shape,
        scratch_shapes=[pltpu.VMEM((blocks, slots, columns), LOW)],
        compiler_params=params(48),
        cost_estimate=cost(
            2 * lhs.size * columns + 2 * select.size * columns,
            2 * lhs.size + 2 * select.size + (12 if adds else 4) * blocks * tokens * columns,
        ),
        name="combine_own" if adds else "combine_other",
    )(*operands, *after)


def without(first, count, kernel):
    def run(*refs):
        kernel(*refs[:first], *refs[first + count :])

    return run


def spread(rows, columns, width):
    return (
        lax.broadcasted_iota(jnp.int32, (rows, width), 0),
        lax.broadcasted_iota(jnp.int32, (rows, width), 1) + columns,
    )


def turn(values, cosine, sine):
    return values * cosine + pltpu.roll(values, HEAD_DIM // 2, 1) * sine


def mean_last(values):
    return jnp.mean(values, axis=-1, keepdims=True)


def attention_kernel(tile, pre_ref, gain_ref, cos_ref, sin_ref, first_ref, out_refs, mixed_ref, lse_ref):
    length = pre_ref.shape[1]
    cosine, sine = cos_ref[...], sin_ref[...]
    for i in range(2):
        pre = pre_ref[i]
        inverse = lax.rsqrt(mean_last(pre * pre) + EPSILON)
        out_refs[i] = turn(pre * inverse * gain_ref[i], cosine, sine).astype(LOW)
    values = pre_ref[2].astype(LOW)
    out_refs[2] = values
    values_turned = values.T
    for start in range(0, length, tile):
        end = start + tile
        block = pl.ds(start, tile)
        scores = dot(out_refs[1, :end], out_refs[0, block], NT) * HEAD_DIM ** (-0.5)
        key, query = spread(end, start, tile)
        allowed = (key <= query) & (key >= first_ref[:, block])
        scores = jnp.where(allowed, scores, -1e30)
        top = jnp.max(scores, axis=0, keepdims=True)
        weights = jnp.exp(scores - top)
        total = jnp.sum(weights, axis=0, keepdims=True)
        lse_ref[0, :, block] = jnp.log(total) + top
        weights = (weights * (1.0 / total)).astype(LOW)
        mixed_ref[block, :] = dot(values_turned[:, :end], weights).T.astype(LOW)


def attention(projected, gains, cosine, sine, first):
    _, length, width = projected.shape
    tile = math.gcd(length, 256)
    head = lambda h: (0, 0, h)
    whole = lambda h: (0, 0)
    return pl.pallas_call(
        functools.partial(attention_kernel, tile),
        grid=(width // HEAD_DIM,),
        in_specs=[
            pl.BlockSpec((3, length, HEAD_DIM), head),
            pl.BlockSpec((2, 1, HEAD_DIM), head),
            pl.BlockSpec((length, HEAD_DIM), whole),
            pl.BlockSpec((length, HEAD_DIM), whole),
            pl.BlockSpec((1, length), whole),
        ],
        out_specs=[
            pl.BlockSpec((3, length, HEAD_DIM), head),
            pl.BlockSpec((length, HEAD_DIM), lambda h: (0, h)),
            pl.BlockSpec((1, 1, length), lambda h: (h, 0, 0)),
        ],
        out_shape=[
            jax.ShapeDtypeStruct(projected.shape, LOW),
            jax.ShapeDtypeStruct((length, width), LOW),
            jax.ShapeDtypeStruct((width // HEAD_DIM, 1, length), WIDE),
        ],
        compiler_params=params(48),
        cost_estimate=cost(6 * length * length * width, 40 * length * width),
        name="attention",
    )(projected, gains[:, None, :], cosine, sine, first)


def attention_back_kernel(
    tile,
    pre_ref,
    gain_ref,
    cos_ref,
    sin_ref,
    first_ref,
    low_ref,
    lse_ref,
    grad_ref,
    out_refs,
    gain_grad_ref,
    query_grad,
    key_grad,
    value_grad,
):
    length = pre_ref.shape[1]
    scale = HEAD_DIM ** (-0.5)
    keys_turned = low_ref[1].T
    for start in reversed(range(0, length, tile)):
        end = start + tile
        block = pl.ds(start, tile)
        queries, grads = low_ref[0, block], grad_ref[block, :]
        scores = dot(low_ref[1, :end], queries, NT) * scale
        key, query = spread(end, start, tile)
        allowed = (key <= query) & (key >= first_ref[:, block])
        weights = jnp.where(allowed, jnp.exp(scores - lse_ref[0, :, block]), 0.0)
        grad_weights = dot(low_ref[2, :end], grads, NT)
        mean = jnp.sum(grad_weights * weights, axis=0, keepdims=True)
        grad_scores = (weights * (grad_weights - mean)).astype(LOW)
        query_grad[block, :] = dot(keys_turned[:, :end], grad_scores).T
        key_term = dot(grad_scores, queries)
        value_term = dot(weights.astype(LOW), grads)
        if end == length:
            key_grad[...] = key_term
            value_grad[...] = value_term
        else:
            key_grad[:end] += key_term
            value_grad[:end] += value_term
    out_refs[2] = value_grad[...].astype(LOW)
    cosine, sine = cos_ref[...], sin_ref[...]
    for i, grad in enumerate((query_grad, key_grad)):
        grad = turn(grad[...] * scale, cosine, -sine)
        pre = pre_ref[i]
        inverse = lax.rsqrt(mean_last(pre * pre) + EPSILON)
        scaled = pre * inverse
        weighted = grad * gain_ref[i]
        out_refs[i] = (inverse * (weighted - scaled * mean_last(weighted * scaled))).astype(LOW)
        gain_grad_ref[i] = jnp.sum(grad * scaled, axis=0, keepdims=True)


def attention_back(projected, gains, cosine, sine, first, low, lse, grads, after=()):
    _, length, width = projected.shape
    tile = math.gcd(length, 256)
    head = lambda h: (0, 0, h)
    whole = lambda h: (0, 0)
    return pl.pallas_call(
        without(8, len(after), functools.partial(attention_back_kernel, tile)),
        grid=(width // HEAD_DIM,),
        in_specs=[
            pl.BlockSpec((3, length, HEAD_DIM), head),
            pl.BlockSpec((2, 1, HEAD_DIM), head),
            pl.BlockSpec((length, HEAD_DIM), whole),
            pl.BlockSpec((length, HEAD_DIM), whole),
            pl.BlockSpec((1, length), whole),
            pl.BlockSpec((3, length, HEAD_DIM), head),
            pl.BlockSpec((1, 1, length), lambda h: (h, 0, 0)),
            pl.BlockSpec((length, HEAD_DIM), lambda h: (0, h)),
        ]
        + [pl.BlockSpec(memory_space=pl.ANY)] * len(after),
        out_specs=[
            pl.BlockSpec((3, length, HEAD_DIM), head),
            pl.BlockSpec((2, 1, HEAD_DIM), head),
        ],
        out_shape=[
            jax.ShapeDtypeStruct(projected.shape, LOW),
            jax.ShapeDtypeStruct((2, 1, width), WIDE),
        ],
        scratch_shapes=[pltpu.VMEM((length, HEAD_DIM), WIDE)] * 3,
        compiler_params=params(48),
        cost_estimate=cost(14 * length * length * width, 40 * length * width),
        name="attention_back",
    )(projected, gains[:, None, :], cosine, sine, first, low, lse, grads, *after)


def weight_grad_kernel(left_ref, right_ref, out_ref):
    out_ref[0, 0] = dot(left_ref[0, 0], right_ref[0, 0], TN)


def weight_grad(left, right, tile_left, tile_right, first, last, into=None, after=()):
    experts, left_pairs, count, left_width = left.shape
    _, right_pairs, _, right_width = right.shape
    pairs = max(left_pairs, right_pairs)

    def left_map(e, i, j, p):
        return (e + first, p if left_pairs > 1 else 0, 0, i)

    def right_map(e, i, j, p):
        return (e + first, p if right_pairs > 1 else 0, 0, j)

    rest = ([] if into is None else [into]) + list(after)
    return pl.pallas_call(
        without(2, len(rest), weight_grad_kernel),
        grid=(last - first, left_width // tile_left, right_width // tile_right, pairs),
        in_specs=[
            pl.BlockSpec((1, 1, count, tile_left), left_map),
            pl.BlockSpec((1, 1, count, tile_right), right_map),
        ]
        + [pl.BlockSpec(memory_space=pl.ANY)] * len(rest),
        out_specs=pl.BlockSpec(
            (1, 1, tile_left, tile_right), lambda e, i, j, p: (e + first, p, i, j)
        ),
        out_shape=jax.ShapeDtypeStruct((experts, pairs, left_width, right_width), WIDE),
        input_output_aliases={} if into is None else {2: 0},
        compiler_params=params(48),
        cost_estimate=cost(
            2 * (last - first) * pairs * count * left_width * right_width,
            (2 * left.size + 2 * right.size + 4 * experts * pairs * left_width * right_width)
            * (last - first)
            // experts,
        ),
        name="weight_grad",
    )(left, right, *rest)


def shards(
    grid,
    hidden,
    segments,
    routes,
    attn_gain,
    qkv_weight,
    qk_gain,
    out_weight,
    moe_gain,
    router_weight,
    expert_up,
    expert_down,
    cotangent,
):
    tok_rows, width = hidden.shape
    length = segments.shape[0]
    local_experts = expert_up.shape[0]
    all_experts = router_weight.shape[1]
    nz, ny, nx = (1 << len(axes) for axes in (grid.z, grid.y, grid.x))
    n_tensor = nx * 2
    blocks = nz * ny * n_tensor
    capacity = max(2, 3 * length // (16 * n_tensor))
    capacity = -(-capacity // 16) * 16
    slots = local_experts * capacity
    expert_index = index_of(grid.expert)
    order_x = grid.x[::-1] + grid.y[::-1] + grid.z[::-1]
    order_y = grid.y[::-1] + grid.x[::-1] + grid.z[::-1]
    normed, inverse_attn = normalize(hidden, attn_gain)
    normed_all = gather_tensor(normed.astype(LOW), grid)
    cotangent_all = lax.all_gather(cotangent.astype(LOW), grid.all, axis=0, tiled=True)
    named = gather_relative(routes.T[None], (grid.core + order_x)[::-1])

    order = block_order(grid, grid.core + order_x)
    own_experts = expert_index * local_experts + jnp.arange(local_experts, dtype=jnp.int32)
    member = jnp.any(named[:, None, :, :] == own_experts[None, :, None, None], axis=2)
    token = jnp.arange(tok_rows, dtype=jnp.int32)
    earlier = (token[:, None] < token[None, :]).astype(LOW)
    rank = jnp.einsum("beu,ut->bet", member.astype(LOW), earlier, preferred_element_type=WIDE)
    rank = jnp.where(member, rank.astype(jnp.int32), -1)
    slot = jnp.arange(capacity, dtype=jnp.int32)
    chosen = rank[:, :, None, :] == slot[None, None, :, None]
    select = chosen.reshape(blocks, slots, tok_rows).astype(LOW)
    rank_back = jnp.swapaxes(rank, 1, 2)
    select_back = (rank_back[:, :, :, None] == slot).reshape(blocks, tok_rows, slots).astype(LOW)

    projected = jnp.einsum("td,cdf->ctf", normed_all, qkv_weight, preferred_element_type=WIDE)
    first_key = doc_starts(segments)
    cosine, sine = rope_tables(jnp.arange(length, dtype=jnp.int32) - first_key, HEAD_DIM // 2)
    first_key = first_key[None]
    heads_low, mixed, lse = attention(projected, qk_gain, cosine, sine, first_key)
    attended = hidden + scatter_tensor(
        jnp.dot(mixed, out_weight, preferred_element_type=WIDE).astype(LOW), grid
    ).astype(WIDE)
    moe_normed, inverse_moe = normalize(attended, moe_gain)
    routed_low = moe_normed.astype(LOW)
    routed_low, cotangent_all = lax.optimization_barrier((routed_low, cotangent_all))
    routed_all = lax.all_gather(routed_low, grid.all, axis=0, tiled=True)
    logits = jnp.dot(routed_low, router_weight, preferred_element_type=WIDE)
    shifted = jnp.exp(logits - jnp.max(logits, axis=-1, keepdims=True))
    probs = shifted / jnp.sum(shifted, axis=-1, keepdims=True)
    own_probs = probs.T[None]
    for axis in (grid.core + order_x)[::-1]:
        if axis in grid.expert:
            me = lax.axis_index(axis)
            count, columns, tokens = own_probs.shape
            parts = jnp.swapaxes(own_probs.reshape(count, 2, columns // 2, tokens), 0, 1)
            own_probs = jnp.concatenate(
                [pick(parts, me), swap(pick(parts, 1 - me), axis)]
            )
        else:
            own_probs = jnp.concatenate([own_probs, swap(own_probs, axis)])

    grad_slots = dispatch(order, select, cotangent_all, local_experts)
    grad_units = grad_active(grad_slots, expert_down)
    slot_gates = jnp.sum(
        jnp.where(chosen, own_probs[:, :, None, :], 0.0), axis=-1
    )
    slot_gates = jnp.swapaxes(slot_gates, 0, 1).reshape(local_experts, blocks * capacity, 1)
    row_slots = dispatch(order, select, routed_all, local_experts)
    gated_act, grad_pair, gate_grads = hidden_units(row_slots, expert_up, grad_units, slot_gates)

    gate_grads = jnp.swapaxes(gate_grads.reshape(local_experts, blocks, capacity), 0, 1)
    own_grads = jnp.sum(jnp.where(chosen, gate_grads[:, :, :, None], 0.0), axis=2)
    sizes = (nx, ny, nz)
    chunk = 512
    act, down_weight = gated_act[:, None], expert_down[:, None]
    units = expert_up.shape[-1]

    def to_other(lhs, weight, transposed, at, flip, after):
        (other,) = combine(
            lhs, weight, select_back, None, at, chunk, transposed, sizes, flip, after
        )
        return other, swap(other, "core")

    def to_own(lhs, weight, transposed, at, flip, received, after):
        return combine(
            lhs, weight, select_back, received, at, chunk, transposed, sizes, flip, after
        )

    def step(total, axis):
        parts = halves(total)
        return add_low(parts[0], swap(parts[1], axis))

    def first(own, rest, axis):
        total = add_low(own, swap(rest, axis))
        return total.reshape((-1,) + total.shape[2:])

    def gather_experts(values, axis):
        parts = halves(values)
        other = swap(parts[1], axis)
        me = lax.axis_index(axis)
        return jnp.concatenate(
            [jnp.where(me == 0, parts[0], other), jnp.where(me == 0, other, parts[0])], axis=1
        )

    orders = (order_x, order_y, order_x, order_y)
    grads = (grad_pair, expert_up, True)
    outs = (act, down_weight, False)
    other, sent, own, total = [None] * 4, [None] * 4, [None] * 4, [None] * 4
    small = own_grads
    small_steps = [functools.partial(lambda axis, v: step(v, axis), axis) for axis in grid.core + grid.x[::-1]]
    small_steps += [
        functools.partial(lambda axis, v: gather_experts(v, axis), axis) for axis in order_x[len(grid.x) :]
    ]
    before = ()
    for name, i in (
        ("other", 0),
        ("other", 1),
        ("own", 0),
        ("own", 1),
        ("other", 2),
        ("other", 3),
        ("own", 2),
    ):
        if name == "other":
            other[i], sent[i] = to_other(*grads, i, i % 2 == 1, before)
            before = (other[i],)
        else:
            own[i] = to_own(*grads, i, i % 2 == 1, sent[i], before)
            before = (own[i][0],)
        if small_steps:
            small = small_steps.pop(0)(tie(small, before[0]))
            before += (small,)
    for run in small_steps:
        small = run(small)
    grad_probs = small[0].T
    for i in (0, 1):
        total[i] = first(*own[i], orders[i][0])
    own[3] = to_own(*grads, 3, True, sent[3], before + (total[0], total[1]))
    o_other, o_sent, o_own = [None] * 4, [None] * 4, [None] * 4
    o_other[0], o_sent[0] = to_other(*outs, 0, False, (own[3][0],))
    for i in (0, 1):
        total[i] = step(total[i], orders[i][1])
    o_other[1], o_sent[1] = to_other(*outs, 1, False, (o_other[0], total[0], total[1]))
    o_own[0] = to_own(*outs, 0, False, o_sent[0], (o_other[1],))
    for i in (0, 1):
        total[i] = step(total[i], orders[i][2])
    for i in (2, 3):
        total[i] = first(*own[i], orders[i][0])
    o_other[2], o_sent[2] = to_other(*outs, 2, False, (o_own[0][0],) + tuple(total))
    o_own[1] = to_own(*outs, 1, False, o_sent[1], (o_other[2],))
    for i in (0, 1):
        total[i] = step(total[i], orders[i][3])
    for i in (2, 3):
        total[i] = step(total[i], orders[i][1])
    o_other[3], o_sent[3] = to_other(*outs, 3, False, (o_own[1][0],) + tuple(total))
    for i in (2, 3):
        total[i] = step(total[i], orders[i][2])
    o_own[2] = to_own(*outs, 2, False, o_sent[2], (o_other[3], total[2], total[3]))
    for i in (2, 3):
        total[i] = step(total[i], orders[i][3])
    for i in range(4):
        total[i] = scatter(total[i], orders[i][4:])[0]
    rows_back = jnp.concatenate(total, axis=-1).astype(WIDE)

    chose = jnp.any(routes[:, :, None] == jnp.arange(all_experts, dtype=jnp.int32), axis=1)
    grad_probs = jnp.where(chose, grad_probs, 0.0)
    grad_logits = probs * (grad_probs - jnp.sum(probs * grad_probs, axis=-1, keepdims=True))
    logits_low = grad_logits.astype(LOW)
    router_grad = jnp.einsum("td,te->de", routed_low, logits_low, preferred_element_type=WIDE)
    grad_moe = jnp.einsum("te,de->td", logits_low, router_weight, preferred_element_type=WIDE)
    grad_moe = grad_moe + rows_back
    grad_attended, moe_gain_grad = norm_back(grad_moe, attended, inverse_moe, moe_gain)
    grad_attended = grad_attended + cotangent
    grad_low = grad_attended.astype(LOW)
    piece = gather_tensor(grad_low, grid)

    o_own[3] = to_own(*outs, 3, False, o_sent[3], (grad_low, o_own[2][0]))
    piece = tie(piece, o_own[3][0])
    outputs = []
    for i in range(4):
        mine, rest = o_own[i]
        outputs.append(scatter(first(mine, tie(rest, piece), order_x[0]), order_x[1:])[0])
    output = attended + jnp.concatenate(outputs, axis=-1).astype(WIDE)

    grad_mixed = jnp.einsum("td,fd->tf", piece, out_weight, preferred_element_type=WIDE).astype(LOW)
    out_acc = jnp.einsum(
        "tf,td->fd", mixed, tie(piece, grad_mixed), preferred_element_type=WIDE
    ).astype(LOW)
    out_grad = sum_expert(out_acc, grid)
    grad_proj, qk_gain_grad = attention_back(
        projected, qk_gain, cosine, sine, first_key, heads_low, lse, grad_mixed, (out_acc,)
    )
    qk_gain_grad = qk_gain_grad.reshape(2, -1)
    grad_normed = jnp.einsum(
        "ctf,cdf->td", grad_proj, qkv_weight, preferred_element_type=WIDE
    ).astype(LOW)
    qkv_parts = [
        jnp.einsum("td,tf->df", normed_all, grad_proj[i], preferred_element_type=WIDE).astype(LOW)
        for i in range(3)
    ]
    down_grad = weight_grad(
        act, grad_slots[:, None], units, 512, 0, local_experts, None, tuple(qkv_parts) + (grad_normed,)
    )
    up_grad = weight_grad(
        row_slots[:, None], grad_pair, 512, units, 0, local_experts, None, (down_grad,)
    )
    down_grad = down_grad.reshape(expert_down.shape)
    qkv_grad = jnp.stack([sum_expert(part, grid) for part in qkv_parts])
    grad_normed = scatter_tensor(grad_normed, grid).astype(WIDE)
    grad_hidden, attn_gain_grad = norm_back(grad_normed, hidden, inverse_attn, attn_gain)
    grad_hidden = grad_hidden + grad_attended
    qk_gain_grad = sum_over(qk_gain_grad, grid.expert)
    router_grad = lax.psum(router_grad, grid.all)
    attn_gain_grad, moe_gain_grad = sum_over(
        jnp.stack([attn_gain_grad, moe_gain_grad]), grid.all[::-1]
    )
    return (
        output,
        grad_hidden,
        attn_gain_grad,
        qkv_grad,
        qk_gain_grad,
        out_grad,
        moe_gain_grad,
        router_grad,
        up_grad,
        down_grad,
    )


def solution(mesh):
    grid = Grid(mesh.shape["expert"], mesh.shape["tensor"])
    devices = Mesh(mesh.devices.reshape((2,) * len(grid.all)), grid.all)
    rows = P(grid.all, None)
    return jax.shard_map(
        functools.partial(shards, grid),
        mesh=devices,
        in_specs=(
            rows,
            P(grid.expert),
            rows,
            P(),
            P(None, None, grid.tensor),
            P(None, grid.tensor),
            P(grid.tensor, None),
            P(),
            P(),
            P(grid.expert, None, None, grid.tensor),
            P(grid.expert, grid.tensor, None),
            rows,
        ),
        out_specs=(
            rows,
            rows,
            P(),
            P(None, None, grid.tensor),
            P(None, grid.tensor),
            P(grid.tensor, None),
            P(),
            P(),
            P(grid.expert, None, None, grid.tensor),
            P(grid.expert, grid.tensor, None),
        ),
        check_vma=False,
    )
```

time: 2010 us -> 1540 us (0.77)
  starting transfers between devices: 372 us -> 96 us
  other arithmetic: 177 us -> 89.1 us
  Pallas kernels: 447 us -> 529 us
  blocking collectives: 76.3 us -> 0 us
  matrix products: 100 us -> 40.9 us
  local copies, waits for them, and re-layouts: 134 us -> 78.8 us
    ppermute x37 -> x95, waiting for transfers between devices: 190 us -> 549 us  [swap(): return lax.ppermute(values, axis, [(0, 1), (1, 0)])]
    ppermute x111 -> x0, starting transfers between devices: 314 us -> none  [the longest x41 188 us: line_scatter(): up = lax.ppermute(block, axis, [(i, i + 1) for i in range(step)])]
    all_gather x5 -> x2, waiting for transfers between devices: 310 us -> 127 us  [the longest x1 80.2 us: shards(): lax.all_gather(cotangent.astype(LOW), grid.all, axis=0, tiled=True)]
    ppermute x111 -> x0, waiting for transfers between devices: 164 us -> none  [the longest x5 68.7 us: sum_all(): lax.ppermute(values, axis, [(i, i ^ step) for i in range(n)])]
    pallas_call x10 -> x20, Pallas kernels: 281 us -> 363 us  [the longest x16 205 us: combine(): pl.pallas_call(without(len(operands), len(after), functools.partial(combi...]
    dot_general x14 -> x6, matrix products: 88.7 us -> 32 us  [the longest x1 11.2 us: shards(): jnp.einsum('ctf,cdf->td', grad_proj, qkv_weight, preferred_element_type=W...]
    convert_element_type x78 -> x40, other arithmetic: 75.8 us -> 22.8 us  [add_low(): return total.astype(terms[0].dtype)]
    all_gather x1 -> x0, blocking collectives: 40.5 us -> none  [shards(): routes_all = lax.all_gather(routes, ALL, axis=0, tiled=True)]
  transfers between devices with their start and end apart: 154 -> 98, of which waited for: 54 -> 57; matrix products, arithmetic and copies ran while one was open for 14% -> 11% of each run, Pallas kernels for 18% -> 26%
where the time goes in v2:
time: 1540 us; the launch traced here: 1530 us
  waiting for transfers between devices  676 us (44%)
  Pallas kernels  529 us (34%)
  starting transfers between devices  96 us (6%)
  other arithmetic  89.1 us (6%)
  local copies, waits for them, and re-layouts  78.8 us (5%)
  matrix products  40.9 us (3%)
  between operations  16.5 us (1%)
    ppermute x95, waiting for transfers between devices, swap(): return lax.ppermute(values, axis, [(0, 1), (1, 0)])  549 us
    pallas_call x16, Pallas kernels, combine(): pl.pallas_call(without(len(operands), len(after), functools.partial(combi...  205 us
    pallas_call x2, Pallas kernels, weight_grad(): pl.pallas_call(without(2, len(rest), weight_grad_kernel), grid=(last - fi...  126 us
    ppermute x95, starting transfers between devices, swap(): return lax.ppermute(values, axis, [(0, 1), (1, 0)])  95.9 us
    pallas_call x2, Pallas kernels, dispatch(): pl.pallas_call(dispatch_kernel, grid_spec=pltpu.PrefetchScalarGridSpec(nu...  89 us
    all_gather x1, waiting for transfers between devices, shards(): lax.all_gather(cotangent.astype(LOW), grid.all, axis=0, tiled=True)  80.2 us
    pallas_call x1, Pallas kernels, hidden_units(): pl.pallas_call(hidden_kernel, grid=(experts, count // tile), in_specs=[pl...  47.3 us
    all_gather x1, waiting for transfers between devices, shards(): routed_all = lax.all_gather(routed_low, grid.all, axis=0, tiled=True)  46.8 us
  transfers between devices with their start and end apart: 98, of which 57 were waited for; matrix products, arithmetic and copies ran while one was open for 11% of the time, Pallas kernels for 26%

profile of v2, /device:TPU:0, one launch (start us, length us, event | category | flops | bytes accessed | tf_op | source)
XLA Modules:
  0.0 1526.8 jit_solution(2426108347066028113)
XLA Ops:
  15.6 30.8 %collective-permute-done = bf16[256,2048]{1,0:T(8,128)(2,1)} collective-permute-done((bf16[256,2048]{1,0:T(8,128)(2,1)S(1)}, bf16[256,2048]{1,0:T(8,128)(2,1)}, u32[]{:S(2)}, u32[]{:S(2)}) %collective-permute-start) | collective-permute-done | bytes 1048608 | tf_op jit(solution)/shard_map/ppermute | solution.py:72
  71.5 14.9 attention.1
  102.8 36.1 %collective-permute-done.3 = bf16[256,2048]{1,0:T(8,128)(2,1)} collective-permute-done((bf16[256,2048]{1,0:T(8,128)(2,1)S(1)}, bf16[256,2048]{1,0:T(8,128)(2,1)}, u32[]{:S(2)}, u32[]{:S(2)}) %collective-permute-start.3) | collective-permute-done | bytes 1048608 | tf_op jit(solution)/shard_map/ppermute | solution.py:72
  144.1 80.2 %all-gather.3.cloned.1.call-done = bf16[8192,2048]{1,0:T(8,128)(2,1)} async-done(((bf16[256,2048]{1,0:T(8,128)(2,1)}), bf16[8192,2048]{1,0:T(8,128)(2,1)}) %all-gather.3.cloned.1.call-update) | async-done | bytes 33554448 | tf_op jit(solution)/shard_map/all_gather | solution.py:612
  261.7 13.1 copy.48
  288.6 45.3 %dispatch.3.rows_ref = bf16[8,1536,2048]{2,1,0:T(8,128)(2,1)} custom-call(s32[32]{0:T(128)S(1)} %add.397.order_ref, bf16[32,384,256]{2,1,0:T(8,128)(2,1)S(1)} %fusion.select_ref, bf16[32,256,2048]{2,1,0:T(8,128)(2,1)} %bitcast.398), custom_call_target="tpu_custom_call" | custom-call | flops 25769803776 | bytes 167772160 | tf_op jit(solution)/shard_map/dispatch/pallas_call | solution.py:181
  334.0 30.6 %grad_active.1.grad_ref = f32[8,1536,256]{2,1,0:T(8,128)S(1)} custom-call(bf16[8,1536,2048]{2,1,0:T(8,128)(2,1)} %dispatch.3.rows_ref, bf16[8,256,2048]{2,1,0:T(8,128)(2,1)S(1)} %bitcast.328), custom_call_target="tpu_custom_call" | custom-call | flops 25769803776 | bytes 100663296 | tf_op jit(solution)/shard_map/grad_active/pallas_call | solution.py:211
  377.2 46.8 %all-gather.5.cloned.1.call-done = bf16[8192,2048]{1,0:T(8,128)(2,1)} async-done(((bf16[256,2048]{1,0:T(8,128)(2,1)}), bf16[8192,2048]{1,0:T(8,128)(2,1)}) %all-gather.5.cloned.1.call-update) | async-done | bytes 33554448 | tf_op jit(solution)/shard_map/all_gather | solution.py:639
  426.8 43.7 %dispatch.2.rows_ref = bf16[8,1536,2048]{2,1,0:T(8,128)(2,1)} custom-call(s32[32]{0:T(128)S(1)} %add.397.order_ref, bf16[32,384,256]{2,1,0:T(8,128)(2,1)S(1)} %copy-done.2, bf16[32,256,2048]{2,1,0:T(8,128)(2,1)} %bitcast.399), custom_call_target="tpu_custom_call" | custom-call | flops 25769803776 | bytes 167772160 | tf_op jit(solution)/shard_map/dispatch/pallas_call | solution.py:181
  470.5 47.3 %hidden_units.1 = (bf16[8,1536,256]{2,1,0:T(8,128)(2,1)S(1)}, bf16[8,2,1536,256]{3,2,1,0:T(8,128)(2,1)}, f32[8,1536,1]{2,1,0:T(8,128)S(1)}) custom-call(bf16[8,1536,2048]{2,1,0:T(8,128)(2,1)} %dispatch.2.rows_ref, bf16[8,2,2048,256]{3,2,1,0:T(8,128)(2,1)} %refs_1_.15, f32[8,1536,256]{2,1,0:T(8,128)} %copy-done.40, f32[8,1536,1]{2,1,0:T(8,128)} %reshape.659.gate_ref), custom_call_target="tpu_custom_call" | custom-call | flops 51539607552 | bytes 100663296 | tf_op jit(solution)/shard_map/hidden_units/pallas_call | solution.py:246
  527.9 12.8 combine_other.8.refs_3_
  548.1 14.1 combine_other.9.refs_4_
  568.8 13.7 combine_own.8
  589.1 13.8 combine_own.9
  611.0 14.0 combine_other.10.refs_3_
  629.9 12.8 combine_other.11.refs_4_
  642.9 28.0 %collective-permute-done.23 = bf16[2,4,256,512]{3,2,1,0:T(8,128)(2,1)} collective-permute-done((bf16[2,4,256,512]{3,2,1,0:T(8,128)(2,1)}, bf16[2,4,256,512]{3,2,1,0:T(8,128)(2,1)}, u32[]{:S(2)}, u32[]{:S(2)}) %collective-permute-start.23) | collective-permute-done | bytes 2097184 | tf_op jit(solution)/shard_map/ppermute | solution.py:72
  679.0 13.6 combine_own.10
  694.6 14.1 combine_own.11
  714.5 13.3 collective-permute-done.28
  746.3 11.1 collective-permute-done.36
  759.6 11.8 combine_other.12.refs_3_
  776.7 11.8 combine_other.13.refs_4_
  790.8 12.0 collective-permute-done.38
  820.3 11.5 combine_own.12
  831.8 13.1 combine_other.14.refs_4_
  845.0 11.9 combine_own.13
  860.6 11.9 combine_other.15.refs_4_
  879.2 12.4 combine_own.14
  892.9 11.5 combine_own.15
  911.5 16.4 %attention_back.1 = (bf16[3,1024,512]{2,1,0:T(8,128)(2,1)}, f32[2,1,512]{2,1,0:T(1,128)S(1)}) custom-call(f32[3,1024,512]{2,1,0:T(8,128)} %convolution_bitcast_fusion.pre_ref.refs_0_, f32[2,1,512]{2,1,0:T(1,128)S(1)} %copy-done.28, f32[1024,128]{1,0:T(8,128)S(1)} %copy-done.22, f32[1024,128]{1,0:T(8,128)S(1)} %copy-done.24, s32[1,1024]{1,0:T(1,128)S(1)} %bitcast.318, ...), custom_call_target="tpu_custom_call" | custom-call | flops 15032385536 | bytes 41943040 | tf_op jit(solution)/shard_map/attention_back/pallas_call | solution.py:513
  928.0 11.2 bitcast_convert_fusion.refs_5_
  951.9 41.0 %weight_grad.2.refs_2_ = f32[8,1,256,2048]{3,2,1,0:T(8,128)} custom-call(bf16[8,1,1536,256]{3,2,1,0:T(8,128)(2,1)} %bitcast.337, bf16[8,1,1536,2048]{3,2,1,0:T(8,128)(2,1)} %bitcast.402, bf16[2048,512]{1,0:T(8,128)(2,1)S(1)} %convolution_convert_fusion.3.refs_2_, bf16[2048,512]{1,0:T(8,128)(2,1)S(1)} %convolution_convert_fusion.2.refs_3_, ...), custom_call_target="tpu_custom_call" | custom-call | flops 25769803776 | bytes 146800640 | tf_op jit(solution)/shard_map/weight_grad/pallas_call | solution.py:558
  992.9 85.5 %weight_grad.3 = f32[8,2,2048,256]{3,2,1,0:T(8,128)} custom-call(bf16[8,1,1536,2048]{3,2,1,0:T(8,128)(2,1)} %bitcast.403, bf16[8,2,1536,256]{3,2,1,0:T(8,128)(2,1)} %get-tuple-element.51.refs_0_.refs_1_, f32[8,1,256,2048]{3,2,1,0:T(8,128)} %weight_grad.2.refs_2_), custom_call_target="tpu_custom_call" | custom-call | flops 51539607552 | bytes 192937984 | tf_op jit(solution)/shard_map/weight_grad/pallas_call | solution.py:558
  1096.3 20.8 %collective-permute-done.74 = bf16[1024,512]{1,0:T(8,128)(2,1)S(1)} collective-permute-done((bf16[1024,512]{1,0:T(8,128)(2,1)S(1)}, bf16[1024,512]{1,0:T(8,128)(2,1)S(1)}, u32[]{:S(2)}, u32[]{:S(2)}) %collective-permute-start.74) | collective-permute-done | bytes 1048608 | tf_op jit(solution)/shard_map/ppermute | solution.py:72
  1119.3 15.9 %collective-permute-done.68 = bf16[1024,512]{1,0:T(8,128)(2,1)S(1)} collective-permute-done((bf16[1024,512]{1,0:T(8,128)(2,1)S(1)}, bf16[1024,512]{1,0:T(8,128)(2,1)S(1)}, u32[]{:S(2)}, u32[]{:S(2)}) %collective-permute-start.68) | collective-permute-done | bytes 1048608 | tf_op jit(solution)/shard_map/ppermute | solution.py:72
  1137.8 12.3 collective-permute-done.81
  1152.0 12.2 collective-permute-done.75
  1189.1 13.8 collective-permute-done.76
  1203.0 11.1 collective-permute-done.70
  1214.2 11.1 collective-permute-done.83
  1225.4 11.2 collective-permute-done.77
  1242.3 13.9 collective-permute-done.71
  1265.4 18.7 %collective-permute-done.45 = bf16[2,4,256,512]{3,2,1,0:T(8,128)(2,1)S(1)} collective-permute-done((bf16[2,4,256,512]{3,2,1,0:T(8,128)(2,1)S(1)}, bf16[2,4,256,512]{3,2,1,0:T(8,128)(2,1)S(1)}, u32[]{:S(2)}, u32[]{:S(2)}) %collective-permute-start.45) | collective-permute-done | bytes 2097184 | tf_op jit(solution)/shard_map/ppermute | solution.py:72
  1306.1 11.8 collective-permute-done.62
  1335.2 86.5 %collective-permute-done.65 = f32[2,2048]{1,0:T(2,128)S(1)} collective-permute-done((f32[2,2048]{1,0:T(2,128)S(1)}, f32[2,2048]{1,0:T(2,128)S(1)}, u32[]{:S(2)}, u32[]{:S(2)}) %collective-permute-start.65) | collective-permute-done | bytes 16416 | tf_op jit(solution)/shard_map/ppermute | solution.py:72
  1454.7 12.5 collective-permute-done.94
  1482.2 19.5 %collective-permute-done.60 = bf16[1,256,512]{2,1,0:T(8,128)(2,1)S(1)} collective-permute-done((bf16[1,256,512]{2,1,0:T(8,128)(2,1)S(1)}, bf16[1,256,512]{2,1,0:T(8,128)(2,1)S(1)}, u32[]{:S(2)}, u32[]{:S(2)}) %collective-permute-start.60) | collective-permute-done | bytes 262176 | tf_op jit(solution)/shard_map/ppermute | solution.py:72
  (592 shorter events, 426.8 us)
Async XLA Ops:
  7.2 217.2 %all-gather.3.cloned.1.call-start = ((), (), s32[]{:S(2)}) async-start(), calls=%async_computation | async-start | bytes 34603008 | tf_op jit(solution)/shard_map/all_gather | solution.py:612
  10.1 413.9 %all-gather.5.cloned.1.call-start = ((), (), s32[]{:S(2)}) async-start(), calls=%async_computation.1 | async-start | bytes 34603008 | tf_op jit(solution)/shard_map/all_gather | solution.py:639
  12.6 33.8 %collective-permute-start = (bf16[256,2048]{1,0:T(8,128)(2,1)S(1)}, bf16[256,2048]{1,0:T(8,128)(2,1)}, u32[]{:S(2)}, u32[]{:S(2)}) collective-permute-start(bf16[256,2048]{1,0:T(8,128)(2,1)S(1)} %multiply_convert_fusion.1), channel_id=1, source_target_pairs={{0,2},{2,0},{1,3},{3,1},{4,6},{6,4},{5,7},{7,5},{8,10},{10,8},{9,1... | collective-permute-start | bytes 3145736 | tf_op jit(solution)/shard_map/ppermute | solution.py:72
  101.0 37.9 %collective-permute-start.3 = (bf16[256,2048]{1,0:T(8,128)(2,1)S(1)}, bf16[256,2048]{1,0:T(8,128)(2,1)}, u32[]{:S(2)}, u32[]{:S(2)}) collective-permute-start(bf16[256,2048]{1,0:T(8,128)(2,1)S(1)} %dynamic-slice_bitcast_fusion.7), channel_id=1, source_target_pairs={{0,2},{2,0},{1,3},{3,1},{4,6},{6,4},{5,7},{7,5},{8,10},{10,8},{9,1... | collective-permute-start | bytes 3145736 | tf_op jit(solution)/shard_map/ppermute | solution.py:72
  224.4 1293.5 %all-reduce.2.cloned.1.call-start = ((), (), s32[]{:S(2)}) async-start(), calls=%async_computation.2 | async-start | bytes 1048576 | tf_op jit(solution)/shard_map/psum | solution.py:806
  287.0 46.8 %collective-permute-start.12 = (f32[8,8,256]{2,1,0:T(8,128)S(1)}, f32[8,8,256]{2,1,0:T(8,128)S(1)}, u32[]{:S(2)}, u32[]{:S(2)}) collective-permute-start(f32[8,8,256]{2,1,0:T(8,128)S(1)} %pad_maximum_fusion.16), channel_id=1, source_target_pairs={{0,2},{2,0},{1,3},{3,1},{4,6},{6,4},{5,7},{7,5},{8,10},{10,8},{9,1... | collective-permute-start | bytes 196616 | tf_op jit(solution)/shard_map/ppermute | solution.py:72
  333.9 35.5 %collective-permute-start.13 = (f32[16,8,256]{2,1,0:T(8,128)S(1)}, f32[16,8,256]{2,1,0:T(8,128)S(1)}, u32[]{:S(2)}, u32[]{:S(2)}) collective-permute-start(f32[16,8,256]{2,1,0:T(8,128)S(1)} %pad_maximum_fusion.15), channel_id=1, source_target_pairs={{0,1},{1,0},{2,3},{3,2},{4,5},{5,4},{6,7},{7,6},{8,9},{9,8},{10,11... | collective-permute-start | bytes 393224 | tf_op jit(solution)/shard_map/ppermute | solution.py:72
  626.5 44.4 %collective-permute-start.23 = (bf16[2,4,256,512]{3,2,1,0:T(8,128)(2,1)}, bf16[2,4,256,512]{3,2,1,0:T(8,128)(2,1)}, u32[]{:S(2)}, u32[]{:S(2)}) collective-permute-start(bf16[2,4,256,512]{3,2,1,0:T(8,128)(2,1)} %copy-done.35), channel_id=1, source_target_pairs={{0,2},{2,0},{1,3},{3,1},{4,6},{6,4},{5,7},{7,5},{8,10},{10,8},{9,1... | collective-permute-start | bytes 6291464 | tf_op jit(solution)/shard_map/ppermute | solution.py:72
  627.9 47.8 %collective-permute-start.24 = (bf16[2,4,256,512]{3,2,1,0:T(8,128)(2,1)}, bf16[2,4,256,512]{3,2,1,0:T(8,128)(2,1)S(1)}, u32[]{:S(2)}, u32[]{:S(2)}) collective-permute-start(bf16[2,4,256,512]{3,2,1,0:T(8,128)(2,1)} %copy-done.36), channel_id=1, source_target_pairs={{0,4},{4,0},{1,5},{5,1},{2,6},{6,2},{3,7},{7,3},{8,12},{12,8},{9,1... | collective-permute-start | bytes 6291464 | tf_op jit(solution)/shard_map/ppermute | solution.py:72
  628.5 50.5 %collective-permute-start.22 = (bf16[4,4,256,512]{3,2,1,0:T(8,128)(2,1)}, bf16[4,4,256,512]{3,2,1,0:T(8,128)(2,1)}, u32[]{:S(2)}, u32[]{:S(2)}) collective-permute-start(bf16[4,4,256,512]{3,2,1,0:T(8,128)(2,1)} %combine_other.10.refs_3_), channel_id=1, source_target_pairs={{0,1},{1,0},{2,3},{3,2},{4,5},{5,4},{6,7},{7,6},{8,9},{9,8},{10,11... | collective-permute-start | bytes 12582920 | tf_op jit(solution)/shard_map/ppermute | solution.py:72
  642.7 51.9 %collective-permute-start.21 = (bf16[4,4,256,512]{3,2,1,0:T(8,128)(2,1)S(1)}, bf16[4,4,256,512]{3,2,1,0:T(8,128)(2,1)}, u32[]{:S(2)}, u32[]{:S(2)}) collective-permute-start(bf16[4,4,256,512]{3,2,1,0:T(8,128)(2,1)S(1)} %combine_other.11.refs_4_), channel_id=1, source_target_pairs={{0,1},{1,0},{2,3},{3,2},{4,5},{5,4},{6,7},{7,6},{8,9},{9,8},{10,11... | collective-permute-start | bytes 12582920 | tf_op jit(solution)/shard_map/ppermute | solution.py:72
  674.2 36.0 %collective-permute-start.26 = (bf16[4,256,512]{2,1,0:T(8,128)(2,1)}, bf16[4,256,512]{2,1,0:T(8,128)(2,1)S(1)}, u32[]{:S(2)}, u32[]{:S(2)}) collective-permute-start(bf16[4,256,512]{2,1,0:T(8,128)(2,1)} %slice_bitcast_fusion.14), channel_id=1, source_target_pairs={{0,4},{4,0},{1,5},{5,1},{2,6},{6,2},{3,7},{7,3},{8,12},{12,8},{9,1... | collective-permute-start | bytes 3145736 | tf_op jit(solution)/shard_map/ppermute | solution.py:72
  677.6 33.6 %collective-permute-start.27 = (bf16[4,256,512]{2,1,0:T(8,128)(2,1)}, bf16[4,256,512]{2,1,0:T(8,128)(2,1)}, u32[]{:S(2)}, u32[]{:S(2)}) collective-permute-start(bf16[4,256,512]{2,1,0:T(8,128)(2,1)} %slice_bitcast_fusion.12), channel_id=1, source_target_pairs={{0,2},{2,0},{1,3},{3,1},{4,6},{6,4},{5,7},{7,5},{8,10},{10,8},{9,1... | collective-permute-start | bytes 3145736 | tf_op jit(solution)/shard_map/ppermute | solution.py:72
  694.0 50.9 %collective-permute-start.32 = (bf16[2,4,256,512]{3,2,1,0:T(8,128)(2,1)S(1)}, bf16[2,4,256,512]{3,2,1,0:T(8,128)(2,1)S(1)}, u32[]{:S(2)}, u32[]{:S(2)}) collective-permute-start(bf16[2,4,256,512]{3,2,1,0:T(8,128)(2,1)S(1)} %get-tuple-element.66), channel_id=1, source_target_pairs={{0,2},{2,0},{1,3},{3,1},{4,6},{6,4},{5,7},{7,5},{8,10},{10,8},{9,1... | collective-permute-start | bytes 6291464 | tf_op jit(solution)/shard_map/ppermute | solution.py:72
  708.7 48.6 %collective-permute-start.36 = (bf16[2,4,256,512]{3,2,1,0:T(8,128)(2,1)S(1)}, bf16[2,4,256,512]{3,2,1,0:T(8,128)(2,1)S(1)}, u32[]{:S(2)}, u32[]{:S(2)}) collective-permute-start(bf16[2,4,256,512]{3,2,1,0:T(8,128)(2,1)S(1)} %get-tuple-element.67), channel_id=1, source_target_pairs={{0,4},{4,0},{1,5},{5,1},{2,6},{6,2},{3,7},{7,3},{8,12},{12,8},{9,1... | collective-permute-start | bytes 6291464 | tf_op jit(solution)/shard_map/ppermute | solution.py:72
  736.0 67.2 %collective-permute-start.31 = (bf16[1,256,512]{2,1,0:T(8,128)(2,1)S(1)}, bf16[1,256,512]{2,1,0:T(8,128)(2,1)S(1)}, u32[]{:S(2)}, u32[]{:S(2)}) collective-permute-start(bf16[1,256,512]{2,1,0:T(8,128)(2,1)S(1)} %slice.318), channel_id=1, source_target_pairs={{0,16},{16,0},{1,17},{17,1},{2,18},{18,2},{3,19},{19,3},{4,20},{20... | collective-permute-start | bytes 786440 | tf_op jit(solution)/shard_map/ppermute | solution.py:72
  771.4 48.9 %collective-permute-start.25 = (bf16[4,4,256,512]{3,2,1,0:T(8,128)(2,1)}, bf16[4,4,256,512]{3,2,1,0:T(8,128)(2,1)}, u32[]{:S(2)}, u32[]{:S(2)}) collective-permute-start(bf16[4,4,256,512]{3,2,1,0:T(8,128)(2,1)} %combine_other.12.refs_3_), channel_id=1, source_target_pairs={{0,1},{1,0},{2,3},{3,2},{4,5},{5,4},{6,7},{7,6},{8,9},{9,8},{10,11... | collective-permute-start | bytes 12582920 | tf_op jit(solution)/shard_map/ppermute | solution.py:72
  788.5 56.5 %collective-permute-start.42 = (bf16[4,4,256,512]{3,2,1,0:T(8,128)(2,1)}, bf16[4,4,256,512]{3,2,1,0:T(8,128)(2,1)}, u32[]{:S(2)}, u32[]{:S(2)}) collective-permute-start(bf16[4,4,256,512]{3,2,1,0:T(8,128)(2,1)} %combine_other.13.refs_4_), channel_id=1, source_target_pairs={{0,1},{1,0},{2,3},{3,2},{4,5},{5,4},{6,7},{7,6},{8,9},{9,8},{10,11... | collective-permute-start | bytes 12582920 | tf_op jit(solution)/shard_map/ppermute | solution.py:72
  818.9 38.0 %collective-permute-start.40 = (bf16[256,2048]{1,0:T(8,128)(2,1)S(1)}, bf16[256,2048]{1,0:T(8,128)(2,1)S(1)}, u32[]{:S(2)}, u32[]{:S(2)}) collective-permute-start(bf16[256,2048]{1,0:T(8,128)(2,1)S(1)} %get-tuple-element.89.refs_4_), channel_id=1, source_target_pairs={{0,2},{2,0},{1,3},{3,1},{4,6},{6,4},{5,7},{7,5},{8,10},{10,8},{9,1... | collective-permute-start | bytes 3145736 | tf_op jit(solution)/shard_map/ppermute | solution.py:72
  844.9 33.7 %collective-permute-start.44 = (bf16[4,4,256,512]{3,2,1,0:T(8,128)(2,1)}, bf16[4,4,256,512]{3,2,1,0:T(8,128)(2,1)}, u32[]{:S(2)}, u32[]{:S(2)}) collective-permute-start(bf16[4,4,256,512]{3,2,1,0:T(8,128)(2,1)} %combine_other.14.refs_4_), channel_id=1, source_target_pairs={{0,1},{1,0},{2,3},{3,2},{4,5},{5,4},{6,7},{7,6},{8,9},{9,8},{10,11... | collective-permute-start | bytes 12582920 | tf_op jit(solution)/shard_map/ppermute | solution.py:72
  946.6 309.7 %collective-permute-start.57 = (bf16[2,4,256,512]{3,2,1,0:T(8,128)(2,1)S(1)}, bf16[2,4,256,512]{3,2,1,0:T(8,128)(2,1)}, u32[]{:S(2)}, u32[]{:S(2)}) collective-permute-start(bf16[2,4,256,512]{3,2,1,0:T(8,128)(2,1)S(1)} %get-tuple-element.78), channel_id=1, source_target_pairs={{0,2},{2,0},{1,3},{3,1},{4,6},{6,4},{5,7},{7,5},{8,10},{10,8},{9,1... | collective-permute-start | bytes 6291464 | tf_op jit(solution)/shard_map/ppermute | solution.py:72
  947.3 311.5 %collective-permute-start.53 = (bf16[2,4,256,512]{3,2,1,0:T(8,128)(2,1)S(1)}, bf16[2,4,256,512]{3,2,1,0:T(8,128)(2,1)}, u32[]{:S(2)}, u32[]{:S(2)}) collective-permute-start(bf16[2,4,256,512]{3,2,1,0:T(8,128)(2,1)S(1)} %get-tuple-element.76), channel_id=1, source_target_pairs={{0,2},{2,0},{1,3},{3,1},{4,6},{6,4},{5,7},{7,5},{8,10},{10,8},{9,1... | collective-permute-start | bytes 6291464 | tf_op jit(solution)/shard_map/ppermute | solution.py:72
  949.7 141.2 %collective-permute-start.80 = (bf16[1024,512]{1,0:T(8,128)(2,1)}, bf16[1024,512]{1,0:T(8,128)(2,1)}, u32[]{:S(2)}, u32[]{:S(2)}) collective-permute-start(bf16[1024,512]{1,0:T(8,128)(2,1)} %dynamic-slice_bitcast_fusion.3), channel_id=1, source_target_pairs={{0,4},{4,0},{1,5},{5,1},{2,6},{6,2},{3,7},{7,3},{8,12},{12,8},{9,1... | collective-permute-start | bytes 3145736 | tf_op jit(solution)/shard_map/ppermute | solution.py:72
  950.4 132.0 %collective-permute-start.86 = (f32[2,512]{1,0:T(2,128)S(1)}, f32[2,512]{1,0:T(2,128)S(1)}, u32[]{:S(2)}, u32[]{:S(2)}) collective-permute-start(f32[2,512]{1,0:T(2,128)S(1)} %bitcast.397), channel_id=1, source_target_pairs={{0,16},{16,0},{1,17},{17,1},{2,18},{18,2},{3,19},{19,3},{4,20},{20... | collective-permute-start | bytes 12296 | tf_op jit(solution)/shard_map/ppermute | solution.py:72
  950.5 143.4 %collective-permute-start.89 = (bf16[256,2048]{1,0:T(8,128)(2,1)S(1)}, bf16[256,2048]{1,0:T(8,128)(2,1)}, u32[]{:S(2)}, u32[]{:S(2)}) collective-permute-start(bf16[256,2048]{1,0:T(8,128)(2,1)S(1)} %dynamic-slice_bitcast_fusion.2), channel_id=1, source_target_pairs={{0,4},{4,0},{1,5},{5,1},{2,6},{6,2},{3,7},{7,3},{8,12},{12,8},{9,1... | collective-permute-start | bytes 3145736 | tf_op jit(solution)/shard_map/ppermute | solution.py:72
  1089.7 173.5 %collective-permute-start.49 = (bf16[2,4,256,512]{3,2,1,0:T(8,128)(2,1)S(1)}, bf16[2,4,256,512]{3,2,1,0:T(8,128)(2,1)S(1)}, u32[]{:S(2)}, u32[]{:S(2)}) collective-permute-start(bf16[2,4,256,512]{3,2,1,0:T(8,128)(2,1)S(1)} %copy-done.34), channel_id=1, source_target_pairs={{0,2},{2,0},{1,3},{3,1},{4,6},{6,4},{5,7},{7,5},{8,10},{10,8},{9,1... | collective-permute-start | bytes 6291464 | tf_op jit(solution)/shard_map/ppermute | solution.py:72
  1093.9 41.3 %collective-permute-start.68 = (bf16[1024,512]{1,0:T(8,128)(2,1)S(1)}, bf16[1024,512]{1,0:T(8,128)(2,1)S(1)}, u32[]{:S(2)}, u32[]{:S(2)}) collective-permute-start(bf16[1024,512]{1,0:T(8,128)(2,1)S(1)} %dynamic-slice_bitcast_fusion.5), channel_id=1, source_target_pairs={{0,4},{4,0},{1,5},{5,1},{2,6},{6,2},{3,7},{7,3},{8,12},{12,8},{9,1... | collective-permute-start | bytes 3145736 | tf_op jit(solution)/shard_map/ppermute | solution.py:72
  1236.6 47.5 %collective-permute-start.45 = (bf16[2,4,256,512]{3,2,1,0:T(8,128)(2,1)S(1)}, bf16[2,4,256,512]{3,2,1,0:T(8,128)(2,1)S(1)}, u32[]{:S(2)}, u32[]{:S(2)}) collective-permute-start(bf16[2,4,256,512]{3,2,1,0:T(8,128)(2,1)S(1)} %copy-done.32), channel_id=1, source_target_pairs={{0,2},{2,0},{1,3},{3,1},{4,6},{6,4},{5,7},{7,5},{8,10},{10,8},{9,1... | collective-permute-start | bytes 6291464 | tf_op jit(solution)/shard_map/ppermute | solution.py:72
  1256.2 28.5 %collective-permute-start.61 = (bf16[512,2048]{1,0:T(8,128)(2,1)}, bf16[512,2048]{1,0:T(8,128)(2,1)S(1)}, u32[]{:S(2)}, u32[]{:S(2)}) collective-permute-start(bf16[512,2048]{1,0:T(8,128)(2,1)} %dynamic-slice_bitcast_fusion), channel_id=1, source_target_pairs={{0,1},{1,0},{2,3},{3,2},{4,5},{5,4},{6,7},{7,6},{8,9},{9,8},{10,11... | collective-permute-start | bytes 6291464 | tf_op jit(solution)/shard_map/ppermute | solution.py:72
  1256.3 30.9 %collective-permute-start.84 = (bf16[512,512]{1,0:T(8,128)(2,1)S(1)}, bf16[512,512]{1,0:T(8,128)(2,1)S(1)}, u32[]{:S(2)}, u32[]{:S(2)}) collective-permute-start(bf16[512,512]{1,0:T(8,128)(2,1)S(1)} %pad_maximum_fusion.12), channel_id=1, source_target_pairs={{0,8},{8,0},{1,9},{9,1},{2,10},{10,2},{3,11},{11,3},{4,12},{12,4},... | collective-permute-start | bytes 1572872 | tf_op jit(solution)/shard_map/ppermute | solution.py:72
  1258.8 29.3 %collective-permute-start.78 = (bf16[512,512]{1,0:T(8,128)(2,1)S(1)}, bf16[512,512]{1,0:T(8,128)(2,1)S(1)}, u32[]{:S(2)}, u32[]{:S(2)}) collective-permute-start(bf16[512,512]{1,0:T(8,128)(2,1)S(1)} %pad_maximum_fusion.11), channel_id=1, source_target_pairs={{0,8},{8,0},{1,9},{9,1},{2,10},{10,2},{3,11},{11,3},{4,12},{12,4},... | collective-permute-start | bytes 1572872 | tf_op jit(solution)/shard_map/ppermute | solution.py:72
  1263.2 30.4 %collective-permute-start.72 = (bf16[512,512]{1,0:T(8,128)(2,1)S(1)}, bf16[512,512]{1,0:T(8,128)(2,1)S(1)}, u32[]{:S(2)}, u32[]{:S(2)}) collective-permute-start(bf16[512,512]{1,0:T(8,128)(2,1)S(1)} %pad_maximum_fusion.10), channel_id=1, source_target_pairs={{0,8},{8,0},{1,9},{9,1},{2,10},{10,2},{3,11},{11,3},{4,12},{12,4},... | collective-permute-start | bytes 1572872 | tf_op jit(solution)/shard_map/ppermute | solution.py:72
  1284.7 37.8 %collective-permute-start.58 = (bf16[4,256,512]{2,1,0:T(8,128)(2,1)S(1)}, bf16[4,256,512]{2,1,0:T(8,128)(2,1)S(1)}, u32[]{:S(2)}, u32[]{:S(2)}) collective-permute-start(bf16[4,256,512]{2,1,0:T(8,128)(2,1)S(1)} %slice_bitcast_fusion), channel_id=1, source_target_pairs={{0,4},{4,0},{1,5},{5,1},{2,6},{6,2},{3,7},{7,3},{8,12},{12,8},{9,1... | collective-permute-start | bytes 3145736 | tf_op jit(solution)/shard_map/ppermute | solution.py:72
  1287.3 46.1 %collective-permute-start.54 = (bf16[4,256,512]{2,1,0:T(8,128)(2,1)S(1)}, bf16[4,256,512]{2,1,0:T(8,128)(2,1)S(1)}, u32[]{:S(2)}, u32[]{:S(2)}) collective-permute-start(bf16[4,256,512]{2,1,0:T(8,128)(2,1)S(1)} %slice_bitcast_fusion.2), channel_id=1, source_target_pairs={{0,4},{4,0},{1,5},{5,1},{2,6},{6,2},{3,7},{7,3},{8,12},{12,8},{9,1... | collective-permute-start | bytes 3145736 | tf_op jit(solution)/shard_map/ppermute | solution.py:72
  1288.1 135.0 %collective-permute-start.50 = (bf16[4,256,512]{2,1,0:T(8,128)(2,1)S(1)}, bf16[4,256,512]{2,1,0:T(8,128)(2,1)S(1)}, u32[]{:S(2)}, u32[]{:S(2)}) collective-permute-start(bf16[4,256,512]{2,1,0:T(8,128)(2,1)S(1)} %slice_bitcast_fusion.4), channel_id=1, source_target_pairs={{0,4},{4,0},{1,5},{5,1},{2,6},{6,2},{3,7},{7,3},{8,12},{12,8},{9,1... | collective-permute-start | bytes 3145736 | tf_op jit(solution)/shard_map/ppermute | solution.py:72
  1304.4 123.0 %collective-permute-start.46 = (bf16[4,256,512]{2,1,0:T(8,128)(2,1)S(1)}, bf16[4,256,512]{2,1,0:T(8,128)(2,1)S(1)}, u32[]{:S(2)}, u32[]{:S(2)}) collective-permute-start(bf16[4,256,512]{2,1,0:T(8,128)(2,1)S(1)} %slice_bitcast_fusion.6), channel_id=1, source_target_pairs={{0,4},{4,0},{1,5},{5,1},{2,6},{6,2},{3,7},{7,3},{8,12},{12,8},{9,1... | collective-permute-start | bytes 3145736 | tf_op jit(solution)/shard_map/ppermute | solution.py:72
  1321.1 113.7 %collective-permute-start.85 = (bf16[1024,512]{1,0:T(8,128)(2,1)S(1)}, bf16[1024,512]{1,0:T(8,128)(2,1)S(1)}, u32[]{:S(2)}, u32[]{:S(2)}) collective-permute-start(bf16[1024,512]{1,0:T(8,128)(2,1)S(1)} %pad_maximum_fusion.6), channel_id=1, source_target_pairs={{0,4},{4,0},{1,5},{5,1},{2,6},{6,2},{3,7},{7,3},{8,12},{12,8},{9,1... | collective-permute-start | bytes 3145736 | tf_op jit(solution)/shard_map/ppermute | solution.py:72
  1326.4 109.0 %collective-permute-start.79 = (bf16[1024,512]{1,0:T(8,128)(2,1)S(1)}, bf16[1024,512]{1,0:T(8,128)(2,1)S(1)}, u32[]{:S(2)}, u32[]{:S(2)}) collective-permute-start(bf16[1024,512]{1,0:T(8,128)(2,1)S(1)} %pad_maximum_fusion.5), channel_id=1, source_target_pairs={{0,4},{4,0},{1,5},{5,1},{2,6},{6,2},{3,7},{7,3},{8,12},{12,8},{9,1... | collective-permute-start | bytes 3145736 | tf_op jit(solution)/shard_map/ppermute | solution.py:72
  1333.3 88.3 %collective-permute-start.65 = (f32[2,2048]{1,0:T(2,128)S(1)}, f32[2,2048]{1,0:T(2,128)S(1)}, u32[]{:S(2)}, u32[]{:S(2)}) collective-permute-start(f32[2,2048]{1,0:T(2,128)S(1)} %fusion.86), channel_id=1, source_target_pairs={{0,4},{4,0},{1,5},{5,1},{2,6},{6,2},{3,7},{7,3},{8,12},{12,8},{9,1... | collective-permute-start | bytes 49160 | tf_op jit(solution)/shard_map/ppermute | solution.py:72
  1426.9 40.4 %collective-permute-start.94 = (bf16[256,2048]{1,0:T(8,128)(2,1)S(1)}, bf16[256,2048]{1,0:T(8,128)(2,1)S(1)}, u32[]{:S(2)}, u32[]{:S(2)}) collective-permute-start(bf16[256,2048]{1,0:T(8,128)(2,1)S(1)} %pad_maximum_fusion.7), channel_id=1, source_target_pairs={{0,4},{4,0},{1,5},{5,1},{2,6},{6,2},{3,7},{7,3},{8,12},{12,8},{9,1... | collective-permute-start | bytes 3145736 | tf_op jit(solution)/shard_map/ppermute | solution.py:72
  1432.3 38.1 %collective-permute-start.59 = (bf16[2,256,512]{2,1,0:T(8,128)(2,1)S(1)}, bf16[2,256,512]{2,1,0:T(8,128)(2,1)S(1)}, u32[]{:S(2)}, u32[]{:S(2)}) collective-permute-start(bf16[2,256,512]{2,1,0:T(8,128)(2,1)S(1)} %slice.352), channel_id=1, source_target_pairs={{0,8},{8,0},{1,9},{9,1},{2,10},{10,2},{3,11},{11,3},{4,12},{12,4},... | collective-permute-start | bytes 1572872 | tf_op jit(solution)/shard_map/ppermute | solution.py:72
  1434.8 37.8 %collective-permute-start.55 = (bf16[2,256,512]{2,1,0:T(8,128)(2,1)S(1)}, bf16[2,256,512]{2,1,0:T(8,128)(2,1)S(1)}, u32[]{:S(2)}, u32[]{:S(2)}) collective-permute-start(bf16[2,256,512]{2,1,0:T(8,128)(2,1)S(1)} %slice.346), channel_id=1, source_target_pairs={{0,8},{8,0},{1,9},{9,1},{2,10},{10,2},{3,11},{11,3},{4,12},{12,4},... | collective-permute-start | bytes 1572872 | tf_op jit(solution)/shard_map/ppermute | solution.py:72
  1435.4 38.4 %collective-permute-start.51 = (bf16[2,256,512]{2,1,0:T(8,128)(2,1)S(1)}, bf16[2,256,512]{2,1,0:T(8,128)(2,1)S(1)}, u32[]{:S(2)}, u32[]{:S(2)}) collective-permute-start(bf16[2,256,512]{2,1,0:T(8,128)(2,1)S(1)} %slice.340), channel_id=1, source_target_pairs={{0,8},{8,0},{1,9},{9,1},{2,10},{10,2},{3,11},{11,3},{4,12},{12,4},... | collective-permute-start | bytes 1572872 | tf_op jit(solution)/shard_map/ppermute | solution.py:72
  1447.7 32.0 %collective-permute-start.47 = (bf16[2,256,512]{2,1,0:T(8,128)(2,1)S(1)}, bf16[2,256,512]{2,1,0:T(8,128)(2,1)S(1)}, u32[]{:S(2)}, u32[]{:S(2)}) collective-permute-start(bf16[2,256,512]{2,1,0:T(8,128)(2,1)S(1)} %slice.334), channel_id=1, source_target_pairs={{0,8},{8,0},{1,9},{9,1},{2,10},{10,2},{3,11},{11,3},{4,12},{12,4},... | collective-permute-start | bytes 1572872 | tf_op jit(solution)/shard_map/ppermute | solution.py:72
  1470.5 31.1 %collective-permute-start.60 = (bf16[1,256,512]{2,1,0:T(8,128)(2,1)S(1)}, bf16[1,256,512]{2,1,0:T(8,128)(2,1)S(1)}, u32[]{:S(2)}, u32[]{:S(2)}) collective-permute-start(bf16[1,256,512]{2,1,0:T(8,128)(2,1)S(1)} %slice.354), channel_id=1, source_target_pairs={{0,16},{16,0},{1,17},{17,1},{2,18},{18,2},{3,19},{19,3},{4,20},{20... | collective-permute-start | bytes 786440 | tf_op jit(solution)/shard_map/ppermute | solution.py:72
  1472.8 34.5 %collective-permute-start.56 = (bf16[1,256,512]{2,1,0:T(8,128)(2,1)S(1)}, bf16[1,256,512]{2,1,0:T(8,128)(2,1)S(1)}, u32[]{:S(2)}, u32[]{:S(2)}) collective-permute-start(bf16[1,256,512]{2,1,0:T(8,128)(2,1)S(1)} %slice.348), channel_id=1, source_target_pairs={{0,16},{16,0},{1,17},{17,1},{2,18},{18,2},{3,19},{19,3},{4,20},{20... | collective-permute-start | bytes 786440 | tf_op jit(solution)/shard_map/ppermute | solution.py:72
  1473.9 39.0 %collective-permute-start.52 = (bf16[1,256,512]{2,1,0:T(8,128)(2,1)S(1)}, bf16[1,256,512]{2,1,0:T(8,128)(2,1)S(1)}, u32[]{:S(2)}, u32[]{:S(2)}) collective-permute-start(bf16[1,256,512]{2,1,0:T(8,128)(2,1)S(1)} %slice.342), channel_id=1, source_target_pairs={{0,16},{16,0},{1,17},{17,1},{2,18},{18,2},{3,19},{19,3},{4,20},{20... | collective-permute-start | bytes 786440 | tf_op jit(solution)/shard_map/ppermute | solution.py:72
  1479.9 36.3 %collective-permute-start.48 = (bf16[1,256,512]{2,1,0:T(8,128)(2,1)S(1)}, bf16[1,256,512]{2,1,0:T(8,128)(2,1)S(1)}, u32[]{:S(2)}, u32[]{:S(2)}) collective-permute-start(bf16[1,256,512]{2,1,0:T(8,128)(2,1)S(1)} %slice.336), channel_id=1, source_target_pairs={{0,16},{16,0},{1,17},{17,1},{2,18},{18,2},{3,19},{19,3},{4,20},{20... | collective-permute-start | bytes 786440 | tf_op jit(solution)/shard_map/ppermute | solution.py:72
  (143 other events, 2090.7 us)
Sparse Core Ops, SparseCore 0:
  11.5 212.8 all-gather.2
  227.2 196.7 all-gather.4
  873.9 126.5 all-reduce.1

commit v3 on v2

--- a/solution.py
+++ b/solution.py
@@ -11,6 +11,7 @@
 HEAD_DIM = 128
 LOW = jnp.bfloat16
 WIDE = jnp.float32
+EST = 100
 
 
 EPSILON = 1e-05
@@ -96,31 +97,81 @@
     return total.reshape((2, total.shape[0] // 2) + total.shape[1:])
 
 
-def scatter(total, axes):
-    for axis in axes:
+class Transfers:
+    def __init__(self, steps, zero=None):
+        self.steps = steps
+        self.result = None
+        self.sent, axis = next(steps)
+        if zero is not None:
+            self.sent = later(self.sent, zero)
+        self.moving = swap(self.sent, axis)
+
+    def advance(self, zero=None):
+        if self.result is not None:
+            return
+        try:
+            arrived = self.moving if zero is None else later(self.moving, zero)
+            self.sent, axis = self.steps.send(arrived)
+            self.moving = swap(self.sent, axis)
+        except StopIteration as stop:
+            self.sent = self.result = stop.value
+
+    def finish(self):
+        while self.result is None:
+            self.advance()
+        return self.result
+
+
+def later(values, done):
+    return values + done[0, 0].astype(values.dtype)
+
+
+def advance(transfers, done):
+    sent = [done]
+    for one in transfers:
+        one.advance(done)
+        sent.append(one.sent)
+    return tuple(sent)
+
+
+def scattering(own, rest, axes):
+    total = add_low(own, (yield rest, axes[0]))
+    total = total.reshape((-1,) + total.shape[2:])
+    for axis in axes[1:]:
         parts = halves(total)
-        total = add_low(parts[0], swap(parts[1], axis))
-    return total
-
-
-def scatter_rows(total, axes):
+        total = add_low(parts[0], (yield parts[1], axis))
+    return total[0]
+
+
+def scattering_rows(total, axes):
     for axis in axes:
         me = lax.axis_index(axis)
         parts = halves(total)
-        total = add_low(pick(parts, me), swap(pick(parts, 1 - me), axis))
+        total = add_low(pick(parts, me), (yield pick(parts, 1 - me), axis))
     return total
 
 
-def gather_rows(values, axes):
+def gathering_rows(values, axes):
     for axis in reversed(axes):
         me = lax.axis_index(axis)
-        other = swap(values, axis)
+        other = yield values, axis
         values = jnp.concatenate(
             [jnp.where(me == 0, values, other), jnp.where(me == 0, other, values)]
         )
     return values
 
 
+def summing(values, axes):
+    own = yield from scattering_rows(values, axes)
+    return (yield from gathering_rows(own, axes))
+
+
+def scattering_tensor(partial, grid):
+    rows, width = partial.shape
+    parts = jnp.swapaxes(partial.reshape(1 << len(grid.x), 2, -1, width), 0, 1)
+    return (yield from scattering_rows(parts.reshape(rows, width), grid.core + grid.x))
+
+
 def gather_relative(values, axes):
     for axis in axes:
         values = jnp.concatenate([values, swap(values, axis)])
@@ -129,25 +180,14 @@
 
 def gather_tensor(values, grid):
     rows, width = values.shape
-    pieces = gather_rows(gather_rows(values, grid.x), grid.core)
+    pieces = Transfers(gathering_rows(values, grid.core + grid.x)).finish()
     return jnp.swapaxes(pieces.reshape(2, -1, rows, width), 0, 1).reshape(-1, width)
 
 
-def scatter_tensor(partial, grid):
-    rows, width = partial.shape
-    parts = jnp.swapaxes(partial.reshape(1 << len(grid.x), 2, -1, width), 0, 1)
-    return scatter_rows(parts.reshape(rows, width), grid.core + grid.x)
-
-
-def sum_over(values, axes):
+def pair_steps(values, axes):
     for axis in axes:
-        values = values + swap(values, axis)
+        values = values + (yield values, axis)
     return values
-
-
-def sum_expert(values, grid):
-    axes = grid.y + grid.z[::-1]
-    return gather_rows(scatter_rows(values, axes), axes).astype(WIDE)
 
 
 NT = (((1,), (1,)), ((), ()))
@@ -165,7 +205,7 @@
 
 
 def cost(flops, moved):
-    return pl.CostEstimate(flops=int(2 * flops), bytes_accessed=int(2 * moved), transcendentals=0)
+    return pl.CostEstimate(flops=int(flops / EST), bytes_accessed=int(moved / EST), transcendentals=0)
 
 
 def dispatch_kernel(order_ref, select_ref, rows_ref, out_ref):
@@ -227,7 +267,8 @@
     rows = rows_ref[0]
     gate_pre = dot(rows, up_ref[0, 0])
     upper = dot(rows, up_ref[0, 1])
-    gate = gate_ref[0]
+    tile = rows.shape[0]
+    gate = jnp.broadcast_to(gate_ref[0], (128, tile)).T[:, :1]
     sigma = jax.nn.sigmoid(gate_pre)
     silu = gate_pre * sigma
     active = silu * upper
@@ -236,7 +277,8 @@
     act_ref[0] = (gate * active).astype(LOW)
     pair_ref[0, 0] = (gated * upper * (sigma * (1.0 + gate_pre * (1.0 - sigma)))).astype(LOW)
     pair_ref[0, 1] = (gated * silu).astype(LOW)
-    gate_grad_ref[0] = jnp.sum(active * grad, axis=-1, keepdims=True)
+    gate_grad = jnp.sum(active * grad, axis=-1, keepdims=True)
+    gate_grad_ref[0] = jnp.broadcast_to(gate_grad, (tile, 128)).T[:1]
 
 
 def hidden_units(rows, expert_up, grads, gates):
@@ -250,17 +292,17 @@
             pl.BlockSpec((1, tile, width), lambda e, r: (e, r, 0)),
             pl.BlockSpec((1, 2, width, units), lambda e, r: (e, 0, 0, 0)),
             pl.BlockSpec((1, tile, units), lambda e, r: (e, r, 0)),
-            pl.BlockSpec((1, tile, 1), lambda e, r: (e, r, 0)),
+            pl.BlockSpec((1, 1, tile), lambda e, r: (e, 0, r)),
         ],
         out_specs=[
             pl.BlockSpec((1, tile, units), lambda e, r: (e, r, 0)),
             pl.BlockSpec((1, 2, tile, units), lambda e, r: (e, 0, r, 0)),
-            pl.BlockSpec((1, tile, 1), lambda e, r: (e, r, 0)),
+            pl.BlockSpec((1, 1, tile), lambda e, r: (e, 0, r)),
         ],
         out_shape=[
             jax.ShapeDtypeStruct((experts, count, units), LOW),
             jax.ShapeDtypeStruct((experts, 2, count, units), LOW),
-            jax.ShapeDtypeStruct((experts, count, 1), WIDE),
+            jax.ShapeDtypeStruct((experts, 1, count), WIDE),
         ],
         compiler_params=params(40),
         cost_estimate=cost(4 * rows.size * units, 2 * rows.size),
@@ -268,11 +310,15 @@
     )(rows, expert_up, grads, gates)
 
 
-def combine_kernel(transposed, experts, adds, group_of, *refs):
+def combine_kernel(transposed, experts, adds, extra, group_of, groups, *refs):
     lhs_ref, weight_ref, select_ref = refs[:3]
-    received = refs[3] if adds else None
-    outs, rows = refs[3 + adds : -1], refs[-1]
+    refs = refs[3:]
+    if extra:
+        gate_ref, first_ref, refs = refs[0], refs[1], refs[2:]
+    received, refs = (refs[:groups], refs[groups:]) if adds else ((None,) * groups, refs)
+    outs, done_ref, rows = refs[:-2], refs[-2], refs[-1]
     step = pl.program_id(0)
+    done_ref[...] = jnp.zeros_like(done_ref)
     blocks, slots, columns = rows.shape
     capacity = slots // experts
     group = select_ref.shape[0]
@@ -288,30 +334,37 @@
             for i in range(pairs):
                 term = dot(lhs_ref[0, i, piece, :], weight_ref[0, i], NT if transposed else None)
                 total = term if total is None else total + term
-            rows[first : first + many, pl.ds(start, capacity), :] = total.astype(LOW).reshape(
-                many, capacity, columns
-            )
+            shape = (many, capacity, total.shape[-1])
+            if extra:
+                gates = jnp.broadcast_to(gate_ref[0, :, piece], (128, many * capacity)).T
+                lane = lax.broadcasted_iota(jnp.int32, gates.shape, 1)
+                gates = jnp.where(lane == first_ref[0] + step, gates, 0.0)
+                rows[first : first + many, pl.ds(start, capacity), shape[-1] :] = gates.astype(
+                    LOW
+                ).reshape(many, capacity, 128)
+            rows[first : first + many, pl.ds(start, capacity), : shape[-1]] = total.astype(
+                LOW
+            ).reshape(shape)
 
     @pl.when(step >= experts)
     def _():
         at = group_of(step) * group
 
-        def put(ref):
+        def put(out, more):
             for i in range(group):
                 total = dot(select_ref[i], rows[at + i])
                 if adds:
-                    total = total + received[0, i].astype(WIDE)
-                ref[0, i] = total.astype(LOW)
-
-        if adds:
-            half = blocks // group // 2
-            pl.when(step - experts < half)(lambda: put(outs[0]))
-            pl.when(step - experts >= half)(lambda: put(outs[1]))
-        else:
-            put(outs[0])
-
-
-def combine(lhs, weight, select, received, at, columns, transposed, sizes, flip, after=()):
+                    total = total + more[0, i].astype(WIDE)
+                out[0, i] = total.astype(LOW)
+
+        each = groups // len(outs)
+        for place in range(groups):
+            pl.when(step - experts == place)(
+                functools.partial(put, outs[place // each], received[place])
+            )
+
+
+def combine(lhs, weight, select, received, at, columns, transposed, sizes, flip, after=(), gates=None):
     experts, pairs, count, units = lhs.shape
     blocks, tokens, slots = select.shape
     nx, ny, nz = sizes
@@ -338,36 +391,37 @@
         pl.BlockSpec((nz, tokens, slots), lambda s: (part * groups + group_of(s), 0, 0)),
     ]
     operands = [lhs, weight, select]
+    if gates is not None:
+        in_specs += [
+            pl.BlockSpec((1, 1, count), lambda s: (expert_of(s), 0, part)),
+            pl.BlockSpec(memory_space=pltpu.SMEM),
+        ]
+        operands += gates
+        columns += 128
     if adds:
-        in_specs.append(
-            pl.BlockSpec((1, nz, tokens, columns), lambda s: (jnp.clip(s - experts, 0, groups - 1), 0, 0, 0))
-        )
-        operands.append(received)
-        half = groups // 2
-        out_specs = [
-            pl.BlockSpec(
-                (1, nz, tokens, columns), lambda s: (jnp.clip(s - experts, 0, half - 1), 0, 0, 0)
-            ),
-            pl.BlockSpec(
-                (1, nz, tokens, columns), lambda s: (jnp.clip(s - experts - half, 0, half - 1), 0, 0, 0)
-            ),
-        ]
-        out_shape = [jax.ShapeDtypeStruct((half, nz, tokens, columns), LOW)] * 2
+        in_specs += [pl.BlockSpec((1, nz, tokens, columns), lambda s: (0, 0, 0, 0))] * groups
+        operands += received
+        outs, half = 2, groups // 2
+        place_of = lambda o, s: jnp.clip(s - experts - o * half, 0, half - 1)
     else:
-        out_specs = [
-            pl.BlockSpec(
-                (1, nz, tokens, columns), lambda s: (jnp.clip(s - experts, 0, groups - 1), 0, 0, 0)
-            )
-        ]
-        out_shape = [jax.ShapeDtypeStruct((groups, nz, tokens, columns), LOW)]
+        outs, half = groups, 1
+        place_of = lambda o, s: 0
+    out_specs = [
+        pl.BlockSpec((1, nz, tokens, columns), functools.partial(lambda o, s: (place_of(o, s), 0, 0, 0), o))
+        for o in range(outs)
+    ]
+    kernel = functools.partial(
+        combine_kernel, transposed, experts, adds, gates is not None, group_of, groups
+    )
     return pl.pallas_call(
-        without(len(operands), len(after), functools.partial(combine_kernel, transposed, experts, adds, group_of)),
+        without(len(operands), len(after), kernel),
         grid=(experts + groups,),
         in_specs=in_specs + [pl.BlockSpec(memory_space=pl.ANY)] * len(after),
-        out_specs=out_specs,
-        out_shape=out_shape,
+        out_specs=out_specs + [pl.BlockSpec((8, 128), lambda s: (0, 0))],
+        out_shape=[jax.ShapeDtypeStruct((half, nz, tokens, columns), LOW)] * outs
+        + [jax.ShapeDtypeStruct((8, 128), WIDE)],
         scratch_shapes=[pltpu.VMEM((blocks, slots, columns), LOW)],
-        compiler_params=params(48),
+        compiler_params=params(56),
         cost_estimate=cost(
             2 * lhs.size * columns + 2 * select.size * columns,
             2 * lhs.size + 2 * select.size + (12 if adds else 4) * blocks * tokens * columns,
@@ -466,12 +520,14 @@
     grad_ref,
     out_refs,
     gain_grad_ref,
+    done_ref,
     query_grad,
     key_grad,
     value_grad,
 ):
     length = pre_ref.shape[1]
     scale = HEAD_DIM ** (-0.5)
+    done_ref[...] = jnp.zeros_like(done_ref)
     keys_turned = low_ref[1].T
     for start in reversed(range(0, length, tile)):
         end = start + tile
@@ -527,10 +583,12 @@
         out_specs=[
             pl.BlockSpec((3, length, HEAD_DIM), head),
             pl.BlockSpec((2, 1, HEAD_DIM), head),
+            pl.BlockSpec((8, 128), whole),
         ],
         out_shape=[
             jax.ShapeDtypeStruct(projected.shape, LOW),
             jax.ShapeDtypeStruct((2, 1, width), WIDE),
+            jax.ShapeDtypeStruct((8, 128), WIDE),
         ],
         scratch_shapes=[pltpu.VMEM((length, HEAD_DIM), WIDE)] * 3,
         compiler_params=params(48),
@@ -539,8 +597,9 @@
     )(projected, gains[:, None, :], cosine, sine, first, low, lse, grads, *after)
 
 
-def weight_grad_kernel(left_ref, right_ref, out_ref):
+def weight_grad_kernel(left_ref, right_ref, out_ref, done_ref):
     out_ref[0, 0] = dot(left_ref[0, 0], right_ref[0, 0], TN)
+    done_ref[...] = jnp.zeros_like(done_ref)
 
 
 def weight_grad(left, right, tile_left, tile_right, first, last, into=None, after=()):
@@ -563,10 +622,14 @@
             pl.BlockSpec((1, 1, count, tile_right), right_map),
         ]
         + [pl.BlockSpec(memory_space=pl.ANY)] * len(rest),
-        out_specs=pl.BlockSpec(
-            (1, 1, tile_left, tile_right), lambda e, i, j, p: (e + first, p, i, j)
-        ),
-        out_shape=jax.ShapeDtypeStruct((experts, pairs, left_width, right_width), WIDE),
+        out_specs=[
+            pl.BlockSpec((1, 1, tile_left, tile_right), lambda e, i, j, p: (e + first, p, i, j)),
+            pl.BlockSpec((8, 128), lambda e, i, j, p: (0, 0)),
+        ],
+        out_shape=[
+            jax.ShapeDtypeStruct((experts, pairs, left_width, right_width), WIDE),
+            jax.ShapeDtypeStruct((8, 128), WIDE),
+        ],
         input_output_aliases={} if into is None else {2: 0},
         compiler_params=params(48),
         cost_estimate=cost(
@@ -630,9 +693,8 @@
     cosine, sine = rope_tables(jnp.arange(length, dtype=jnp.int32) - first_key, HEAD_DIM // 2)
     first_key = first_key[None]
     heads_low, mixed, lse = attention(projected, qk_gain, cosine, sine, first_key)
-    attended = hidden + scatter_tensor(
-        jnp.dot(mixed, out_weight, preferred_element_type=WIDE).astype(LOW), grid
-    ).astype(WIDE)
+    partial = jnp.dot(mixed, out_weight, preferred_element_type=WIDE).astype(LOW)
+    attended = hidden + Transfers(scattering_tensor(partial, grid)).finish().astype(WIDE)
     moe_normed, inverse_moe = normalize(attended, moe_gain)
     routed_low = moe_normed.astype(LOW)
     routed_low, cotangent_all = lax.optimization_barrier((routed_low, cotangent_all))
@@ -657,103 +719,82 @@
     slot_gates = jnp.sum(
         jnp.where(chosen, own_probs[:, :, None, :], 0.0), axis=-1
     )
-    slot_gates = jnp.swapaxes(slot_gates, 0, 1).reshape(local_experts, blocks * capacity, 1)
+    slot_gates = jnp.swapaxes(slot_gates, 0, 1).reshape(local_experts, 1, blocks * capacity)
     row_slots = dispatch(order, select, routed_all, local_experts)
     gated_act, grad_pair, gate_grads = hidden_units(row_slots, expert_up, grad_units, slot_gates)
 
-    gate_grads = jnp.swapaxes(gate_grads.reshape(local_experts, blocks, capacity), 0, 1)
-    own_grads = jnp.sum(jnp.where(chosen, gate_grads[:, :, :, None], 0.0), axis=2)
     sizes = (nx, ny, nz)
     chunk = 512
     act, down_weight = gated_act[:, None], expert_down[:, None]
     units = expert_up.shape[-1]
 
-    def to_other(lhs, weight, transposed, at, flip, after):
-        (other,) = combine(
-            lhs, weight, select_back, None, at, chunk, transposed, sizes, flip, after
+    def to_other(lhs, weight, transposed, at, flip, after, gates=None):
+        parts = combine(
+            lhs, weight, select_back, None, at, chunk, transposed, sizes, flip, after, gates
         )
-        return other, swap(other, "core")
-
-    def to_own(lhs, weight, transposed, at, flip, received, after):
+        return parts[-1], [swap(part, "core") for part in parts[:-1]]
+
+    def to_own(lhs, weight, transposed, at, flip, received, after, gates=None):
         return combine(
-            lhs, weight, select_back, received, at, chunk, transposed, sizes, flip, after
-        )
-
-    def step(total, axis):
-        parts = halves(total)
-        return add_low(parts[0], swap(parts[1], axis))
-
-    def first(own, rest, axis):
-        total = add_low(own, swap(rest, axis))
-        return total.reshape((-1,) + total.shape[2:])
-
-    def gather_experts(values, axis):
-        parts = halves(values)
-        other = swap(parts[1], axis)
-        me = lax.axis_index(axis)
-        return jnp.concatenate(
-            [jnp.where(me == 0, parts[0], other), jnp.where(me == 0, other, parts[0])], axis=1
+            lhs, weight, select_back, received, at, chunk, transposed, sizes, flip, after, gates
         )
 
     orders = (order_x, order_y, order_x, order_y)
     grads = (grad_pair, expert_up, True)
     outs = (act, down_weight, False)
-    other, sent, own, total = [None] * 4, [None] * 4, [None] * 4, [None] * 4
-    small = own_grads
-    small_steps = [functools.partial(lambda axis, v: step(v, axis), axis) for axis in grid.core + grid.x[::-1]]
-    small_steps += [
-        functools.partial(lambda axis, v: gather_experts(v, axis), axis) for axis in order_x[len(grid.x) :]
-    ]
-    before = ()
-    for name, i in (
-        ("other", 0),
-        ("other", 1),
-        ("own", 0),
-        ("own", 1),
-        ("other", 2),
-        ("other", 3),
-        ("own", 2),
-    ):
-        if name == "other":
-            other[i], sent[i] = to_other(*grads, i, i % 2 == 1, before)
-            before = (other[i],)
-        else:
-            own[i] = to_own(*grads, i, i % 2 == 1, sent[i], before)
-            before = (own[i][0],)
-        if small_steps:
-            small = small_steps.pop(0)(tie(small, before[0]))
-            before += (small,)
-    for run in small_steps:
-        small = run(small)
-    grad_probs = small[0].T
-    for i in (0, 1):
-        total[i] = first(*own[i], orders[i][0])
-    own[3] = to_own(*grads, 3, True, sent[3], before + (total[0], total[1]))
-    o_other, o_sent, o_own = [None] * 4, [None] * 4, [None] * 4
-    o_other[0], o_sent[0] = to_other(*outs, 0, False, (own[3][0],))
-    for i in (0, 1):
-        total[i] = step(total[i], orders[i][1])
-    o_other[1], o_sent[1] = to_other(*outs, 1, False, (o_other[0], total[0], total[1]))
-    o_own[0] = to_own(*outs, 0, False, o_sent[0], (o_other[1],))
-    for i in (0, 1):
-        total[i] = step(total[i], orders[i][2])
-    for i in (2, 3):
-        total[i] = first(*own[i], orders[i][0])
-    o_other[2], o_sent[2] = to_other(*outs, 2, False, (o_own[0][0],) + tuple(total))
-    o_own[1] = to_own(*outs, 1, False, o_sent[1], (o_other[2],))
-    for i in (0, 1):
-        total[i] = step(total[i], orders[i][3])
-    for i in (2, 3):
-        total[i] = step(total[i], orders[i][1])
-    o_other[3], o_sent[3] = to_other(*outs, 3, False, (o_own[1][0],) + tuple(total))
-    for i in (2, 3):
-        total[i] = step(total[i], orders[i][2])
-    o_own[2] = to_own(*outs, 2, False, o_sent[2], (o_other[3], total[2], total[3]))
-    for i in (2, 3):
-        total[i] = step(total[i], orders[i][3])
-    for i in range(4):
-        total[i] = scatter(total[i], orders[i][4:])[0]
-    rows_back = jnp.concatenate(total, axis=-1).astype(WIDE)
+    extra = [[gate_grads, (expert_index * local_experts)[None]], None, None, None]
+    other, sent, own, rows = [None] * 4, [None] * 4, [None] * 4, [None] * 4
+
+    def grad_other(i, before):
+        done, sent[i] = to_other(*grads, i, i % 2 == 1, before, extra[i])
+        return done
+
+    def grad_own(i, before):
+        *own, done = to_own(*grads, i, i % 2 == 1, sent[i], before, extra[i])
+        rows[i] = Transfers(scattering(*own, orders[i]))
+        return done
+
+    o_sent, o_own, outputs = [None] * 4, [None] * 4, [None] * 4
+    o_orders = (order_x, order_y, order_x, order_x)
+
+    def out_other(i, before):
+        done, o_sent[i] = to_other(*outs, i, i == 1, before)
+        return done
+
+    def out_own(i, before):
+        *o_own[i], done = to_own(*outs, i, i == 1, o_sent[i], before)
+        return done
+
+    def out_start(i, done):
+        outputs[i] = Transfers(scattering(*o_own[i], o_orders[i]), done)
+
+    done = grad_other(0, ())
+    done = grad_other(1, (done,))
+    done = grad_own(0, (done,))
+    done = grad_own(1, (done,))
+    done = grad_other(2, (done,))
+    done = grad_other(3, (done,))
+    now = advance([rows[0]], done)
+    done = grad_own(2, now)
+    now = advance([rows[1]], done)
+    done = grad_own(3, now)
+    now = advance([rows[0]], done)
+    done = out_other(0, now)
+    done = out_other(1, (done,))
+    now = advance([rows[0], rows[2]], done)
+    done = out_own(0, now)
+    now = advance([rows[1], rows[3], rows[0]], done)
+    done = out_own(1, now)
+    out_start(0, done)
+    out_start(1, done)
+    now = advance([rows[2], rows[1]], done)
+    done = out_other(2, now)
+    now = advance([rows[3], rows[1], rows[2]], done)
+    done = out_other(3, now)
+    advance([rows[2], rows[3]], done)
+    advance([rows[3]], done)
+    rows_back = jnp.concatenate([run.finish()[:, :chunk] for run in rows], axis=-1).astype(WIDE)
+    grad_probs = rows[0].result[:, chunk : chunk + all_experts].astype(WIDE)
 
     chose = jnp.any(routes[:, :, None] == jnp.arange(all_experts, dtype=jnp.int32), axis=1)
     grad_probs = jnp.where(chose, grad_probs, 0.0)
@@ -767,46 +808,84 @@
     grad_low = grad_attended.astype(LOW)
     piece = gather_tensor(grad_low, grid)
 
-    o_own[3] = to_own(*outs, 3, False, o_sent[3], (grad_low, o_own[2][0]))
-    piece = tie(piece, o_own[3][0])
-    outputs = []
-    for i in range(4):
-        mine, rest = o_own[i]
-        outputs.append(scatter(first(mine, tie(rest, piece), order_x[0]), order_x[1:])[0])
-    output = attended + jnp.concatenate(outputs, axis=-1).astype(WIDE)
-
+    done = out_own(2, (grad_low,))
+    done = out_own(3, (done,))
+    now = advance([outputs[0], outputs[1]], done)
+    piece = later(piece, done)
+    out_start(2, done)
+    out_start(3, done)
+
+    sum_axes = grid.y + grid.z[::-1]
     grad_mixed = jnp.einsum("td,fd->tf", piece, out_weight, preferred_element_type=WIDE).astype(LOW)
-    out_acc = jnp.einsum(
-        "tf,td->fd", mixed, tie(piece, grad_mixed), preferred_element_type=WIDE
-    ).astype(LOW)
-    out_grad = sum_expert(out_acc, grid)
-    grad_proj, qk_gain_grad = attention_back(
-        projected, qk_gain, cosine, sine, first_key, heads_low, lse, grad_mixed, (out_acc,)
+    out_acc = jnp.einsum("tf,td->fd", mixed, piece, preferred_element_type=WIDE).astype(LOW)
+    out_sum = Transfers(summing(out_acc, sum_axes))
+    grad_proj, qk_gain_grad, done = attention_back(
+        projected, qk_gain, cosine, sine, first_key, heads_low, lse, grad_mixed, (out_acc,) + now
     )
-    qk_gain_grad = qk_gain_grad.reshape(2, -1)
+    qkv_sums = [
+        Transfers(
+            summing(
+                jnp.einsum(
+                    "td,tf->df", normed_all, grad_proj[i], preferred_element_type=WIDE
+                ).astype(LOW),
+                sum_axes,
+            )
+        )
+        for i in (2, 0, 1)
+    ]
     grad_normed = jnp.einsum(
         "ctf,cdf->td", grad_proj, qkv_weight, preferred_element_type=WIDE
     ).astype(LOW)
-    qkv_parts = [
-        jnp.einsum("td,tf->df", normed_all, grad_proj[i], preferred_element_type=WIDE).astype(LOW)
-        for i in range(3)
-    ]
-    down_grad = weight_grad(
-        act, grad_slots[:, None], units, 512, 0, local_experts, None, tuple(qkv_parts) + (grad_normed,)
+    normed_sum = Transfers(scattering_tensor(grad_normed, grid))
+    gain_sum = Transfers(pair_steps(qk_gain_grad.reshape(2, -1), grid.expert))
+    v_sum, q_sum, k_sum = qkv_sums
+    now = (done, grad_normed) + tuple(run.sent for run in qkv_sums)
+    gains = None
+    waves = (
+        (2, 0, [normed_sum, outputs[0], outputs[1], out_sum, v_sum]),
+        (2, 0, [out_sum, v_sum, outputs[0], outputs[1], q_sum, k_sum, outputs[2]]),
+        (2, 0, [normed_sum, out_sum, v_sum, q_sum, k_sum, outputs[0], outputs[1], gain_sum]),
+        (2, 0, [out_sum, v_sum, q_sum, k_sum, outputs[3], outputs[2]]),
+        (0, 4, [out_sum, v_sum, q_sum, k_sum, outputs[2], outputs[3], gain_sum]),
+        (0, 4, [q_sum, k_sum, outputs[2], outputs[3]]),
+        (0, 0, [outputs[3], gain_sum]),
     )
-    up_grad = weight_grad(
-        row_slots[:, None], grad_pair, 512, units, 0, local_experts, None, (down_grad,)
-    )
+
+    def attention_norm_back(done):
+        grad_normed = normed_sum.finish().astype(WIDE)
+        grad_in, attn_gain_grad = norm_back(grad_normed, hidden, inverse_attn, attn_gain)
+        both = jnp.stack([attn_gain_grad, moe_gain_grad])
+        return grad_in + grad_attended, Transfers(pair_steps(both, grid.all[::-1]), done)
+
+    up_left, down_left = list(range(local_experts)), list(range(local_experts))
+    down_grad = up_grad = None
+    for up_count, down_count, wave in waves:
+        now_up, up_left = up_left[:up_count], up_left[up_count:]
+        now_down, down_left = down_left[:down_count], down_left[down_count:]
+        for e in now_up:
+            up_grad, done = weight_grad(
+                row_slots[:, None], grad_pair, 512, units, e, e + 1, up_grad, now
+            )
+            now = (done,)
+        for e in now_down:
+            down_grad, done = weight_grad(
+                act, grad_slots[:, None], units, 512, e, e + 1, down_grad, now
+            )
+            now = (done,)
+        now = advance(wave, done)
+        if normed_sum.result is not None and gains is None:
+            grad_hidden, gains = attention_norm_back(done)
+        elif gains is not None:
+            gains.advance(done)
+    if gains is None:
+        grad_hidden, gains = attention_norm_back(done)
     down_grad = down_grad.reshape(expert_down.shape)
-    qkv_grad = jnp.stack([sum_expert(part, grid) for part in qkv_parts])
-    grad_normed = scatter_tensor(grad_normed, grid).astype(WIDE)
-    grad_hidden, attn_gain_grad = norm_back(grad_normed, hidden, inverse_attn, attn_gain)
-    grad_hidden = grad_hidden + grad_attended
-    qk_gain_grad = sum_over(qk_gain_grad, grid.expert)
+    qkv_grad = jnp.stack([run.finish().astype(WIDE) for run in (q_sum, k_sum, v_sum)])
+    out_grad = out_sum.finish().astype(WIDE)
+    qk_gain_grad = gain_sum.finish()
+    output = attended + jnp.concatenate([run.finish() for run in outputs], axis=-1).astype(WIDE)
     router_grad = lax.psum(router_grad, grid.all)
-    attn_gain_grad, moe_gain_grad = sum_over(
-        jnp.stack([attn_gain_grad, moe_gain_grad]), grid.all[::-1]
-    )
+    attn_gain_grad, moe_gain_grad = gains.finish()
     return (
         output,
         grad_hidden,

time: 1540 us -> 1400 us (0.909)
  waiting for transfers between devices: 676 us -> 417 us
  other arithmetic: 89.1 us -> 165 us
  Pallas kernels: 529 us -> 570 us
    ppermute x95 -> x114, waiting for transfers between devices: 549 us -> 294 us  [swap(): return lax.ppermute(values, axis, [(0, 1), (1, 0)])]
    convert_element_type x40 -> x38, other arithmetic: 22.8 us -> 67.1 us  [add_low(): return total.astype(terms[0].dtype)]
    pallas_call x16, Pallas kernels: 205 us -> 229 us  [combine(): pl.pallas_call(without(len(operands), len(after), kernel), grid=(experts...]
    add x12 -> x16, other arithmetic: 4.45 us -> 21.6 us  [the longest x6 12.1 us: later(): return values + done[0, 0].astype(values.dtype)]
    pallas_call x2 -> x16, Pallas kernels: 126 us -> 143 us  [weight_grad(): pl.pallas_call(without(2, len(rest), weight_grad_kernel), grid=(last - fi...]
    ppermute x95 -> x114, starting transfers between devices: 95.9 us -> 92 us  [swap(): return lax.ppermute(values, axis, [(0, 1), (1, 0)])]
    unnamed x192 -> x374, local copies, waits for them, and re-layouts: 40.2 us -> 37.4 us
  transfers between devices with their start and end apart: 98 -> 117, of which waited for: 57 -> 41; matrix products, arithmetic and copies ran while one was open for 11% -> 18% of each run, Pallas kernels for 26% -> 32%
where the time goes in v3:
time: 1400 us; the launch traced here: 1380 us
  Pallas kernels  570 us (41%)
  waiting for transfers between devices  417 us (30%)
  other arithmetic  165 us (12%)
  starting transfers between devices  92.1 us (7%)
  local copies, waits for them, and re-layouts  80.6 us (6%)
  matrix products  37.5 us (3%)
  between operations  19.6 us (1%)
    ppermute x114, waiting for transfers between devices, swap(): return lax.ppermute(values, axis, [(0, 1), (1, 0)])  294 us
    pallas_call x16, Pallas kernels, combine(): pl.pallas_call(without(len(operands), len(after), kernel), grid=(experts...  229 us
    pallas_call x16, Pallas kernels, weight_grad(): pl.pallas_call(without(2, len(rest), weight_grad_kernel), grid=(last - fi...  143 us
    ppermute x114, starting transfers between devices, swap(): return lax.ppermute(values, axis, [(0, 1), (1, 0)])  92 us
    pallas_call x2, Pallas kernels, dispatch(): pl.pallas_call(dispatch_kernel, grid_spec=pltpu.PrefetchScalarGridSpec(nu...  88.1 us
    all_gather x1, waiting for transfers between devices, shards(): lax.all_gather(cotangent.astype(LOW), grid.all, axis=0, tiled=True)  79.6 us
    convert_element_type x38, other arithmetic, add_low(): return total.astype(terms[0].dtype)  67.1 us
    pallas_call x1, Pallas kernels, hidden_units(): pl.pallas_call(hidden_kernel, grid=(experts, count // tile), in_specs=[pl...  47.9 us
  transfers between devices with their start and end apart: 117, of which 41 were waited for; matrix products, arithmetic and copies ran while one was open for 18% of the time, Pallas kernels for 32%

profile of v3, /device:TPU:0, one launch (start us, length us, event | category | flops | bytes accessed | tf_op | source)
XLA Modules:
  0.0 1381.7 jit_solution(13170801561619642664)
XLA Ops:
  15.7 30.8 %collective-permute-done = bf16[256,2048]{1,0:T(8,128)(2,1)} collective-permute-done((bf16[256,2048]{1,0:T(8,128)(2,1)S(1)}, bf16[256,2048]{1,0:T(8,128)(2,1)}, u32[]{:S(2)}, u32[]{:S(2)}) %collective-permute-start) | collective-permute-done | bytes 1048608 | tf_op jit(solution)/shard_map/ppermute | solution.py:73
  62.8 8.8 convolution_bitcast_fusion.pre_ref.refs_0_
  71.6 14.9 %attention.1 = (bf16[3,1024,512]{2,1,0:T(8,128)(2,1)S(1)}, bf16[1024,512]{1,0:T(8,128)(2,1)S(1)}, f32[4,1,1024]{2,1,0:T(1,128)S(1)}) custom-call(f32[3,1024,512]{2,1,0:T(8,128)} %convolution_bitcast_fusion.pre_ref.refs_0_, f32[2,1,512]{2,1,0:T(1,128)S(1)} %broadcast_in_dim.37.gain_ref.refs_1_, f32[1024,128]{1,0:T(8,128)S(1)} %get-tuple-element.291.cos_ref.refs_2_, ...), custom_call_target="tpu_custom_call" | custom-call | flops 32212254 | bytes 209715 | tf_op jit(solution)/shard_map/attention/pallas_call | solution.py:485
  103.4 36.7 %collective-permute-done.3 = bf16[256,2048]{1,0:T(8,128)(2,1)} collective-permute-done((bf16[256,2048]{1,0:T(8,128)(2,1)S(1)}, bf16[256,2048]{1,0:T(8,128)(2,1)}, u32[]{:S(2)}, u32[]{:S(2)}) %collective-permute-start.3) | collective-permute-done | bytes 1048608 | tf_op jit(solution)/shard_map/ppermute | solution.py:73
  145.3 79.6 %all-gather.3.cloned.1.call-done = bf16[8192,2048]{1,0:T(8,128)(2,1)} async-done(((bf16[256,2048]{1,0:T(8,128)(2,1)}), bf16[8192,2048]{1,0:T(8,128)(2,1)}) %all-gather.3.cloned.1.call-update) | async-done | bytes 33554448 | tf_op jit(solution)/shard_map/all_gather | solution.py:675
  271.1 13.1 copy.64
  284.3 9.0 compare_convert_fusion.refs_2_
  295.0 44.2 %dispatch.3.rows_ref = bf16[8,1536,2048]{2,1,0:T(8,128)(2,1)} custom-call(s32[32]{0:T(128)S(1)} %add.770.order_ref, bf16[32,384,256]{2,1,0:T(8,128)(2,1)S(1)} %fusion.select_ref, bf16[32,256,2048]{2,1,0:T(8,128)(2,1)} %bitcast.357), custom_call_target="tpu_custom_call" | custom-call | flops 128849016 | bytes 838860 | tf_op jit(solution)/shard_map/dispatch/pallas_call | solution.py:221
  341.9 30.5 %grad_active.1.grad_ref = f32[8,1536,256]{2,1,0:T(8,128)S(1)} custom-call(bf16[8,1536,2048]{2,1,0:T(8,128)(2,1)} %dispatch.3.rows_ref, bf16[8,256,2048]{2,1,0:T(8,128)(2,1)S(1)} %bitcast.336), custom_call_target="tpu_custom_call" | custom-call | flops 128849016 | bytes 503316 | tf_op jit(solution)/shard_map/grad_active/pallas_call | solution.py:251
  380.3 42.9 %all-gather.5.cloned.1.call-done = bf16[8192,2048]{1,0:T(8,128)(2,1)} async-done(((bf16[256,2048]{1,0:T(8,128)(2,1)}), bf16[8192,2048]{1,0:T(8,128)(2,1)}) %all-gather.5.cloned.1.call-update) | async-done | bytes 33554448 | tf_op jit(solution)/shard_map/all_gather | solution.py:701
  426.0 43.8 %dispatch.2.rows_ref = bf16[8,1536,2048]{2,1,0:T(8,128)(2,1)} custom-call(s32[32]{0:T(128)S(1)} %add.770.order_ref, bf16[32,384,256]{2,1,0:T(8,128)(2,1)S(1)} %copy-done.4, bf16[32,256,2048]{2,1,0:T(8,128)(2,1)} %bitcast.358), custom_call_target="tpu_custom_call" | custom-call | flops 128849016 | bytes 838860 | tf_op jit(solution)/shard_map/dispatch/pallas_call | solution.py:221
  469.8 47.9 %hidden_units.1 = (bf16[8,1536,256]{2,1,0:T(8,128)(2,1)S(1)}, bf16[8,2,1536,256]{3,2,1,0:T(8,128)(2,1)}, f32[8,1,1536]{2,1,0:T(1,128)S(1)}) custom-call(bf16[8,1536,2048]{2,1,0:T(8,128)(2,1)} %dispatch.2.rows_ref, bf16[8,2,2048,256]{3,2,1,0:T(8,128)(2,1)} %refs_1_.15, f32[8,1536,256]{2,1,0:T(8,128)} %copy-done.5, f32[8,1,1536]{2,1,0:T(1,128)S(1)} %reshape.578.gate_ref), custom_call_target="tpu_custom_call" | custom-call | flops 257698032 | bytes 503316 | tf_op jit(solution)/shard_map/hidden_units/pallas_call | solution.py:288
  521.0 15.6 %combine_other.8 = (bf16[1,4,256,640]{3,2,1,0:T(8,128)(2,1)}, bf16[1,4,256,640]{3,2,1,0:T(8,128)(2,1)}, bf16[1,4,256,640]{3,2,1,0:T(8,128)(2,1)}, bf16[1,4,256,640]{3,2,1,0:T(8,128)(2,1)}, f32[8,128]{1,0:T(8,128)}) custom-call(bf16[8,2,1536,256]{3,2,1,0:T(8,128)(2,1)} %get-tuple-element.121.refs_0_.refs_1_, bf16[8,2,2048,256]{3,2,1,0:T(8,128)(2,1)} %refs_1_.15, ...), custom_call_target="tpu_custom_call" | custom-call | flops 120795952 | bytes 293601 | tf_op jit(solution)/shard_map/combine_other/pallas_call | solution.py:416
  537.7 14.7 %combine_other.9 = (bf16[1,4,256,512]{3,2,1,0:T(8,128)(2,1)}, bf16[1,4,256,512]{3,2,1,0:T(8,128)(2,1)}, bf16[1,4,256,512]{3,2,1,0:T(8,128)(2,1)}, bf16[1,4,256,512]{3,2,1,0:T(8,128)(2,1)}, f32[8,128]{1,0:T(8,128)}) custom-call(bf16[8,2,1536,256]{3,2,1,0:T(8,128)(2,1)} %get-tuple-element.121.refs_0_.refs_1_, bf16[8,2,2048,256]{3,2,1,0:T(8,128)(2,1)} %refs_1_.15, ...), custom_call_target="tpu_custom_call" | custom-call | flops 96636768 | bytes 272629 | tf_op jit(solution)/shard_map/combine_other/pallas_call | solution.py:416
  554.7 16.8 %combine_own.8 = (bf16[2,4,256,640]{3,2,1,0:T(8,128)(2,1)}, bf16[2,4,256,640]{3,2,1,0:T(8,128)(2,1)}, f32[8,128]{1,0:T(8,128)}) custom-call(bf16[8,2,1536,256]{3,2,1,0:T(8,128)(2,1)} %get-tuple-element.121.refs_0_.refs_1_, bf16[8,2,2048,256]{3,2,1,0:T(8,128)(2,1)} %refs_1_.15, bf16[32,256,384]{2,1,0:T(8,128)(2,1)} %compare_convert_fusion.refs_2_, ...), custom_call_target="tpu_custom_call" | custom-call | flops 120795952 | bytes 503316 | tf_op jit(solution)/shard_map/combine_own/pallas_call | solution.py:416
  581.3 15.9 %combine_own.9 = (bf16[2,4,256,512]{3,2,1,0:T(8,128)(2,1)}, bf16[2,4,256,512]{3,2,1,0:T(8,128)(2,1)}, f32[8,128]{1,0:T(8,128)}) custom-call(bf16[8,2,1536,256]{3,2,1,0:T(8,128)(2,1)} %get-tuple-element.121.refs_0_.refs_1_, bf16[8,2,2048,256]{3,2,1,0:T(8,128)(2,1)} %refs_1_.15, bf16[32,256,384]{2,1,0:T(8,128)(2,1)} %compare_convert_fusion.refs_2_, ...), custom_call_target="tpu_custom_call" | custom-call | flops 96636768 | bytes 440401 | tf_op jit(solution)/shard_map/combine_own/pallas_call | solution.py:416
  597.2 14.7 %combine_other.10 = (bf16[1,4,256,512]{3,2,1,0:T(8,128)(2,1)}, bf16[1,4,256,512]{3,2,1,0:T(8,128)(2,1)}, bf16[1,4,256,512]{3,2,1,0:T(8,128)(2,1)}, bf16[1,4,256,512]{3,2,1,0:T(8,128)(2,1)}, f32[8,128]{1,0:T(8,128)}) custom-call(bf16[8,2,1536,256]{3,2,1,0:T(8,128)(2,1)} %get-tuple-element.121.refs_0_.refs_1_, bf16[8,2,2048,256]{3,2,1,0:T(8,128)(2,1)} %refs_1_.15, ...), custom_call_target="tpu_custom_call" | custom-call | flops 96636768 | bytes 272629 | tf_op jit(solution)/shard_map/combine_other/pallas_call | solution.py:416
  612.7 14.8 %combine_other.11 = (bf16[1,4,256,512]{3,2,1,0:T(8,128)(2,1)}, bf16[1,4,256,512]{3,2,1,0:T(8,128)(2,1)}, bf16[1,4,256,512]{3,2,1,0:T(8,128)(2,1)}, bf16[1,4,256,512]{3,2,1,0:T(8,128)(2,1)}, f32[8,128]{1,0:T(8,128)}) custom-call(bf16[8,2,1536,256]{3,2,1,0:T(8,128)(2,1)} %get-tuple-element.121.refs_0_.refs_1_, bf16[8,2,2048,256]{3,2,1,0:T(8,128)(2,1)} %refs_1_.15, ...), custom_call_target="tpu_custom_call" | custom-call | flops 96636768 | bytes 272629 | tf_op jit(solution)/shard_map/combine_other/pallas_call | solution.py:416
  638.6 15.6 %combine_own.10 = (bf16[2,4,256,512]{3,2,1,0:T(8,128)(2,1)}, bf16[2,4,256,512]{3,2,1,0:T(8,128)(2,1)}, f32[8,128]{1,0:T(8,128)}) custom-call(bf16[8,2,1536,256]{3,2,1,0:T(8,128)(2,1)} %get-tuple-element.121.refs_0_.refs_1_, bf16[8,2,2048,256]{3,2,1,0:T(8,128)(2,1)} %refs_1_.15, bf16[32,256,384]{2,1,0:T(8,128)(2,1)} %compare_convert_fusion.refs_2_, ...), custom_call_target="tpu_custom_call" | custom-call | flops 96636768 | bytes 440401 | tf_op jit(solution)/shard_map/combine_own/pallas_call | solution.py:416
  667.2 16.1 %combine_own.11 = (bf16[2,4,256,512]{3,2,1,0:T(8,128)(2,1)}, bf16[2,4,256,512]{3,2,1,0:T(8,128)(2,1)}, f32[8,128]{1,0:T(8,128)}) custom-call(bf16[8,2,1536,256]{3,2,1,0:T(8,128)(2,1)} %get-tuple-element.121.refs_0_.refs_1_, bf16[8,2,2048,256]{3,2,1,0:T(8,128)(2,1)} %refs_1_.15, bf16[32,256,384]{2,1,0:T(8,128)(2,1)} %compare_convert_fusion.refs_2_, ...), custom_call_target="tpu_custom_call" | custom-call | flops 96636768 | bytes 440401 | tf_op jit(solution)/shard_map/combine_own/pallas_call | solution.py:416
  692.1 12.5 combine_other.12
  707.6 12.5 combine_other.13
  728.6 13.7 combine_own.12
  749.0 11.8 collective-permute-done.45
  767.7 13.7 combine_own.13
  789.5 12.5 combine_other.14
  812.4 12.7 combine_other.15
  831.5 9.4 collective-permute-done.62
  854.2 17.0 %collective-permute-done.64 = bf16[256,2048]{1,0:T(8,128)(2,1)} collective-permute-done((bf16[256,2048]{1,0:T(8,128)(2,1)S(1)}, bf16[256,2048]{1,0:T(8,128)(2,1)}, u32[]{:S(2)}, u32[]{:S(2)}) %collective-permute-start.64) | collective-permute-done | bytes 1048608 | tf_op jit(solution)/shard_map/ppermute | solution.py:73
  876.4 13.5 combine_own.14
  890.0 13.7 combine_own.15
  909.2 8.4 collective-permute-done.46
  940.1 16.7 %attention_back.1 = (bf16[3,1024,512]{2,1,0:T(8,128)(2,1)}, f32[2,1,512]{2,1,0:T(1,128)S(1)}, f32[8,128]{1,0:T(8,128)S(1)}) custom-call(f32[3,1024,512]{2,1,0:T(8,128)} %convolution_bitcast_fusion.pre_ref.refs_0_, f32[2,1,512]{2,1,0:T(1,128)S(1)} %copy-done.21, f32[1024,128]{1,0:T(8,128)S(1)} %copy-done.7, f32[1024,128]{1,0:T(8,128)S(1)} %copy-done.9, ...), custom_call_target="tpu_custom_call" | custom-call | flops 75161928 | bytes 209715 | tf_op jit(solution)/shard_map/attention_back/pallas_call | solution.py:569
  979.6 11.6 weight_grad.16
  991.2 11.9 weight_grad.17
  1013.9 8.7 collective-permute-done.70
  1030.1 12.3 weight_grad.18
  1042.3 11.7 weight_grad.19
  1057.4 9.1 collective-permute-done.75
  1098.3 11.6 weight_grad.20
  1109.9 11.6 weight_grad.21
  1130.4 16.8 %collective-permute-done.83 = bf16[256,512]{1,0:T(8,128)(2,1)S(1)} collective-permute-done((bf16[256,512]{1,0:T(8,128)(2,1)S(1)}, bf16[256,512]{1,0:T(8,128)(2,1)S(1)}, u32[]{:S(2)}, u32[]{:S(2)}) %collective-permute-start.83) | collective-permute-done | bytes 262176 | tf_op jit(solution)/shard_map/ppermute | solution.py:73
  1156.7 11.6 weight_grad.22
  1168.3 11.8 weight_grad.23
  1195.9 9.7 collective-permute-done.90
  1254.4 13.8 %collective-permute-done.95 = bf16[512,512]{1,0:T(8,128)(2,1)S(1)} collective-permute-done((bf16[512,512]{1,0:T(8,128)(2,1)S(1)}, bf16[512,512]{1,0:T(8,128)(2,1)S(1)}, u32[]{:S(2)}, u32[]{:S(2)}) %collective-permute-start.95) | collective-permute-done | bytes 524320 | tf_op jit(solution)/shard_map/ppermute | solution.py:73
  1306.5 8.4 collective-permute-done.93
  1348.2 19.6 %collective-permute-done.110 = bf16[1024,512]{1,0:T(8,128)(2,1)S(1)} collective-permute-done((bf16[1024,512]{1,0:T(8,128)(2,1)S(1)}, bf16[1024,512]{1,0:T(8,128)(2,1)S(1)}, u32[]{:S(2)}, u32[]{:S(2)}) %collective-permute-start.110) | collective-permute-done | bytes 1048608 | tf_op jit(solution)/shard_map/ppermute | solution.py:73
  (844 shorter events, 487.4 us)
Async XLA Ops:
  7.2 217.8 %all-gather.3.cloned.1.call-start = ((), (), s32[]{:S(2)}) async-start(), calls=%async_computation | async-start | bytes 34603008 | tf_op jit(solution)/shard_map/all_gather | solution.py:675
  10.1 413.1 %all-gather.5.cloned.1.call-start = ((), (), s32[]{:S(2)}) async-start(), calls=%async_computation.1 | async-start | bytes 34603008 | tf_op jit(solution)/shard_map/all_gather | solution.py:701
  12.6 33.8 %collective-permute-start = (bf16[256,2048]{1,0:T(8,128)(2,1)S(1)}, bf16[256,2048]{1,0:T(8,128)(2,1)}, u32[]{:S(2)}, u32[]{:S(2)}) collective-permute-start(bf16[256,2048]{1,0:T(8,128)(2,1)S(1)} %multiply_convert_fusion.1), channel_id=1, source_target_pairs={{0,2},{2,0},{1,3},{3,1},{4,6},{6,4},{5,7},{7,5},{8,10},{10,8},{9,1... | collective-permute-start | bytes 3145736 | tf_op jit(solution)/shard_map/ppermute | solution.py:73
  101.6 38.5 %collective-permute-start.3 = (bf16[256,2048]{1,0:T(8,128)(2,1)S(1)}, bf16[256,2048]{1,0:T(8,128)(2,1)}, u32[]{:S(2)}, u32[]{:S(2)}) collective-permute-start(bf16[256,2048]{1,0:T(8,128)(2,1)S(1)} %dynamic-slice_bitcast_fusion.7), channel_id=1, source_target_pairs={{0,2},{2,0},{1,3},{3,1},{4,6},{6,4},{5,7},{7,5},{8,10},{10,8},{9,1... | collective-permute-start | bytes 3145736 | tf_op jit(solution)/shard_map/ppermute | solution.py:73
  225.0 1148.2 %all-reduce.2.cloned.1.call-start = ((), (), s32[]{:S(2)}) async-start(), calls=%async_computation.2 | async-start | bytes 1048576 | tf_op jit(solution)/shard_map/psum | solution.py:887
  284.2 93.0 %collective-permute-start.13 = (f32[16,8,256]{2,1,0:T(8,128)S(1)}, f32[16,8,256]{2,1,0:T(8,128)S(1)}, u32[]{:S(2)}, u32[]{:S(2)}) collective-permute-start(f32[16,8,256]{2,1,0:T(8,128)S(1)} %pad_maximum_fusion.14), channel_id=1, source_target_pairs={{0,1},{1,0},{2,3},{3,2},{4,5},{5,4},{6,7},{7,6},{8,9},{9,8},{10,11... | collective-permute-start | bytes 393224 | tf_op jit(solution)/shard_map/ppermute | solution.py:73
  571.5 59.3 %collective-permute-start.30 = (bf16[2,4,256,640]{3,2,1,0:T(8,128)(2,1)}, bf16[2,4,256,640]{3,2,1,0:T(8,128)(2,1)S(1)}, u32[]{:S(2)}, u32[]{:S(2)}) collective-permute-start(bf16[2,4,256,640]{3,2,1,0:T(8,128)(2,1)} %get-tuple-element.146), channel_id=1, source_target_pairs={{0,2},{2,0},{1,3},{3,1},{4,6},{6,4},{5,7},{7,5},{8,10},{10,8},{9,1... | collective-permute-start | bytes 7864328 | tf_op jit(solution)/shard_map/ppermute | solution.py:73
  612.0 48.7 %collective-permute-start.31 = (bf16[2,4,256,512]{3,2,1,0:T(8,128)(2,1)}, bf16[2,4,256,512]{3,2,1,0:T(8,128)(2,1)S(1)}, u32[]{:S(2)}, u32[]{:S(2)}) collective-permute-start(bf16[2,4,256,512]{3,2,1,0:T(8,128)(2,1)} %get-tuple-element.149), channel_id=1, source_target_pairs={{0,4},{4,0},{1,5},{5,1},{2,6},{6,2},{3,7},{7,3},{8,12},{12,8},{9,1... | collective-permute-start | bytes 6291464 | tf_op jit(solution)/shard_map/ppermute | solution.py:73
  636.5 52.4 %collective-permute-start.32 = (bf16[4,256,640]{2,1,0:T(8,128)(2,1)S(1)}, bf16[4,256,640]{2,1,0:T(8,128)(2,1)}, u32[]{:S(2)}, u32[]{:S(2)}) collective-permute-start(bf16[4,256,640]{2,1,0:T(8,128)(2,1)S(1)} %slice_bitcast_fusion.1.refs_8_), channel_id=1, source_target_pairs={{0,4},{4,0},{1,5},{5,1},{2,6},{6,2},{3,7},{7,3},{8,12},{12,8},{9,1... | collective-permute-start | bytes 3932168 | tf_op jit(solution)/shard_map/ppermute | solution.py:73
  638.0 29.1 %collective-permute-start.23 = (bf16[1,4,256,512]{3,2,1,0:T(8,128)(2,1)}, bf16[1,4,256,512]{3,2,1,0:T(8,128)(2,1)}, u32[]{:S(2)}, u32[]{:S(2)}) collective-permute-start(bf16[1,4,256,512]{3,2,1,0:T(8,128)(2,1)} %get-tuple-element.137), channel_id=1, source_target_pairs={{0,1},{1,0},{2,3},{3,2},{4,5},{5,4},{6,7},{7,6},{8,9},{9,8},{10,11... | collective-permute-start | bytes 3145736 | tf_op jit(solution)/shard_map/ppermute | solution.py:73
  638.1 29.1 %collective-permute-start.24 = (bf16[1,4,256,512]{3,2,1,0:T(8,128)(2,1)}, bf16[1,4,256,512]{3,2,1,0:T(8,128)(2,1)}, u32[]{:S(2)}, u32[]{:S(2)}) collective-permute-start(bf16[1,4,256,512]{3,2,1,0:T(8,128)(2,1)} %get-tuple-element.138), channel_id=1, source_target_pairs={{0,1},{1,0},{2,3},{3,2},{4,5},{5,4},{6,7},{7,6},{8,9},{9,8},{10,11... | collective-permute-start | bytes 3145736 | tf_op jit(solution)/shard_map/ppermute | solution.py:73
  660.7 46.9 %collective-permute-start.38 = (bf16[2,4,256,512]{3,2,1,0:T(8,128)(2,1)}, bf16[2,4,256,512]{3,2,1,0:T(8,128)(2,1)}, u32[]{:S(2)}, u32[]{:S(2)}) collective-permute-start(bf16[2,4,256,512]{3,2,1,0:T(8,128)(2,1)} %get-tuple-element.158), channel_id=1, source_target_pairs={{0,2},{2,0},{1,3},{3,1},{4,6},{6,4},{5,7},{7,5},{8,10},{10,8},{9,1... | collective-permute-start | bytes 6291464 | tf_op jit(solution)/shard_map/ppermute | solution.py:73
  684.5 59.1 %collective-permute-start.44 = (bf16[2,4,256,512]{3,2,1,0:T(8,128)(2,1)}, bf16[2,4,256,512]{3,2,1,0:T(8,128)(2,1)}, u32[]{:S(2)}, u32[]{:S(2)}) collective-permute-start(bf16[2,4,256,512]{3,2,1,0:T(8,128)(2,1)} %get-tuple-element.167), channel_id=1, source_target_pairs={{0,4},{4,0},{1,5},{5,1},{2,6},{6,2},{3,7},{7,3},{8,12},{12,8},{9,1... | collective-permute-start | bytes 6291464 | tf_op jit(solution)/shard_map/ppermute | solution.py:73
  723.7 40.9 %collective-permute-start.39 = (bf16[1,4,256,512]{3,2,1,0:T(8,128)(2,1)}, bf16[1,4,256,512]{3,2,1,0:T(8,128)(2,1)}, u32[]{:S(2)}, u32[]{:S(2)}) collective-permute-start(bf16[1,4,256,512]{3,2,1,0:T(8,128)(2,1)} %get-tuple-element.161), channel_id=1, source_target_pairs={{0,1},{1,0},{2,3},{3,2},{4,5},{5,4},{6,7},{7,6},{8,9},{9,8},{10,11... | collective-permute-start | bytes 3145736 | tf_op jit(solution)/shard_map/ppermute | solution.py:73
  727.0 38.6 %collective-permute-start.40 = (bf16[1,4,256,512]{3,2,1,0:T(8,128)(2,1)}, bf16[1,4,256,512]{3,2,1,0:T(8,128)(2,1)}, u32[]{:S(2)}, u32[]{:S(2)}) collective-permute-start(bf16[1,4,256,512]{3,2,1,0:T(8,128)(2,1)} %get-tuple-element.162), channel_id=1, source_target_pairs={{0,1},{1,0},{2,3},{3,2},{4,5},{5,4},{6,7},{7,6},{8,9},{9,8},{10,11... | collective-permute-start | bytes 3145736 | tf_op jit(solution)/shard_map/ppermute | solution.py:73
  728.6 39.0 %collective-permute-start.41 = (bf16[1,4,256,512]{3,2,1,0:T(8,128)(2,1)}, bf16[1,4,256,512]{3,2,1,0:T(8,128)(2,1)}, u32[]{:S(2)}, u32[]{:S(2)}) collective-permute-start(bf16[1,4,256,512]{3,2,1,0:T(8,128)(2,1)} %get-tuple-element.163), channel_id=1, source_target_pairs={{0,1},{1,0},{2,3},{3,2},{4,5},{5,4},{6,7},{7,6},{8,9},{9,8},{10,11... | collective-permute-start | bytes 3145736 | tf_op jit(solution)/shard_map/ppermute | solution.py:73
  765.6 37.6 %collective-permute-start.49 = (bf16[4,256,512]{2,1,0:T(8,128)(2,1)S(1)}, bf16[4,256,512]{2,1,0:T(8,128)(2,1)}, u32[]{:S(2)}, u32[]{:S(2)}) collective-permute-start(bf16[4,256,512]{2,1,0:T(8,128)(2,1)S(1)} %slice_bitcast_fusion.12.refs_9_), channel_id=1, source_target_pairs={{0,2},{2,0},{1,3},{3,1},{4,6},{6,4},{5,7},{7,5},{8,10},{10,8},{9,1... | collective-permute-start | bytes 3145736 | tf_op jit(solution)/shard_map/ppermute | solution.py:73
  848.7 56.2 %collective-permute-start.66 = (bf16[2,4,256,512]{3,2,1,0:T(8,128)(2,1)}, bf16[2,4,256,512]{3,2,1,0:T(8,128)(2,1)}, u32[]{:S(2)}, u32[]{:S(2)}) collective-permute-start(bf16[2,4,256,512]{3,2,1,0:T(8,128)(2,1)} %broadcast_add_fusion.2), channel_id=1, source_target_pairs={{0,4},{4,0},{1,5},{5,1},{2,6},{6,2},{3,7},{7,3},{8,12},{12,8},{9,1... | collective-permute-start | bytes 6291464 | tf_op jit(solution)/shard_map/ppermute | solution.py:73
  852.5 65.1 %collective-permute-start.46 = (bf16[2,4,256,512]{3,2,1,0:T(8,128)(2,1)}, bf16[2,4,256,512]{3,2,1,0:T(8,128)(2,1)}, u32[]{:S(2)}, u32[]{:S(2)}) collective-permute-start(bf16[2,4,256,512]{3,2,1,0:T(8,128)(2,1)} %broadcast_add_fusion.3), channel_id=1, source_target_pairs={{0,2},{2,0},{1,3},{3,1},{4,6},{6,4},{5,7},{7,5},{8,10},{10,8},{9,1... | collective-permute-start | bytes 6291464 | tf_op jit(solution)/shard_map/ppermute | solution.py:73
  853.7 36.2 %collective-permute-start.54 = (bf16[1,4,256,512]{3,2,1,0:T(8,128)(2,1)}, bf16[1,4,256,512]{3,2,1,0:T(8,128)(2,1)}, u32[]{:S(2)}, u32[]{:S(2)}) collective-permute-start(bf16[1,4,256,512]{3,2,1,0:T(8,128)(2,1)} %get-tuple-element.172), channel_id=1, source_target_pairs={{0,1},{1,0},{2,3},{3,2},{4,5},{5,4},{6,7},{7,6},{8,9},{9,8},{10,11... | collective-permute-start | bytes 3145736 | tf_op jit(solution)/shard_map/ppermute | solution.py:73
  874.6 52.8 %collective-permute-start.65 = (bf16[512,2048]{1,0:T(8,128)(2,1)}, bf16[512,2048]{1,0:T(8,128)(2,1)}, u32[]{:S(2)}, u32[]{:S(2)}) collective-permute-start(bf16[512,2048]{1,0:T(8,128)(2,1)} %pad_maximum_fusion.2), channel_id=1, source_target_pairs={{0,1},{1,0},{2,3},{3,2},{4,5},{5,4},{6,7},{7,6},{8,9},{9,8},{10,11... | collective-permute-start | bytes 6291464 | tf_op jit(solution)/shard_map/ppermute | solution.py:73
  907.9 95.8 %collective-permute-start.69 = (bf16[4,256,512]{2,1,0:T(8,128)(2,1)S(1)}, bf16[4,256,512]{2,1,0:T(8,128)(2,1)S(1)}, u32[]{:S(2)}, u32[]{:S(2)}) collective-permute-start(bf16[4,256,512]{2,1,0:T(8,128)(2,1)S(1)} %slice_bitcast_fusion.7.refs_11_), channel_id=1, source_target_pairs={{0,2},{2,0},{1,3},{3,1},{4,6},{6,4},{5,7},{7,5},{8,10},{10,8},{9,1... | collective-permute-start | bytes 3145736 | tf_op jit(solution)/shard_map/ppermute | solution.py:73
  920.6 86.7 %collective-permute-start.63 = (bf16[4,256,512]{2,1,0:T(8,128)(2,1)S(1)}, bf16[4,256,512]{2,1,0:T(8,128)(2,1)}, u32[]{:S(2)}, u32[]{:S(2)}) collective-permute-start(bf16[4,256,512]{2,1,0:T(8,128)(2,1)S(1)} %slice_bitcast_fusion.8.refs_10_), channel_id=1, source_target_pairs={{0,4},{4,0},{1,5},{5,1},{2,6},{6,2},{3,7},{7,3},{8,12},{12,8},{9,1... | collective-permute-start | bytes 3145736 | tf_op jit(solution)/shard_map/ppermute | solution.py:73
  972.7 37.9 %collective-permute-start.71 = (bf16[1024,512]{1,0:T(8,128)(2,1)S(1)}, bf16[1024,512]{1,0:T(8,128)(2,1)}, u32[]{:S(2)}, u32[]{:S(2)}) collective-permute-start(bf16[1024,512]{1,0:T(8,128)(2,1)S(1)} %dynamic-slice_bitcast_fusion.6.refs_4_), channel_id=1, source_target_pairs={{0,4},{4,0},{1,5},{5,1},{2,6},{6,2},{3,7},{7,3},{8,12},{12,8},{9,1... | collective-permute-start | bytes 3145736 | tf_op jit(solution)/shard_map/ppermute | solution.py:73
  977.0 49.0 %collective-permute-start.68 = (bf16[512,2048]{1,0:T(8,128)(2,1)}, bf16[512,2048]{1,0:T(8,128)(2,1)}, u32[]{:S(2)}, u32[]{:S(2)}) collective-permute-start(bf16[512,2048]{1,0:T(8,128)(2,1)} %dynamic-slice_bitcast_fusion), channel_id=1, source_target_pairs={{0,1},{1,0},{2,3},{3,2},{4,5},{5,4},{6,7},{7,6},{8,9},{9,8},{10,11... | collective-permute-start | bytes 6291464 | tf_op jit(solution)/shard_map/ppermute | solution.py:73
  978.5 44.0 %collective-permute-start.70 = (bf16[256,2048]{1,0:T(8,128)(2,1)}, bf16[256,2048]{1,0:T(8,128)(2,1)}, u32[]{:S(2)}, u32[]{:S(2)}) collective-permute-start(bf16[256,2048]{1,0:T(8,128)(2,1)} %dynamic-slice_bitcast_fusion.2), channel_id=1, source_target_pairs={{0,4},{4,0},{1,5},{5,1},{2,6},{6,2},{3,7},{7,3},{8,12},{12,8},{9,1... | collective-permute-start | bytes 3145736 | tf_op jit(solution)/shard_map/ppermute | solution.py:73
  1003.7 73.9 %collective-permute-start.78 = (bf16[2,4,256,512]{3,2,1,0:T(8,128)(2,1)}, bf16[2,4,256,512]{3,2,1,0:T(8,128)(2,1)}, u32[]{:S(2)}, u32[]{:S(2)}) collective-permute-start(bf16[2,4,256,512]{3,2,1,0:T(8,128)(2,1)} %broadcast_add_fusion.1), channel_id=1, source_target_pairs={{0,2},{2,0},{1,3},{3,1},{4,6},{6,4},{5,7},{7,5},{8,10},{10,8},{9,1... | collective-permute-start | bytes 6291464 | tf_op jit(solution)/shard_map/ppermute | solution.py:73
  1007.3 200.4 %collective-permute-start.92 = (bf16[2,4,256,512]{3,2,1,0:T(8,128)(2,1)}, bf16[2,4,256,512]{3,2,1,0:T(8,128)(2,1)}, u32[]{:S(2)}, u32[]{:S(2)}) collective-permute-start(bf16[2,4,256,512]{3,2,1,0:T(8,128)(2,1)} %broadcast_add_fusion), channel_id=1, source_target_pairs={{0,2},{2,0},{1,3},{3,1},{4,6},{6,4},{5,7},{7,5},{8,10},{10,8},{9,1... | collective-permute-start | bytes 6291464 | tf_op jit(solution)/shard_map/ppermute | solution.py:73
  1010.6 58.7 %collective-permute-start.77 = (bf16[1024,512]{1,0:T(8,128)(2,1)S(1)}, bf16[1024,512]{1,0:T(8,128)(2,1)}, u32[]{:S(2)}, u32[]{:S(2)}) collective-permute-start(bf16[1024,512]{1,0:T(8,128)(2,1)S(1)} %dynamic-slice_bitcast_fusion.4.refs_6_), channel_id=1, source_target_pairs={{0,4},{4,0},{1,5},{5,1},{2,6},{6,2},{3,7},{7,3},{8,12},{12,8},{9,1... | collective-permute-start | bytes 3145736 | tf_op jit(solution)/shard_map/ppermute | solution.py:73
  1022.5 49.9 %collective-permute-start.76 = (bf16[1024,512]{1,0:T(8,128)(2,1)S(1)}, bf16[1024,512]{1,0:T(8,128)(2,1)}, u32[]{:S(2)}, u32[]{:S(2)}) collective-permute-start(bf16[1024,512]{1,0:T(8,128)(2,1)S(1)} %dynamic-slice_bitcast_fusion.5.refs_5_), channel_id=1, source_target_pairs={{0,4},{4,0},{1,5},{5,1},{2,6},{6,2},{3,7},{7,3},{8,12},{12,8},{9,1... | collective-permute-start | bytes 3145736 | tf_op jit(solution)/shard_map/ppermute | solution.py:73
  1069.3 53.3 %collective-permute-start.86 = (f32[2,512]{1,0:T(2,128)S(1)}, f32[2,512]{1,0:T(2,128)S(1)}, u32[]{:S(2)}, u32[]{:S(2)}) collective-permute-start(f32[2,512]{1,0:T(2,128)S(1)} %bitcast.419), channel_id=1, source_target_pairs={{0,16},{16,0},{1,17},{17,1},{2,18},{18,2},{3,19},{19,3},{4,20},{20... | collective-permute-start | bytes 12296 | tf_op jit(solution)/shard_map/ppermute | solution.py:73
  1077.6 45.9 %collective-permute-start.82 = (bf16[64,2048]{1,0:T(8,128)(2,1)S(1)}, bf16[64,2048]{1,0:T(8,128)(2,1)}, u32[]{:S(2)}, u32[]{:S(2)}) collective-permute-start(bf16[64,2048]{1,0:T(8,128)(2,1)S(1)} %dynamic-slice_bitcast_fusion.15.refs_4_), channel_id=1, source_target_pairs={{0,16},{16,0},{1,17},{17,1},{2,18},{18,2},{3,19},{19,3},{4,20},{20... | collective-permute-start | bytes 786440 | tf_op jit(solution)/shard_map/ppermute | solution.py:73
  1095.4 31.2 %collective-permute-start.79 = (bf16[1,256,512]{2,1,0:T(8,128)(2,1)}, bf16[1,256,512]{2,1,0:T(8,128)(2,1)}, u32[]{:S(2)}, u32[]{:S(2)}) collective-permute-start(bf16[1,256,512]{2,1,0:T(8,128)(2,1)} %slice.421.refs_7_), channel_id=1, source_target_pairs={{0,16},{16,0},{1,17},{17,1},{2,18},{18,2},{3,19},{19,3},{4,20},{20... | collective-permute-start | bytes 786440 | tf_op jit(solution)/shard_map/ppermute | solution.py:73
  1095.6 33.0 %collective-permute-start.72 = (bf16[1,256,512]{2,1,0:T(8,128)(2,1)}, bf16[1,256,512]{2,1,0:T(8,128)(2,1)}, u32[]{:S(2)}, u32[]{:S(2)}) collective-permute-start(bf16[1,256,512]{2,1,0:T(8,128)(2,1)} %slice.419.refs_6_), channel_id=1, source_target_pairs={{0,16},{16,0},{1,17},{17,1},{2,18},{18,2},{3,19},{19,3},{4,20},{20... | collective-permute-start | bytes 786440 | tf_op jit(solution)/shard_map/ppermute | solution.py:73
  1147.2 34.8 %collective-permute-start.80 = (bf16[4,256,512]{2,1,0:T(8,128)(2,1)S(1)}, bf16[4,256,512]{2,1,0:T(8,128)(2,1)}, u32[]{:S(2)}, u32[]{:S(2)}) collective-permute-start(bf16[4,256,512]{2,1,0:T(8,128)(2,1)S(1)} %slice_bitcast_fusion.5.refs_10_), channel_id=1, source_target_pairs={{0,4},{4,0},{1,5},{5,1},{2,6},{6,2},{3,7},{7,3},{8,12},{12,8},{9,1... | collective-permute-start | bytes 3145736 | tf_op jit(solution)/shard_map/ppermute | solution.py:73
  1147.9 93.9 %collective-permute-start.99 = (f32[2,512]{1,0:T(2,128)S(1)}, f32[2,512]{1,0:T(2,128)S(1)}, u32[]{:S(2)}, u32[]{:S(2)}) collective-permute-start(f32[2,512]{1,0:T(2,128)S(1)} %add_add_fusion.6.refs_11_), channel_id=1, source_target_pairs={{0,8},{8,0},{1,9},{9,1},{2,10},{10,2},{3,11},{11,3},{4,12},{12,4},... | collective-permute-start | bytes 12296 | tf_op jit(solution)/shard_map/ppermute | solution.py:73
  1151.8 61.2 %collective-permute-start.89 = (bf16[256,512]{1,0:T(8,128)(2,1)S(1)}, bf16[256,512]{1,0:T(8,128)(2,1)}, u32[]{:S(2)}, u32[]{:S(2)}) collective-permute-start(bf16[256,512]{1,0:T(8,128)(2,1)S(1)} %fusion.36.refs_6_), channel_id=1, source_target_pairs={{0,16},{16,0},{1,17},{17,1},{2,18},{18,2},{3,19},{19,3},{4,20},{20... | collective-permute-start | bytes 786440 | tf_op jit(solution)/shard_map/ppermute | solution.py:73
  1195.8 56.6 %collective-permute-start.87 = (bf16[2,256,512]{2,1,0:T(8,128)(2,1)}, bf16[2,256,512]{2,1,0:T(8,128)(2,1)}, u32[]{:S(2)}, u32[]{:S(2)}) collective-permute-start(bf16[2,256,512]{2,1,0:T(8,128)(2,1)} %slice.426.refs_8_), channel_id=1, source_target_pairs={{0,8},{8,0},{1,9},{9,1},{2,10},{10,2},{3,11},{11,3},{4,12},{12,4},... | collective-permute-start | bytes 1572872 | tf_op jit(solution)/shard_map/ppermute | solution.py:73
  1205.6 40.9 %collective-permute-start.97 = (bf16[256,512]{1,0:T(8,128)(2,1)S(1)}, bf16[256,512]{1,0:T(8,128)(2,1)}, u32[]{:S(2)}, u32[]{:S(2)}) collective-permute-start(bf16[256,512]{1,0:T(8,128)(2,1)S(1)} %fusion.34.refs_6_), channel_id=1, source_target_pairs={{0,16},{16,0},{1,17},{17,1},{2,18},{18,2},{3,19},{19,3},{4,20},{20... | collective-permute-start | bytes 786440 | tf_op jit(solution)/shard_map/ppermute | solution.py:73
  1207.7 40.6 %collective-permute-start.96 = (bf16[256,512]{1,0:T(8,128)(2,1)S(1)}, bf16[256,512]{1,0:T(8,128)(2,1)}, u32[]{:S(2)}, u32[]{:S(2)}) collective-permute-start(bf16[256,512]{1,0:T(8,128)(2,1)S(1)} %fusion.35.refs_5_), channel_id=1, source_target_pairs={{0,16},{16,0},{1,17},{17,1},{2,18},{18,2},{3,19},{19,3},{4,20},{20... | collective-permute-start | bytes 786440 | tf_op jit(solution)/shard_map/ppermute | solution.py:73
  1248.3 67.6 %collective-permute-start.112 = (f32[2,512]{1,0:T(2,128)S(1)}, f32[2,512]{1,0:T(2,128)S(1)}, u32[]{:S(2)}, u32[]{:S(2)}) collective-permute-start(f32[2,512]{1,0:T(2,128)S(1)} %add_add_fusion.5.refs_10_), channel_id=1, source_target_pairs={{0,4},{4,0},{1,5},{5,1},{2,6},{6,2},{3,7},{7,3},{8,12},{12,8},{9,1... | collective-permute-start | bytes 12296 | tf_op jit(solution)/shard_map/ppermute | solution.py:73
  1252.4 49.6 %collective-permute-start.104 = (f32[2,2048]{1,0:T(2,128)S(1)}, f32[2,2048]{1,0:T(2,128)S(1)}, u32[]{:S(2)}, u32[]{:S(2)}) collective-permute-start(f32[2,2048]{1,0:T(2,128)S(1)} %add_add_fusion.2), channel_id=1, source_target_pairs={{0,4},{4,0},{1,5},{5,1},{2,6},{6,2},{3,7},{7,3},{8,12},{12,8},{9,1... | collective-permute-start | bytes 49160 | tf_op jit(solution)/shard_map/ppermute | solution.py:73
  1268.3 30.8 %collective-permute-start.107 = (bf16[512,512]{1,0:T(8,128)(2,1)}, bf16[512,512]{1,0:T(8,128)(2,1)}, u32[]{:S(2)}, u32[]{:S(2)}) collective-permute-start(bf16[512,512]{1,0:T(8,128)(2,1)} %pad_maximum_fusion.11.refs_6_), channel_id=1, source_target_pairs={{0,8},{8,0},{1,9},{9,1},{2,10},{10,2},{3,11},{11,3},{4,12},{12,4},... | collective-permute-start | bytes 1572872 | tf_op jit(solution)/shard_map/ppermute | solution.py:73
  1269.7 33.7 %collective-permute-start.109 = (bf16[512,512]{1,0:T(8,128)(2,1)}, bf16[512,512]{1,0:T(8,128)(2,1)}, u32[]{:S(2)}, u32[]{:S(2)}) collective-permute-start(bf16[512,512]{1,0:T(8,128)(2,1)} %pad_maximum_fusion.12.refs_7_), channel_id=1, source_target_pairs={{0,8},{8,0},{1,9},{9,1},{2,10},{10,2},{3,11},{11,3},{4,12},{12,4},... | collective-permute-start | bytes 1572872 | tf_op jit(solution)/shard_map/ppermute | solution.py:73
  1271.9 56.9 %collective-permute-start.113 = (bf16[256,2048]{1,0:T(8,128)(2,1)S(1)}, bf16[256,2048]{1,0:T(8,128)(2,1)}, u32[]{:S(2)}, u32[]{:S(2)}) collective-permute-start(bf16[256,2048]{1,0:T(8,128)(2,1)S(1)} %pad_maximum_fusion.3.refs_4_), channel_id=1, source_target_pairs={{0,4},{4,0},{1,5},{5,1},{2,6},{6,2},{3,7},{7,3},{8,12},{12,8},{9,1... | collective-permute-start | bytes 3145736 | tf_op jit(solution)/shard_map/ppermute | solution.py:73
  1299.1 34.0 %collective-permute-start.111 = (bf16[1024,512]{1,0:T(8,128)(2,1)S(1)}, bf16[1024,512]{1,0:T(8,128)(2,1)S(1)}, u32[]{:S(2)}, u32[]{:S(2)}) collective-permute-start(bf16[1024,512]{1,0:T(8,128)(2,1)S(1)} %pad_maximum_fusion.4.refs_5_), channel_id=1, source_target_pairs={{0,4},{4,0},{1,5},{5,1},{2,6},{6,2},{3,7},{7,3},{8,12},{12,8},{9,1... | collective-permute-start | bytes 3145736 | tf_op jit(solution)/shard_map/ppermute | solution.py:73
  1314.9 32.8 %collective-permute-start.108 = (bf16[1024,512]{1,0:T(8,128)(2,1)S(1)}, bf16[1024,512]{1,0:T(8,128)(2,1)S(1)}, u32[]{:S(2)}, u32[]{:S(2)}) collective-permute-start(bf16[1024,512]{1,0:T(8,128)(2,1)S(1)} %pad_maximum_fusion.5), channel_id=1, source_target_pairs={{0,4},{4,0},{1,5},{5,1},{2,6},{6,2},{3,7},{7,3},{8,12},{12,8},{9,1... | collective-permute-start | bytes 3145736 | tf_op jit(solution)/shard_map/ppermute | solution.py:73
  1326.6 41.2 %collective-permute-start.110 = (bf16[1024,512]{1,0:T(8,128)(2,1)S(1)}, bf16[1024,512]{1,0:T(8,128)(2,1)S(1)}, u32[]{:S(2)}, u32[]{:S(2)}) collective-permute-start(bf16[1024,512]{1,0:T(8,128)(2,1)S(1)} %pad_maximum_fusion.6), channel_id=1, source_target_pairs={{0,4},{4,0},{1,5},{5,1},{2,6},{6,2},{3,7},{7,3},{8,12},{12,8},{9,1... | collective-permute-start | bytes 3145736 | tf_op jit(solution)/shard_map/ppermute | solution.py:73
  (254 other events, 2982.2 us)
Sparse Core Ops, SparseCore 0:
  11.5 213.4 all-gather.2
  227.8 195.3 all-gather.4
  876.6 126.7 all-reduce.1

commit v4 on v3

--- a/solution.py
+++ b/solution.py
@@ -598,33 +598,27 @@
 
 
 def weight_grad_kernel(left_ref, right_ref, out_ref, done_ref):
-    out_ref[0, 0] = dot(left_ref[0, 0], right_ref[0, 0], TN)
+    turned = left_ref[0].T
+    for pair in range(out_ref.shape[1]):
+        out_ref[0, pair] = dot(turned, right_ref[0, pair])
     done_ref[...] = jnp.zeros_like(done_ref)
 
 
-def weight_grad(left, right, tile_left, tile_right, first, last, into=None, after=()):
-    experts, left_pairs, count, left_width = left.shape
-    _, right_pairs, _, right_width = right.shape
-    pairs = max(left_pairs, right_pairs)
-
-    def left_map(e, i, j, p):
-        return (e + first, p if left_pairs > 1 else 0, 0, i)
-
-    def right_map(e, i, j, p):
-        return (e + first, p if right_pairs > 1 else 0, 0, j)
-
+def weight_grad(left, right, tile, first, last, into=None, after=()):
+    experts, count, left_width = left.shape
+    _, pairs, _, right_width = right.shape
     rest = ([] if into is None else [into]) + list(after)
     return pl.pallas_call(
         without(2, len(rest), weight_grad_kernel),
-        grid=(last - first, left_width // tile_left, right_width // tile_right, pairs),
+        grid=(last - first, left_width // tile),
         in_specs=[
-            pl.BlockSpec((1, 1, count, tile_left), left_map),
-            pl.BlockSpec((1, 1, count, tile_right), right_map),
+            pl.BlockSpec((1, count, tile), lambda e, i: (e + first, 0, i)),
+            pl.BlockSpec((1, pairs, count, right_width), lambda e, i: (e + first, 0, 0, 0)),
         ]
         + [pl.BlockSpec(memory_space=pl.ANY)] * len(rest),
         out_specs=[
-            pl.BlockSpec((1, 1, tile_left, tile_right), lambda e, i, j, p: (e + first, p, i, j)),
-            pl.BlockSpec((8, 128), lambda e, i, j, p: (0, 0)),
+            pl.BlockSpec((1, pairs, tile, right_width), lambda e, i: (e + first, 0, i, 0)),
+            pl.BlockSpec((8, 128), lambda e, i: (0, 0)),
         ],
         out_shape=[
             jax.ShapeDtypeStruct((experts, pairs, left_width, right_width), WIDE),
@@ -864,12 +858,12 @@
         now_down, down_left = down_left[:down_count], down_left[down_count:]
         for e in now_up:
             up_grad, done = weight_grad(
-                row_slots[:, None], grad_pair, 512, units, e, e + 1, up_grad, now
+                row_slots, grad_pair, 512, e, e + 1, up_grad, now
             )
             now = (done,)
         for e in now_down:
             down_grad, done = weight_grad(
-                act, grad_slots[:, None], units, 512, e, e + 1, down_grad, now
+                gated_act, grad_slots[:, None], units, e, e + 1, down_grad, now
             )
             now = (done,)
         now = advance(wave, done)

time: 1400 us -> 1380 us (0.986)
  Pallas kernels: 570 us -> 541 us
  waiting for transfers between devices: 417 us -> 431 us
    pallas_call x16, Pallas kernels: 143 us -> 114 us  [weight_grad(): pl.pallas_call(without(2, len(rest), weight_grad_kernel), grid=(last - fi...]
    ppermute x114, waiting for transfers between devices: 294 us -> 309 us  [swap(): return lax.ppermute(values, axis, [(0, 1), (1, 0)])]
  transfers between devices with their start and end apart: 117 -> 117, of which waited for: 41 -> 43; matrix products, arithmetic and copies ran while one was open for 18% -> 18% of each run, Pallas kernels for 32% -> 31%
where the time goes in v4:
time: 1380 us; the launch traced here: 1370 us
  Pallas kernels  541 us (39%)
  waiting for transfers between devices  431 us (31%)
  other arithmetic  165 us (12%)
  starting transfers between devices  91.5 us (7%)
  local copies, waits for them, and re-layouts  80.7 us (6%)
  matrix products  37.6 us (3%)
  between operations  19.6 us (1%)
    ppermute x114, waiting for transfers between devices, swap(): return lax.ppermute(values, axis, [(0, 1), (1, 0)])  309 us
    pallas_call x16, Pallas kernels, combine(): pl.pallas_call(without(len(operands), len(after), kernel), grid=(experts...  229 us
    pallas_call x16, Pallas kernels, weight_grad(): pl.pallas_call(without(2, len(rest), weight_grad_kernel), grid=(last - fi...  114 us
    ppermute x114, starting transfers between devices, swap(): return lax.ppermute(values, axis, [(0, 1), (1, 0)])  91.3 us
    pallas_call x2, Pallas kernels, dispatch(): pl.pallas_call(dispatch_kernel, grid_spec=pltpu.PrefetchScalarGridSpec(nu...  88.3 us
    all_gather x1, waiting for transfers between devices, shards(): lax.all_gather(cotangent.astype(LOW), grid.all, axis=0, tiled=True)  79.6 us
    convert_element_type x38, other arithmetic, add_low(): return total.astype(terms[0].dtype)  67.2 us
    pallas_call x1, Pallas kernels, hidden_units(): pl.pallas_call(hidden_kernel, grid=(experts, count // tile), in_specs=[pl...  47.9 us
  transfers between devices with their start and end apart: 117, of which 43 were waited for; matrix products, arithmetic and copies ran while one was open for 18% of the time, Pallas kernels for 31%

profile of v4, /device:TPU:0, one launch (start us, length us, event | category | flops | bytes accessed | tf_op | source)
XLA Modules:
  0.0 1367.0 jit_solution(17782160382384234847)
XLA Ops:
  15.7 30.8 %collective-permute-done = bf16[256,2048]{1,0:T(8,128)(2,1)} collective-permute-done((bf16[256,2048]{1,0:T(8,128)(2,1)S(1)}, bf16[256,2048]{1,0:T(8,128)(2,1)}, u32[]{:S(2)}, u32[]{:S(2)}) %collective-permute-start) | collective-permute-done | bytes 1048608 | tf_op jit(solution)/shard_map/ppermute | solution.py:73
  62.8 8.8 convolution_bitcast_fusion.pre_ref.refs_0_
  71.6 14.9 %attention.1 = (bf16[3,1024,512]{2,1,0:T(8,128)(2,1)S(1)}, bf16[1024,512]{1,0:T(8,128)(2,1)S(1)}, f32[4,1,1024]{2,1,0:T(1,128)S(1)}) custom-call(f32[3,1024,512]{2,1,0:T(8,128)} %convolution_bitcast_fusion.pre_ref.refs_0_, f32[2,1,512]{2,1,0:T(1,128)S(1)} %broadcast_in_dim.31.gain_ref.refs_1_, f32[1024,128]{1,0:T(8,128)S(1)} %get-tuple-element.291.cos_ref.refs_2_, ...), custom_call_target="tpu_custom_call" | custom-call | flops 32212254 | bytes 209715 | tf_op jit(solution)/shard_map/attention/pallas_call | solution.py:485
  103.4 36.7 %collective-permute-done.3 = bf16[256,2048]{1,0:T(8,128)(2,1)} collective-permute-done((bf16[256,2048]{1,0:T(8,128)(2,1)S(1)}, bf16[256,2048]{1,0:T(8,128)(2,1)}, u32[]{:S(2)}, u32[]{:S(2)}) %collective-permute-start.3) | collective-permute-done | bytes 1048608 | tf_op jit(solution)/shard_map/ppermute | solution.py:73
  145.4 79.6 %all-gather.3.cloned.1.call-done = bf16[8192,2048]{1,0:T(8,128)(2,1)} async-done(((bf16[256,2048]{1,0:T(8,128)(2,1)}), bf16[8192,2048]{1,0:T(8,128)(2,1)}) %all-gather.3.cloned.1.call-update) | async-done | bytes 33554448 | tf_op jit(solution)/shard_map/all_gather | solution.py:669
  271.1 13.1 copy.64
  284.4 9.0 compare_convert_fusion.refs_2_
  295.1 44.5 %dispatch.3.rows_ref = bf16[8,1536,2048]{2,1,0:T(8,128)(2,1)} custom-call(s32[32]{0:T(128)S(1)} %add.770.order_ref, bf16[32,384,256]{2,1,0:T(8,128)(2,1)S(1)} %fusion.select_ref, bf16[32,256,2048]{2,1,0:T(8,128)(2,1)} %bitcast.340), custom_call_target="tpu_custom_call" | custom-call | flops 128849016 | bytes 838860 | tf_op jit(solution)/shard_map/dispatch/pallas_call | solution.py:221
  342.2 30.6 %grad_active.1.grad_ref = f32[8,1536,256]{2,1,0:T(8,128)S(1)} custom-call(bf16[8,1536,2048]{2,1,0:T(8,128)(2,1)} %dispatch.3.rows_ref, bf16[8,256,2048]{2,1,0:T(8,128)(2,1)S(1)} %bitcast.327), custom_call_target="tpu_custom_call" | custom-call | flops 128849016 | bytes 503316 | tf_op jit(solution)/shard_map/grad_active/pallas_call | solution.py:251
  380.7 42.5 %all-gather.5.cloned.1.call-done = bf16[8192,2048]{1,0:T(8,128)(2,1)} async-done(((bf16[256,2048]{1,0:T(8,128)(2,1)}), bf16[8192,2048]{1,0:T(8,128)(2,1)}) %all-gather.5.cloned.1.call-update) | async-done | bytes 33554448 | tf_op jit(solution)/shard_map/all_gather | solution.py:695
  426.0 43.9 %dispatch.2.rows_ref.refs_0_ = bf16[8,1536,2048]{2,1,0:T(8,128)(2,1)} custom-call(s32[32]{0:T(128)S(1)} %add.770.order_ref, bf16[32,384,256]{2,1,0:T(8,128)(2,1)S(1)} %copy-done.4, bf16[32,256,2048]{2,1,0:T(8,128)(2,1)} %bitcast.341), custom_call_target="tpu_custom_call" | custom-call | flops 128849016 | bytes 838860 | tf_op jit(solution)/shard_map/dispatch/pallas_call | solution.py:221
  469.9 47.9 %hidden_units.1 = (bf16[8,1536,256]{2,1,0:T(8,128)(2,1)S(1)}, bf16[8,2,1536,256]{3,2,1,0:T(8,128)(2,1)}, f32[8,1,1536]{2,1,0:T(1,128)S(1)}) custom-call(bf16[8,1536,2048]{2,1,0:T(8,128)(2,1)} %dispatch.2.rows_ref.refs_0_, bf16[8,2,2048,256]{3,2,1,0:T(8,128)(2,1)} %refs_1_.15, f32[8,1536,256]{2,1,0:T(8,128)} %copy-done.5, f32[8,1,1536]{2,1,0:T(1,128)S(1)} %reshape.578.gate_ref), custom_call_target="tpu_custom_call" | custom-call | flops 257698032 | bytes 503316 | tf_op jit(solution)/shard_map/hidden_units/pallas_call | solution.py:288
  521.1 15.6 %combine_other.8 = (bf16[1,4,256,640]{3,2,1,0:T(8,128)(2,1)}, bf16[1,4,256,640]{3,2,1,0:T(8,128)(2,1)}, bf16[1,4,256,640]{3,2,1,0:T(8,128)(2,1)}, bf16[1,4,256,640]{3,2,1,0:T(8,128)(2,1)}, f32[8,128]{1,0:T(8,128)}) custom-call(bf16[8,2,1536,256]{3,2,1,0:T(8,128)(2,1)} %get-tuple-element.121.refs_0_.refs_1_, bf16[8,2,2048,256]{3,2,1,0:T(8,128)(2,1)} %refs_1_.15, ...), custom_call_target="tpu_custom_call" | custom-call | flops 120795952 | bytes 293601 | tf_op jit(solution)/shard_map/combine_other/pallas_call | solution.py:416
  537.8 14.7 %combine_other.9 = (bf16[1,4,256,512]{3,2,1,0:T(8,128)(2,1)}, bf16[1,4,256,512]{3,2,1,0:T(8,128)(2,1)}, bf16[1,4,256,512]{3,2,1,0:T(8,128)(2,1)}, bf16[1,4,256,512]{3,2,1,0:T(8,128)(2,1)}, f32[8,128]{1,0:T(8,128)}) custom-call(bf16[8,2,1536,256]{3,2,1,0:T(8,128)(2,1)} %get-tuple-element.121.refs_0_.refs_1_, bf16[8,2,2048,256]{3,2,1,0:T(8,128)(2,1)} %refs_1_.15, ...), custom_call_target="tpu_custom_call" | custom-call | flops 96636768 | bytes 272629 | tf_op jit(solution)/shard_map/combine_other/pallas_call | solution.py:416
  554.8 16.8 %combine_own.8 = (bf16[2,4,256,640]{3,2,1,0:T(8,128)(2,1)}, bf16[2,4,256,640]{3,2,1,0:T(8,128)(2,1)}, f32[8,128]{1,0:T(8,128)}) custom-call(bf16[8,2,1536,256]{3,2,1,0:T(8,128)(2,1)} %get-tuple-element.121.refs_0_.refs_1_, bf16[8,2,2048,256]{3,2,1,0:T(8,128)(2,1)} %refs_1_.15, bf16[32,256,384]{2,1,0:T(8,128)(2,1)} %compare_convert_fusion.refs_2_, ...), custom_call_target="tpu_custom_call" | custom-call | flops 120795952 | bytes 503316 | tf_op jit(solution)/shard_map/combine_own/pallas_call | solution.py:416
  581.4 15.9 %combine_own.9 = (bf16[2,4,256,512]{3,2,1,0:T(8,128)(2,1)}, bf16[2,4,256,512]{3,2,1,0:T(8,128)(2,1)}, f32[8,128]{1,0:T(8,128)}) custom-call(bf16[8,2,1536,256]{3,2,1,0:T(8,128)(2,1)} %get-tuple-element.121.refs_0_.refs_1_, bf16[8,2,2048,256]{3,2,1,0:T(8,128)(2,1)} %refs_1_.15, bf16[32,256,384]{2,1,0:T(8,128)(2,1)} %compare_convert_fusion.refs_2_, ...), custom_call_target="tpu_custom_call" | custom-call | flops 96636768 | bytes 440401 | tf_op jit(solution)/shard_map/combine_own/pallas_call | solution.py:416
  597.3 14.7 %combine_other.10 = (bf16[1,4,256,512]{3,2,1,0:T(8,128)(2,1)}, bf16[1,4,256,512]{3,2,1,0:T(8,128)(2,1)}, bf16[1,4,256,512]{3,2,1,0:T(8,128)(2,1)}, bf16[1,4,256,512]{3,2,1,0:T(8,128)(2,1)}, f32[8,128]{1,0:T(8,128)}) custom-call(bf16[8,2,1536,256]{3,2,1,0:T(8,128)(2,1)} %get-tuple-element.121.refs_0_.refs_1_, bf16[8,2,2048,256]{3,2,1,0:T(8,128)(2,1)} %refs_1_.15, ...), custom_call_target="tpu_custom_call" | custom-call | flops 96636768 | bytes 272629 | tf_op jit(solution)/shard_map/combine_other/pallas_call | solution.py:416
  612.8 14.8 %combine_other.11 = (bf16[1,4,256,512]{3,2,1,0:T(8,128)(2,1)}, bf16[1,4,256,512]{3,2,1,0:T(8,128)(2,1)}, bf16[1,4,256,512]{3,2,1,0:T(8,128)(2,1)}, bf16[1,4,256,512]{3,2,1,0:T(8,128)(2,1)}, f32[8,128]{1,0:T(8,128)}) custom-call(bf16[8,2,1536,256]{3,2,1,0:T(8,128)(2,1)} %get-tuple-element.121.refs_0_.refs_1_, bf16[8,2,2048,256]{3,2,1,0:T(8,128)(2,1)} %refs_1_.15, ...), custom_call_target="tpu_custom_call" | custom-call | flops 96636768 | bytes 272629 | tf_op jit(solution)/shard_map/combine_other/pallas_call | solution.py:416
  638.7 15.6 %combine_own.10 = (bf16[2,4,256,512]{3,2,1,0:T(8,128)(2,1)}, bf16[2,4,256,512]{3,2,1,0:T(8,128)(2,1)}, f32[8,128]{1,0:T(8,128)}) custom-call(bf16[8,2,1536,256]{3,2,1,0:T(8,128)(2,1)} %get-tuple-element.121.refs_0_.refs_1_, bf16[8,2,2048,256]{3,2,1,0:T(8,128)(2,1)} %refs_1_.15, bf16[32,256,384]{2,1,0:T(8,128)(2,1)} %compare_convert_fusion.refs_2_, ...), custom_call_target="tpu_custom_call" | custom-call | flops 96636768 | bytes 440401 | tf_op jit(solution)/shard_map/combine_own/pallas_call | solution.py:416
  667.2 16.1 %combine_own.11 = (bf16[2,4,256,512]{3,2,1,0:T(8,128)(2,1)}, bf16[2,4,256,512]{3,2,1,0:T(8,128)(2,1)}, f32[8,128]{1,0:T(8,128)}) custom-call(bf16[8,2,1536,256]{3,2,1,0:T(8,128)(2,1)} %get-tuple-element.121.refs_0_.refs_1_, bf16[8,2,2048,256]{3,2,1,0:T(8,128)(2,1)} %refs_1_.15, bf16[32,256,384]{2,1,0:T(8,128)(2,1)} %compare_convert_fusion.refs_2_, ...), custom_call_target="tpu_custom_call" | custom-call | flops 96636768 | bytes 440401 | tf_op jit(solution)/shard_map/combine_own/pallas_call | solution.py:416
  692.2 12.5 combine_other.12
  707.6 12.5 combine_other.13
  728.7 13.7 %combine_own.12 = (bf16[2,4,256,512]{3,2,1,0:T(8,128)(2,1)}, bf16[2,4,256,512]{3,2,1,0:T(8,128)(2,1)}, f32[8,128]{1,0:T(8,128)}) custom-call(bf16[8,1,1536,256]{3,2,1,0:T(8,128)(2,1)} %bitcast.312, bf16[8,1,256,2048]{3,2,1,0:T(8,128)(2,1)} %bitcast.320, bf16[32,256,384]{2,1,0:T(8,128)(2,1)} %compare_convert_fusion.refs_2_, ...), custom_call_target="tpu_custom_call" | custom-call | flops 64424508 | bytes 377487 | tf_op jit(solution)/shard_map/combine_own/pallas_call | solution.py:416
  749.1 11.9 collective-permute-done.45
  767.7 13.7 combine_own.13
  789.5 12.5 combine_other.14
  812.4 12.7 combine_other.15
  831.5 9.4 collective-permute-done.62
  854.3 17.0 %collective-permute-done.64 = bf16[256,2048]{1,0:T(8,128)(2,1)} collective-permute-done((bf16[256,2048]{1,0:T(8,128)(2,1)S(1)}, bf16[256,2048]{1,0:T(8,128)(2,1)}, u32[]{:S(2)}, u32[]{:S(2)}) %collective-permute-start.64) | collective-permute-done | bytes 1048608 | tf_op jit(solution)/shard_map/ppermute | solution.py:73
  876.5 13.5 combine_own.14
  890.0 13.7 %combine_own.15 = (bf16[2,4,256,512]{3,2,1,0:T(8,128)(2,1)}, bf16[2,4,256,512]{3,2,1,0:T(8,128)(2,1)}, f32[8,128]{1,0:T(8,128)}) custom-call(bf16[8,1,1536,256]{3,2,1,0:T(8,128)(2,1)} %bitcast.317, bf16[8,1,256,2048]{3,2,1,0:T(8,128)(2,1)} %bitcast.325, bf16[32,256,384]{2,1,0:T(8,128)(2,1)} %compare_convert_fusion.refs_2_, ...), custom_call_target="tpu_custom_call" | custom-call | flops 64424508 | bytes 377487 | tf_op jit(solution)/shard_map/combine_own/pallas_call | solution.py:416
  909.2 8.4 collective-permute-done.46
  940.1 16.7 %attention_back.1 = (bf16[3,1024,512]{2,1,0:T(8,128)(2,1)}, f32[2,1,512]{2,1,0:T(1,128)S(1)}, f32[8,128]{1,0:T(8,128)S(1)}) custom-call(f32[3,1024,512]{2,1,0:T(8,128)} %convolution_bitcast_fusion.pre_ref.refs_0_, f32[2,1,512]{2,1,0:T(1,128)S(1)} %copy-done.21, f32[1024,128]{1,0:T(8,128)S(1)} %copy-done.7, f32[1024,128]{1,0:T(8,128)S(1)} %copy-done.9, ...), custom_call_target="tpu_custom_call" | custom-call | flops 75161928 | bytes 209715 | tf_op jit(solution)/shard_map/attention_back/pallas_call | solution.py:569
  979.6 7.9 weight_grad.16
  987.4 8.2 weight_grad.17
  1006.4 16.1 %collective-permute-done.70 = bf16[256,2048]{1,0:T(8,128)(2,1)} collective-permute-done((bf16[256,2048]{1,0:T(8,128)(2,1)}, bf16[256,2048]{1,0:T(8,128)(2,1)}, u32[]{:S(2)}, u32[]{:S(2)}) %collective-permute-start.70) | collective-permute-done | bytes 1048608 | tf_op jit(solution)/shard_map/ppermute | solution.py:73
  1030.1 8.5 weight_grad.18
  1038.6 7.9 weight_grad.19
  1049.9 9.1 collective-permute-done.75
  1075.4 10.2 collective-permute-done.74
  1098.7 7.8 weight_grad.21
  1115.4 18.9 %collective-permute-done.83 = bf16[256,512]{1,0:T(8,128)(2,1)S(1)} collective-permute-done((bf16[256,512]{1,0:T(8,128)(2,1)S(1)}, bf16[256,512]{1,0:T(8,128)(2,1)S(1)}, u32[]{:S(2)}, u32[]{:S(2)}) %collective-permute-start.83) | collective-permute-done | bytes 262176 | tf_op jit(solution)/shard_map/ppermute | solution.py:73
  1144.7 7.8 weight_grad.22
  1152.6 8.2 weight_grad.23
  1172.4 12.8 collective-permute-done.91
  1239.4 13.9 %collective-permute-done.95 = bf16[512,512]{1,0:T(8,128)(2,1)S(1)} collective-permute-done((bf16[512,512]{1,0:T(8,128)(2,1)S(1)}, bf16[512,512]{1,0:T(8,128)(2,1)S(1)}, u32[]{:S(2)}, u32[]{:S(2)}) %collective-permute-start.95) | collective-permute-done | bytes 524320 | tf_op jit(solution)/shard_map/ppermute | solution.py:73
  1291.9 8.5 collective-permute-done.93
  1333.6 19.4 %collective-permute-done.110 = bf16[1024,512]{1,0:T(8,128)(2,1)S(1)} collective-permute-done((bf16[1024,512]{1,0:T(8,128)(2,1)S(1)}, bf16[1024,512]{1,0:T(8,128)(2,1)S(1)}, u32[]{:S(2)}, u32[]{:S(2)}) %collective-permute-start.110) | collective-permute-done | bytes 1048608 | tf_op jit(solution)/shard_map/ppermute | solution.py:73
  (844 shorter events, 487.7 us)
Async XLA Ops:
  7.2 217.8 %all-gather.3.cloned.1.call-start = ((), (), s32[]{:S(2)}) async-start(), calls=%async_computation | async-start | bytes 34603008 | tf_op jit(solution)/shard_map/all_gather | solution.py:669
  10.1 413.1 %all-gather.5.cloned.1.call-start = ((), (), s32[]{:S(2)}) async-start(), calls=%async_computation.1 | async-start | bytes 34603008 | tf_op jit(solution)/shard_map/all_gather | solution.py:695
  12.6 33.8 %collective-permute-start = (bf16[256,2048]{1,0:T(8,128)(2,1)S(1)}, bf16[256,2048]{1,0:T(8,128)(2,1)}, u32[]{:S(2)}, u32[]{:S(2)}) collective-permute-start(bf16[256,2048]{1,0:T(8,128)(2,1)S(1)} %multiply_convert_fusion.1), channel_id=1, source_target_pairs={{0,2},{2,0},{1,3},{3,1},{4,6},{6,4},{5,7},{7,5},{8,10},{10,8},{9,1... | collective-permute-start | bytes 3145736 | tf_op jit(solution)/shard_map/ppermute | solution.py:73
  101.6 38.5 %collective-permute-start.3 = (bf16[256,2048]{1,0:T(8,128)(2,1)S(1)}, bf16[256,2048]{1,0:T(8,128)(2,1)}, u32[]{:S(2)}, u32[]{:S(2)}) collective-permute-start(bf16[256,2048]{1,0:T(8,128)(2,1)S(1)} %dynamic-slice_bitcast_fusion.7), channel_id=1, source_target_pairs={{0,2},{2,0},{1,3},{3,1},{4,6},{6,4},{5,7},{7,5},{8,10},{10,8},{9,1... | collective-permute-start | bytes 3145736 | tf_op jit(solution)/shard_map/ppermute | solution.py:73
  225.0 1133.4 %all-reduce.2.cloned.1.call-start = ((), (), s32[]{:S(2)}) async-start(), calls=%async_computation.2 | async-start | bytes 1048576 | tf_op jit(solution)/shard_map/psum | solution.py:881
  284.3 93.3 %collective-permute-start.13 = (f32[16,8,256]{2,1,0:T(8,128)S(1)}, f32[16,8,256]{2,1,0:T(8,128)S(1)}, u32[]{:S(2)}, u32[]{:S(2)}) collective-permute-start(f32[16,8,256]{2,1,0:T(8,128)S(1)} %pad_maximum_fusion.14), channel_id=1, source_target_pairs={{0,1},{1,0},{2,3},{3,2},{4,5},{5,4},{6,7},{7,6},{8,9},{9,8},{10,11... | collective-permute-start | bytes 393224 | tf_op jit(solution)/shard_map/ppermute | solution.py:73
  571.6 59.2 %collective-permute-start.30 = (bf16[2,4,256,640]{3,2,1,0:T(8,128)(2,1)}, bf16[2,4,256,640]{3,2,1,0:T(8,128)(2,1)S(1)}, u32[]{:S(2)}, u32[]{:S(2)}) collective-permute-start(bf16[2,4,256,640]{3,2,1,0:T(8,128)(2,1)} %get-tuple-element.146), channel_id=1, source_target_pairs={{0,2},{2,0},{1,3},{3,1},{4,6},{6,4},{5,7},{7,5},{8,10},{10,8},{9,1... | collective-permute-start | bytes 7864328 | tf_op jit(solution)/shard_map/ppermute | solution.py:73
  612.1 48.7 %collective-permute-start.31 = (bf16[2,4,256,512]{3,2,1,0:T(8,128)(2,1)}, bf16[2,4,256,512]{3,2,1,0:T(8,128)(2,1)S(1)}, u32[]{:S(2)}, u32[]{:S(2)}) collective-permute-start(bf16[2,4,256,512]{3,2,1,0:T(8,128)(2,1)} %get-tuple-element.149), channel_id=1, source_target_pairs={{0,4},{4,0},{1,5},{5,1},{2,6},{6,2},{3,7},{7,3},{8,12},{12,8},{9,1... | collective-permute-start | bytes 6291464 | tf_op jit(solution)/shard_map/ppermute | solution.py:73
  636.5 52.5 %collective-permute-start.32 = (bf16[4,256,640]{2,1,0:T(8,128)(2,1)S(1)}, bf16[4,256,640]{2,1,0:T(8,128)(2,1)}, u32[]{:S(2)}, u32[]{:S(2)}) collective-permute-start(bf16[4,256,640]{2,1,0:T(8,128)(2,1)S(1)} %slice_bitcast_fusion.1.refs_8_), channel_id=1, source_target_pairs={{0,4},{4,0},{1,5},{5,1},{2,6},{6,2},{3,7},{7,3},{8,12},{12,8},{9,1... | collective-permute-start | bytes 3932168 | tf_op jit(solution)/shard_map/ppermute | solution.py:73
  638.1 29.1 %collective-permute-start.23 = (bf16[1,4,256,512]{3,2,1,0:T(8,128)(2,1)}, bf16[1,4,256,512]{3,2,1,0:T(8,128)(2,1)}, u32[]{:S(2)}, u32[]{:S(2)}) collective-permute-start(bf16[1,4,256,512]{3,2,1,0:T(8,128)(2,1)} %get-tuple-element.137), channel_id=1, source_target_pairs={{0,1},{1,0},{2,3},{3,2},{4,5},{5,4},{6,7},{7,6},{8,9},{9,8},{10,11... | collective-permute-start | bytes 3145736 | tf_op jit(solution)/shard_map/ppermute | solution.py:73
  638.1 29.1 %collective-permute-start.24 = (bf16[1,4,256,512]{3,2,1,0:T(8,128)(2,1)}, bf16[1,4,256,512]{3,2,1,0:T(8,128)(2,1)}, u32[]{:S(2)}, u32[]{:S(2)}) collective-permute-start(bf16[1,4,256,512]{3,2,1,0:T(8,128)(2,1)} %get-tuple-element.138), channel_id=1, source_target_pairs={{0,1},{1,0},{2,3},{3,2},{4,5},{5,4},{6,7},{7,6},{8,9},{9,8},{10,11... | collective-permute-start | bytes 3145736 | tf_op jit(solution)/shard_map/ppermute | solution.py:73
  638.6 28.6 %collective-permute-start.25 = (bf16[1,4,256,512]{3,2,1,0:T(8,128)(2,1)}, bf16[1,4,256,512]{3,2,1,0:T(8,128)(2,1)}, u32[]{:S(2)}, u32[]{:S(2)}) collective-permute-start(bf16[1,4,256,512]{3,2,1,0:T(8,128)(2,1)} %get-tuple-element.139), channel_id=1, source_target_pairs={{0,1},{1,0},{2,3},{3,2},{4,5},{5,4},{6,7},{7,6},{8,9},{9,8},{10,11... | collective-permute-start | bytes 3145736 | tf_op jit(solution)/shard_map/ppermute | solution.py:73
  660.8 46.9 %collective-permute-start.38 = (bf16[2,4,256,512]{3,2,1,0:T(8,128)(2,1)}, bf16[2,4,256,512]{3,2,1,0:T(8,128)(2,1)}, u32[]{:S(2)}, u32[]{:S(2)}) collective-permute-start(bf16[2,4,256,512]{3,2,1,0:T(8,128)(2,1)} %get-tuple-element.158), channel_id=1, source_target_pairs={{0,2},{2,0},{1,3},{3,1},{4,6},{6,4},{5,7},{7,5},{8,10},{10,8},{9,1... | collective-permute-start | bytes 6291464 | tf_op jit(solution)/shard_map/ppermute | solution.py:73
  684.6 59.1 %collective-permute-start.44 = (bf16[2,4,256,512]{3,2,1,0:T(8,128)(2,1)}, bf16[2,4,256,512]{3,2,1,0:T(8,128)(2,1)}, u32[]{:S(2)}, u32[]{:S(2)}) collective-permute-start(bf16[2,4,256,512]{3,2,1,0:T(8,128)(2,1)} %get-tuple-element.167), channel_id=1, source_target_pairs={{0,4},{4,0},{1,5},{5,1},{2,6},{6,2},{3,7},{7,3},{8,12},{12,8},{9,1... | collective-permute-start | bytes 6291464 | tf_op jit(solution)/shard_map/ppermute | solution.py:73
  723.8 40.9 %collective-permute-start.39 = (bf16[1,4,256,512]{3,2,1,0:T(8,128)(2,1)}, bf16[1,4,256,512]{3,2,1,0:T(8,128)(2,1)}, u32[]{:S(2)}, u32[]{:S(2)}) collective-permute-start(bf16[1,4,256,512]{3,2,1,0:T(8,128)(2,1)} %get-tuple-element.161), channel_id=1, source_target_pairs={{0,1},{1,0},{2,3},{3,2},{4,5},{5,4},{6,7},{7,6},{8,9},{9,8},{10,11... | collective-permute-start | bytes 3145736 | tf_op jit(solution)/shard_map/ppermute | solution.py:73
  727.1 38.5 %collective-permute-start.40 = (bf16[1,4,256,512]{3,2,1,0:T(8,128)(2,1)}, bf16[1,4,256,512]{3,2,1,0:T(8,128)(2,1)}, u32[]{:S(2)}, u32[]{:S(2)}) collective-permute-start(bf16[1,4,256,512]{3,2,1,0:T(8,128)(2,1)} %get-tuple-element.162), channel_id=1, source_target_pairs={{0,1},{1,0},{2,3},{3,2},{4,5},{5,4},{6,7},{7,6},{8,9},{9,8},{10,11... | collective-permute-start | bytes 3145736 | tf_op jit(solution)/shard_map/ppermute | solution.py:73
  728.7 39.0 %collective-permute-start.41 = (bf16[1,4,256,512]{3,2,1,0:T(8,128)(2,1)}, bf16[1,4,256,512]{3,2,1,0:T(8,128)(2,1)}, u32[]{:S(2)}, u32[]{:S(2)}) collective-permute-start(bf16[1,4,256,512]{3,2,1,0:T(8,128)(2,1)} %get-tuple-element.163), channel_id=1, source_target_pairs={{0,1},{1,0},{2,3},{3,2},{4,5},{5,4},{6,7},{7,6},{8,9},{9,8},{10,11... | collective-permute-start | bytes 3145736 | tf_op jit(solution)/shard_map/ppermute | solution.py:73
  765.6 37.6 %collective-permute-start.49 = (bf16[4,256,512]{2,1,0:T(8,128)(2,1)S(1)}, bf16[4,256,512]{2,1,0:T(8,128)(2,1)}, u32[]{:S(2)}, u32[]{:S(2)}) collective-permute-start(bf16[4,256,512]{2,1,0:T(8,128)(2,1)S(1)} %slice_bitcast_fusion.12.refs_9_), channel_id=1, source_target_pairs={{0,2},{2,0},{1,3},{3,1},{4,6},{6,4},{5,7},{7,5},{8,10},{10,8},{9,1... | collective-permute-start | bytes 3145736 | tf_op jit(solution)/shard_map/ppermute | solution.py:73
  848.7 56.2 %collective-permute-start.66 = (bf16[2,4,256,512]{3,2,1,0:T(8,128)(2,1)}, bf16[2,4,256,512]{3,2,1,0:T(8,128)(2,1)}, u32[]{:S(2)}, u32[]{:S(2)}) collective-permute-start(bf16[2,4,256,512]{3,2,1,0:T(8,128)(2,1)} %broadcast_add_fusion.2), channel_id=1, source_target_pairs={{0,4},{4,0},{1,5},{5,1},{2,6},{6,2},{3,7},{7,3},{8,12},{12,8},{9,1... | collective-permute-start | bytes 6291464 | tf_op jit(solution)/shard_map/ppermute | solution.py:73
  852.5 65.1 %collective-permute-start.46 = (bf16[2,4,256,512]{3,2,1,0:T(8,128)(2,1)}, bf16[2,4,256,512]{3,2,1,0:T(8,128)(2,1)}, u32[]{:S(2)}, u32[]{:S(2)}) collective-permute-start(bf16[2,4,256,512]{3,2,1,0:T(8,128)(2,1)} %broadcast_add_fusion.3), channel_id=1, source_target_pairs={{0,2},{2,0},{1,3},{3,1},{4,6},{6,4},{5,7},{7,5},{8,10},{10,8},{9,1... | collective-permute-start | bytes 6291464 | tf_op jit(solution)/shard_map/ppermute | solution.py:73
  853.8 36.2 %collective-permute-start.54 = (bf16[1,4,256,512]{3,2,1,0:T(8,128)(2,1)}, bf16[1,4,256,512]{3,2,1,0:T(8,128)(2,1)}, u32[]{:S(2)}, u32[]{:S(2)}) collective-permute-start(bf16[1,4,256,512]{3,2,1,0:T(8,128)(2,1)} %get-tuple-element.172), channel_id=1, source_target_pairs={{0,1},{1,0},{2,3},{3,2},{4,5},{5,4},{6,7},{7,6},{8,9},{9,8},{10,11... | collective-permute-start | bytes 3145736 | tf_op jit(solution)/shard_map/ppermute | solution.py:73
  874.6 52.8 %collective-permute-start.65 = (bf16[512,2048]{1,0:T(8,128)(2,1)}, bf16[512,2048]{1,0:T(8,128)(2,1)}, u32[]{:S(2)}, u32[]{:S(2)}) collective-permute-start(bf16[512,2048]{1,0:T(8,128)(2,1)} %pad_maximum_fusion.2), channel_id=1, source_target_pairs={{0,1},{1,0},{2,3},{3,2},{4,5},{5,4},{6,7},{7,6},{8,9},{9,8},{10,11... | collective-permute-start | bytes 6291464 | tf_op jit(solution)/shard_map/ppermute | solution.py:73
  907.9 88.2 %collective-permute-start.69 = (bf16[4,256,512]{2,1,0:T(8,128)(2,1)S(1)}, bf16[4,256,512]{2,1,0:T(8,128)(2,1)S(1)}, u32[]{:S(2)}, u32[]{:S(2)}) collective-permute-start(bf16[4,256,512]{2,1,0:T(8,128)(2,1)S(1)} %slice_bitcast_fusion.7.refs_11_), channel_id=1, source_target_pairs={{0,2},{2,0},{1,3},{3,1},{4,6},{6,4},{5,7},{7,5},{8,10},{10,8},{9,1... | collective-permute-start | bytes 3145736 | tf_op jit(solution)/shard_map/ppermute | solution.py:73
  920.6 79.2 %collective-permute-start.63 = (bf16[4,256,512]{2,1,0:T(8,128)(2,1)S(1)}, bf16[4,256,512]{2,1,0:T(8,128)(2,1)}, u32[]{:S(2)}, u32[]{:S(2)}) collective-permute-start(bf16[4,256,512]{2,1,0:T(8,128)(2,1)S(1)} %slice_bitcast_fusion.8.refs_10_), channel_id=1, source_target_pairs={{0,4},{4,0},{1,5},{5,1},{2,6},{6,2},{3,7},{7,3},{8,12},{12,8},{9,1... | collective-permute-start | bytes 3145736 | tf_op jit(solution)/shard_map/ppermute | solution.py:73
  972.7 30.3 %collective-permute-start.71 = (bf16[1024,512]{1,0:T(8,128)(2,1)S(1)}, bf16[1024,512]{1,0:T(8,128)(2,1)}, u32[]{:S(2)}, u32[]{:S(2)}) collective-permute-start(bf16[1024,512]{1,0:T(8,128)(2,1)S(1)} %dynamic-slice_bitcast_fusion.6.refs_4_), channel_id=1, source_target_pairs={{0,4},{4,0},{1,5},{5,1},{2,6},{6,2},{3,7},{7,3},{8,12},{12,8},{9,1... | collective-permute-start | bytes 3145736 | tf_op jit(solution)/shard_map/ppermute | solution.py:73
  977.1 49.0 %collective-permute-start.68 = (bf16[512,2048]{1,0:T(8,128)(2,1)}, bf16[512,2048]{1,0:T(8,128)(2,1)}, u32[]{:S(2)}, u32[]{:S(2)}) collective-permute-start(bf16[512,2048]{1,0:T(8,128)(2,1)} %dynamic-slice_bitcast_fusion), channel_id=1, source_target_pairs={{0,1},{1,0},{2,3},{3,2},{4,5},{5,4},{6,7},{7,6},{8,9},{9,8},{10,11... | collective-permute-start | bytes 6291464 | tf_op jit(solution)/shard_map/ppermute | solution.py:73
  978.5 44.0 %collective-permute-start.70 = (bf16[256,2048]{1,0:T(8,128)(2,1)}, bf16[256,2048]{1,0:T(8,128)(2,1)}, u32[]{:S(2)}, u32[]{:S(2)}) collective-permute-start(bf16[256,2048]{1,0:T(8,128)(2,1)} %dynamic-slice_bitcast_fusion.2), channel_id=1, source_target_pairs={{0,4},{4,0},{1,5},{5,1},{2,6},{6,2},{3,7},{7,3},{8,12},{12,8},{9,1... | collective-permute-start | bytes 3145736 | tf_op jit(solution)/shard_map/ppermute | solution.py:73
  996.1 74.0 %collective-permute-start.78 = (bf16[2,4,256,512]{3,2,1,0:T(8,128)(2,1)}, bf16[2,4,256,512]{3,2,1,0:T(8,128)(2,1)}, u32[]{:S(2)}, u32[]{:S(2)}) collective-permute-start(bf16[2,4,256,512]{3,2,1,0:T(8,128)(2,1)} %broadcast_add_fusion.1), channel_id=1, source_target_pairs={{0,2},{2,0},{1,3},{3,1},{4,6},{6,4},{5,7},{7,5},{8,10},{10,8},{9,1... | collective-permute-start | bytes 6291464 | tf_op jit(solution)/shard_map/ppermute | solution.py:73
  999.8 193.0 %collective-permute-start.92 = (bf16[2,4,256,512]{3,2,1,0:T(8,128)(2,1)}, bf16[2,4,256,512]{3,2,1,0:T(8,128)(2,1)}, u32[]{:S(2)}, u32[]{:S(2)}) collective-permute-start(bf16[2,4,256,512]{3,2,1,0:T(8,128)(2,1)} %broadcast_add_fusion), channel_id=1, source_target_pairs={{0,2},{2,0},{1,3},{3,1},{4,6},{6,4},{5,7},{7,5},{8,10},{10,8},{9,1... | collective-permute-start | bytes 6291464 | tf_op jit(solution)/shard_map/ppermute | solution.py:73
  1003.1 58.8 %collective-permute-start.77 = (bf16[1024,512]{1,0:T(8,128)(2,1)S(1)}, bf16[1024,512]{1,0:T(8,128)(2,1)}, u32[]{:S(2)}, u32[]{:S(2)}) collective-permute-start(bf16[1024,512]{1,0:T(8,128)(2,1)S(1)} %dynamic-slice_bitcast_fusion.4.refs_6_), channel_id=1, source_target_pairs={{0,4},{4,0},{1,5},{5,1},{2,6},{6,2},{3,7},{7,3},{8,12},{12,8},{9,1... | collective-permute-start | bytes 3145736 | tf_op jit(solution)/shard_map/ppermute | solution.py:73
  1022.5 43.2 %collective-permute-start.76 = (bf16[1024,512]{1,0:T(8,128)(2,1)S(1)}, bf16[1024,512]{1,0:T(8,128)(2,1)}, u32[]{:S(2)}, u32[]{:S(2)}) collective-permute-start(bf16[1024,512]{1,0:T(8,128)(2,1)S(1)} %dynamic-slice_bitcast_fusion.5.refs_5_), channel_id=1, source_target_pairs={{0,4},{4,0},{1,5},{5,1},{2,6},{6,2},{3,7},{7,3},{8,12},{12,8},{9,1... | collective-permute-start | bytes 3145736 | tf_op jit(solution)/shard_map/ppermute | solution.py:73
  1061.9 45.8 %collective-permute-start.86 = (f32[2,512]{1,0:T(2,128)S(1)}, f32[2,512]{1,0:T(2,128)S(1)}, u32[]{:S(2)}, u32[]{:S(2)}) collective-permute-start(f32[2,512]{1,0:T(2,128)S(1)} %bitcast.402), channel_id=1, source_target_pairs={{0,16},{16,0},{1,17},{17,1},{2,18},{18,2},{3,19},{19,3},{4,20},{20... | collective-permute-start | bytes 12296 | tf_op jit(solution)/shard_map/ppermute | solution.py:73
  1070.1 38.4 %collective-permute-start.82 = (bf16[64,2048]{1,0:T(8,128)(2,1)S(1)}, bf16[64,2048]{1,0:T(8,128)(2,1)}, u32[]{:S(2)}, u32[]{:S(2)}) collective-permute-start(bf16[64,2048]{1,0:T(8,128)(2,1)S(1)} %dynamic-slice_bitcast_fusion.15.refs_4_), channel_id=1, source_target_pairs={{0,16},{16,0},{1,17},{17,1},{2,18},{18,2},{3,19},{19,3},{4,20},{20... | collective-permute-start | bytes 786440 | tf_op jit(solution)/shard_map/ppermute | solution.py:73
  1108.5 31.3 %collective-permute-start.84 = (bf16[512,512]{1,0:T(8,128)(2,1)S(1)}, bf16[512,512]{1,0:T(8,128)(2,1)S(1)}, u32[]{:S(2)}, u32[]{:S(2)}) collective-permute-start(bf16[512,512]{1,0:T(8,128)(2,1)S(1)} %dynamic-slice_bitcast_fusion.9.refs_8_), channel_id=1, source_target_pairs={{0,8},{8,0},{1,9},{9,1},{2,10},{10,2},{3,11},{11,3},{4,12},{12,4},... | collective-permute-start | bytes 1572872 | tf_op jit(solution)/shard_map/ppermute | solution.py:73
  1134.3 31.1 %collective-permute-start.80 = (bf16[4,256,512]{2,1,0:T(8,128)(2,1)S(1)}, bf16[4,256,512]{2,1,0:T(8,128)(2,1)}, u32[]{:S(2)}, u32[]{:S(2)}) collective-permute-start(bf16[4,256,512]{2,1,0:T(8,128)(2,1)S(1)} %slice_bitcast_fusion.5.refs_10_), channel_id=1, source_target_pairs={{0,4},{4,0},{1,5},{5,1},{2,6},{6,2},{3,7},{7,3},{8,12},{12,8},{9,1... | collective-permute-start | bytes 3145736 | tf_op jit(solution)/shard_map/ppermute | solution.py:73
  1135.6 91.2 %collective-permute-start.99 = (f32[2,512]{1,0:T(2,128)S(1)}, f32[2,512]{1,0:T(2,128)S(1)}, u32[]{:S(2)}, u32[]{:S(2)}) collective-permute-start(f32[2,512]{1,0:T(2,128)S(1)} %add_add_fusion.6.refs_11_), channel_id=1, source_target_pairs={{0,8},{8,0},{1,9},{9,1},{2,10},{10,2},{3,11},{11,3},{4,12},{12,4},... | collective-permute-start | bytes 12296 | tf_op jit(solution)/shard_map/ppermute | solution.py:73
  1139.9 58.2 %collective-permute-start.89 = (bf16[256,512]{1,0:T(8,128)(2,1)S(1)}, bf16[256,512]{1,0:T(8,128)(2,1)}, u32[]{:S(2)}, u32[]{:S(2)}) collective-permute-start(bf16[256,512]{1,0:T(8,128)(2,1)S(1)} %fusion.36.refs_6_), channel_id=1, source_target_pairs={{0,16},{16,0},{1,17},{17,1},{2,18},{18,2},{3,19},{19,3},{4,20},{20... | collective-permute-start | bytes 786440 | tf_op jit(solution)/shard_map/ppermute | solution.py:73
  1185.1 52.3 %collective-permute-start.87 = (bf16[2,256,512]{2,1,0:T(8,128)(2,1)}, bf16[2,256,512]{2,1,0:T(8,128)(2,1)}, u32[]{:S(2)}, u32[]{:S(2)}) collective-permute-start(bf16[2,256,512]{2,1,0:T(8,128)(2,1)} %slice.426.refs_8_), channel_id=1, source_target_pairs={{0,8},{8,0},{1,9},{9,1},{2,10},{10,2},{3,11},{11,3},{4,12},{12,4},... | collective-permute-start | bytes 1572872 | tf_op jit(solution)/shard_map/ppermute | solution.py:73
  1190.7 40.8 %collective-permute-start.97 = (bf16[256,512]{1,0:T(8,128)(2,1)S(1)}, bf16[256,512]{1,0:T(8,128)(2,1)}, u32[]{:S(2)}, u32[]{:S(2)}) collective-permute-start(bf16[256,512]{1,0:T(8,128)(2,1)S(1)} %fusion.34.refs_6_), channel_id=1, source_target_pairs={{0,16},{16,0},{1,17},{17,1},{2,18},{18,2},{3,19},{19,3},{4,20},{20... | collective-permute-start | bytes 786440 | tf_op jit(solution)/shard_map/ppermute | solution.py:73
  1192.8 40.5 %collective-permute-start.96 = (bf16[256,512]{1,0:T(8,128)(2,1)S(1)}, bf16[256,512]{1,0:T(8,128)(2,1)}, u32[]{:S(2)}, u32[]{:S(2)}) collective-permute-start(bf16[256,512]{1,0:T(8,128)(2,1)S(1)} %fusion.35.refs_5_), channel_id=1, source_target_pairs={{0,16},{16,0},{1,17},{17,1},{2,18},{18,2},{3,19},{19,3},{4,20},{20... | collective-permute-start | bytes 786440 | tf_op jit(solution)/shard_map/ppermute | solution.py:73
  1233.3 67.9 %collective-permute-start.112 = (f32[2,512]{1,0:T(2,128)S(1)}, f32[2,512]{1,0:T(2,128)S(1)}, u32[]{:S(2)}, u32[]{:S(2)}) collective-permute-start(f32[2,512]{1,0:T(2,128)S(1)} %add_add_fusion.5.refs_10_), channel_id=1, source_target_pairs={{0,4},{4,0},{1,5},{5,1},{2,6},{6,2},{3,7},{7,3},{8,12},{12,8},{9,1... | collective-permute-start | bytes 12296 | tf_op jit(solution)/shard_map/ppermute | solution.py:73
  1237.4 50.0 %collective-permute-start.104 = (f32[2,2048]{1,0:T(2,128)S(1)}, f32[2,2048]{1,0:T(2,128)S(1)}, u32[]{:S(2)}, u32[]{:S(2)}) collective-permute-start(f32[2,2048]{1,0:T(2,128)S(1)} %add_add_fusion.2), channel_id=1, source_target_pairs={{0,4},{4,0},{1,5},{5,1},{2,6},{6,2},{3,7},{7,3},{8,12},{12,8},{9,1... | collective-permute-start | bytes 49160 | tf_op jit(solution)/shard_map/ppermute | solution.py:73
  1253.3 31.2 %collective-permute-start.107 = (bf16[512,512]{1,0:T(8,128)(2,1)}, bf16[512,512]{1,0:T(8,128)(2,1)}, u32[]{:S(2)}, u32[]{:S(2)}) collective-permute-start(bf16[512,512]{1,0:T(8,128)(2,1)} %pad_maximum_fusion.11.refs_6_), channel_id=1, source_target_pairs={{0,8},{8,0},{1,9},{9,1},{2,10},{10,2},{3,11},{11,3},{4,12},{12,4},... | collective-permute-start | bytes 1572872 | tf_op jit(solution)/shard_map/ppermute | solution.py:73
  1254.7 34.1 %collective-permute-start.109 = (bf16[512,512]{1,0:T(8,128)(2,1)}, bf16[512,512]{1,0:T(8,128)(2,1)}, u32[]{:S(2)}, u32[]{:S(2)}) collective-permute-start(bf16[512,512]{1,0:T(8,128)(2,1)} %pad_maximum_fusion.12.refs_7_), channel_id=1, source_target_pairs={{0,8},{8,0},{1,9},{9,1},{2,10},{10,2},{3,11},{11,3},{4,12},{12,4},... | collective-permute-start | bytes 1572872 | tf_op jit(solution)/shard_map/ppermute | solution.py:73
  1256.9 57.3 %collective-permute-start.113 = (bf16[256,2048]{1,0:T(8,128)(2,1)S(1)}, bf16[256,2048]{1,0:T(8,128)(2,1)}, u32[]{:S(2)}, u32[]{:S(2)}) collective-permute-start(bf16[256,2048]{1,0:T(8,128)(2,1)S(1)} %pad_maximum_fusion.3.refs_4_), channel_id=1, source_target_pairs={{0,4},{4,0},{1,5},{5,1},{2,6},{6,2},{3,7},{7,3},{8,12},{12,8},{9,1... | collective-permute-start | bytes 3145736 | tf_op jit(solution)/shard_map/ppermute | solution.py:73
  1284.5 34.0 %collective-permute-start.111 = (bf16[1024,512]{1,0:T(8,128)(2,1)S(1)}, bf16[1024,512]{1,0:T(8,128)(2,1)S(1)}, u32[]{:S(2)}, u32[]{:S(2)}) collective-permute-start(bf16[1024,512]{1,0:T(8,128)(2,1)S(1)} %pad_maximum_fusion.4.refs_5_), channel_id=1, source_target_pairs={{0,4},{4,0},{1,5},{5,1},{2,6},{6,2},{3,7},{7,3},{8,12},{12,8},{9,1... | collective-permute-start | bytes 3145736 | tf_op jit(solution)/shard_map/ppermute | solution.py:73
  1300.4 32.7 %collective-permute-start.108 = (bf16[1024,512]{1,0:T(8,128)(2,1)S(1)}, bf16[1024,512]{1,0:T(8,128)(2,1)S(1)}, u32[]{:S(2)}, u32[]{:S(2)}) collective-permute-start(bf16[1024,512]{1,0:T(8,128)(2,1)S(1)} %pad_maximum_fusion.5), channel_id=1, source_target_pairs={{0,4},{4,0},{1,5},{5,1},{2,6},{6,2},{3,7},{7,3},{8,12},{12,8},{9,1... | collective-permute-start | bytes 3145736 | tf_op jit(solution)/shard_map/ppermute | solution.py:73
  1312.0 41.0 %collective-permute-start.110 = (bf16[1024,512]{1,0:T(8,128)(2,1)S(1)}, bf16[1024,512]{1,0:T(8,128)(2,1)S(1)}, u32[]{:S(2)}, u32[]{:S(2)}) collective-permute-start(bf16[1024,512]{1,0:T(8,128)(2,1)S(1)} %pad_maximum_fusion.6), channel_id=1, source_target_pairs={{0,4},{4,0},{1,5},{5,1},{2,6},{6,2},{3,7},{7,3},{8,12},{12,8},{9,1... | collective-permute-start | bytes 3145736 | tf_op jit(solution)/shard_map/ppermute | solution.py:73
  (254 other events, 3010.1 us)
Sparse Core Ops, SparseCore 0:
  11.5 213.4 all-gather.2
  227.8 195.3 all-gather.4
  876.6 126.7 all-reduce.1
